TPU v7x, 32 devices: a whole 2x2x4 slice. The times are simulated.
32 devices in a mesh: wq: 16 (over z, x, core), np: 2 (over y).
Axes of the slice: x: 2, y: 2, z: 4, core: 2. Of those that a mesh axis runs over, the one named last changes fastest.
Arguments:
- q_embed: bfloat16 [16384, 768], P(('wq', 'np')), may hold values from -6 to 6
- p_embed: bfloat16 [49152, 768], P(('wq', 'np')), may hold values from -6 to 6
- q_len: int32 [256], P(('wq', 'np')), may hold values from 16 to 64, as said below
- p_len: int32 [192], P(('wq', 'np')), may hold values from 64 to 256, as said below
- q_set: int32 [256], P(('wq', 'np')), may hold values from 0 to 3, as said below
- p_set: int32 [192], P(('wq', 'np')), may hold values from 0 to 3
- gold: int32 [256], P(('wq', 'np')), may hold values from 0 to 191, as said below
- query_key_value_weight: bfloat16 [2, 768, 2304], P(None, 'wq', 'np'), may hold values from -0.21875 to 0.21875
- attention_output_weight: bfloat16 [2, 768, 768], P(None, 'wq', 'np'), may hold values from -0.625 to 0.625
- up_weight: bfloat16 [2, 768, 3072], P(None, 'wq', 'np'), may hold values from -0.21875 to 0.21875
- down_weight: bfloat16 [2, 3072, 768], P(None, 'wq', 'np'), may hold values from -0.109375 to 0.109375
- vectors: bfloat16 [2, 8, 768], P(None, 'np', 'wq')
- hidden_bias: bfloat16 [2, 3072], P(None, ('wq', 'np')), may hold values from -1.5 to 1.5
Outputs:
- loss: float32 [], replicated
- q_out: bfloat16 [16384, 768], P(('wq', 'np'))
- p_out: bfloat16 [49152, 768], P(('wq', 'np'))
- grad_q_embed: float32 [16384, 768], P(('wq', 'np'))
- grad_p_embed: float32 [49152, 768], P(('wq', 'np'))
- grad_w_qkv: float32 [2, 768, 2304], P(None, 'wq', 'np')
- grad_w_out: float32 [2, 768, 768], P(None, 'wq', 'np')
- grad_w_in: float32 [2, 768, 3072], P(None, 'wq', 'np')
- grad_w_back: float32 [2, 3072, 768], P(None, 'wq', 'np')
- grad_vectors: float32 [2, 8, 768], P(None, 'np', 'wq')
- grad_b_in: float32 [2, 3072], P(None, ('wq', 'np'))
Inputs may be any that keep to these rules, and one draw needn't show every extreme that they name: `q_len`: some question has all 64 tokens. `p_len`: some passage has all 256 tokens. `q_set`: equal to the dataset of the question's gold passage. `gold`: an index among all 192 passages.
All inputs are finite; a program needn't handle non-finite values.
Results may differ from a plain program's by a relative error of at most 0.024.
Values may be sent and summed in bfloat16 or wider, within the bound.
A program may use at most 320 MiB of HBM per device.

v0:
```python
import jax
import jax.numpy as jnp
from jax import lax
from jax.sharding import PartitionSpec as P

HEADS = 12


EPSILON = 1e-12
NEGATIVE = -1e30


def combined_all(array, axis, combine):
    everything = jax.tree.map(lambda part: lax.all_gather(part, axis), array)
    leading = jax.tree.map(lambda part: part[0], everything)

    def lap(k, so_far):
        return combine(so_far, jax.tree.map(lambda part: part[k], everything))

    return lax.fori_loop(1, lax.axis_size(axis), lap, leading)


def layer_norm(inputs, gain_row, offset):
    centred = inputs - jnp.mean(inputs, axis=-1, keepdims=True)
    spread = jnp.mean(centred * centred, axis=-1, keepdims=True)
    return centred * lax.rsqrt(spread + EPSILON) * gain_row + offset


def smooth_gate(values):
    return jax.nn.gelu(values, approximate=True)


def column_total(matrix):
    return jnp.sum(matrix.astype(jnp.float32), axis=0)


def gather_weights(
    query_key_value_weight, attention_output_weight, up_weight, down_weight, vectors, hidden_bias
):
    np_parts = (
        lax.all_gather(query_key_value_weight, "np", axis=2, tiled=True),
        lax.all_gather(attention_output_weight, "np", axis=2, tiled=True),
        lax.all_gather(up_weight, "np", axis=2, tiled=True),
        lax.all_gather(down_weight, "np", axis=2, tiled=True),
        lax.all_gather(vectors, "np", axis=1, tiled=True),
        lax.all_gather(hidden_bias, "np", axis=1, tiled=True),
    )
    return (
        lax.all_gather(np_parts[0], "wq", axis=1, tiled=True),
        lax.all_gather(np_parts[1], "wq", axis=1, tiled=True),
        lax.all_gather(np_parts[2], "wq", axis=1, tiled=True),
        lax.all_gather(np_parts[3], "wq", axis=1, tiled=True),
        lax.all_gather(np_parts[4], "wq", axis=2, tiled=True),
        lax.all_gather(np_parts[5], "wq", axis=1, tiled=True),
    )


def reduce_grads(grads):
    wq_parts = (
        lax.psum_scatter(
            grads[0].astype(jnp.bfloat16), "wq", scatter_dimension=1, tiled=True
        ).astype(jnp.float32),
        lax.psum_scatter(
            grads[1].astype(jnp.bfloat16), "wq", scatter_dimension=1, tiled=True
        ).astype(jnp.float32),
        lax.psum_scatter(
            grads[2].astype(jnp.bfloat16), "wq", scatter_dimension=1, tiled=True
        ).astype(jnp.float32),
        lax.psum_scatter(
            grads[3].astype(jnp.bfloat16), "wq", scatter_dimension=1, tiled=True
        ).astype(jnp.float32),
        lax.psum_scatter(
            grads[4].astype(jnp.bfloat16), "wq", scatter_dimension=2, tiled=True
        ).astype(jnp.float32),
        lax.psum_scatter(
            grads[5].astype(jnp.bfloat16), "wq", scatter_dimension=1, tiled=True
        ).astype(jnp.float32),
    )
    return (
        lax.psum_scatter(
            wq_parts[0].astype(jnp.bfloat16), "np", scatter_dimension=2, tiled=True
        ).astype(jnp.float32),
        lax.psum_scatter(
            wq_parts[1].astype(jnp.bfloat16), "np", scatter_dimension=2, tiled=True
        ).astype(jnp.float32),
        lax.psum_scatter(
            wq_parts[2].astype(jnp.bfloat16), "np", scatter_dimension=2, tiled=True
        ).astype(jnp.float32),
        lax.psum_scatter(
            wq_parts[3].astype(jnp.bfloat16), "np", scatter_dimension=2, tiled=True
        ).astype(jnp.float32),
        lax.psum_scatter(
            wq_parts[4].astype(jnp.bfloat16), "np", scatter_dimension=1, tiled=True
        ).astype(jnp.float32),
        lax.psum_scatter(
            wq_parts[5].astype(jnp.bfloat16), "np", scatter_dimension=1, tiled=True
        ).astype(jnp.float32),
    )


def head_split(matrix, seq_count):
    row_count, model_width = matrix.shape
    return matrix.reshape(seq_count, row_count // seq_count, HEADS, model_width // HEADS)


def attention_scores(queries, keys_low, lengths):
    seq_count = lengths.shape[0]
    split_q = head_split(queries, seq_count)
    scores = jnp.einsum(
        "sqhc,skhc->shqk",
        split_q,
        head_split(keys_low, seq_count),
        preferred_element_type=jnp.float32,
    )
    scores = scores * split_q.shape[3] ** (-0.5)
    live_mask = jnp.arange(split_q.shape[1])[None, :] < lengths[:, None]
    return jnp.where(live_mask[:, None, None, :], scores, NEGATIVE)


def encode_forward(token_rows, lengths, weights):
    (
        query_key_value_weight,
        attention_output_weight,
        up_weight,
        down_weight,
        vectors,
        hidden_bias,
    ) = weights
    row_count, model_width = token_rows.shape
    seq_count = lengths.shape[0]
    vec_f32 = vectors.astype(jnp.float32)
    projected_rows = jnp.dot(token_rows, query_key_value_weight, preferred_element_type=jnp.float32)
    queries = (projected_rows[:, :model_width] + vec_f32[0]).astype(jnp.bfloat16)
    keys_low = projected_rows[:, model_width : 2 * model_width].astype(jnp.bfloat16)
    values = (projected_rows[:, 2 * model_width :] + vec_f32[1]).astype(jnp.bfloat16)
    scores = attention_scores(queries, keys_low, lengths)
    totals = jax.nn.logsumexp(scores, axis=-1, keepdims=True)
    soft_low = jnp.exp(scores - totals).astype(jnp.bfloat16)
    attended_tokens = jnp.einsum(
        "shqk,skhc->sqhc",
        soft_low,
        head_split(values, seq_count),
        preferred_element_type=jnp.float32,
    )
    attended_tokens = attended_tokens.reshape(row_count, model_width).astype(jnp.bfloat16)
    residual_branch = (
        jnp.dot(attended_tokens, attention_output_weight, preferred_element_type=jnp.float32)
        + vec_f32[2]
    )
    pre_one = token_rows.astype(jnp.float32) + residual_branch
    first_normed = layer_norm(pre_one, vec_f32[3], vec_f32[4])
    normed_low = first_normed.astype(jnp.bfloat16)
    hidden_rows = jnp.dot(
        normed_low, up_weight, preferred_element_type=jnp.float32
    ) + hidden_bias.astype(jnp.float32)
    activated_hidden = smooth_gate(hidden_rows).astype(jnp.bfloat16)
    feedforward_output = (
        jnp.dot(activated_hidden, down_weight, preferred_element_type=jnp.float32) + vec_f32[5]
    )
    pre_two = first_normed + feedforward_output
    encoded = layer_norm(pre_two, vec_f32[6], vec_f32[7])
    stored = (
        queries,
        keys_low,
        values,
        totals,
        attended_tokens,
        pre_one,
        normed_low,
        hidden_rows,
        activated_hidden,
        pre_two,
    )
    return (encoded, stored)


def encode_backward(token_rows, lengths, weights, stored, grad_encoded):
    (
        query_key_value_weight,
        attention_output_weight,
        up_weight,
        down_weight,
        vectors,
        hidden_bias,
    ) = weights
    (
        queries,
        keys_low,
        values,
        totals,
        attended_tokens,
        pre_one,
        normed_low,
        hidden_rows,
        activated_hidden,
        pre_two,
    ) = stored
    row_count, model_width = token_rows.shape
    seq_count = lengths.shape[0]
    vec_f32 = vectors.astype(jnp.float32)
    norm_two_back = jax.vjp(layer_norm, pre_two, vec_f32[6], vec_f32[7])[1]
    grad_two, grad_gain_two, grad_offset_two = norm_two_back(grad_encoded)
    grad_ffn = grad_two.astype(jnp.bfloat16)
    grad_w_back = jnp.einsum(
        "rf,rd->fd", activated_hidden, grad_ffn, preferred_element_type=jnp.float32
    )
    grad_activated = jnp.einsum(
        "rd,fd->rf", grad_ffn, down_weight, preferred_element_type=jnp.float32
    )
    gate_back = jax.vjp(smooth_gate, hidden_rows)[1]
    grad_hidden = gate_back(grad_activated)[0].astype(jnp.bfloat16)
    grad_w_in = jnp.einsum("rd,rf->df", normed_low, grad_hidden, preferred_element_type=jnp.float32)
    grad_normed = grad_two + jnp.einsum(
        "rf,df->rd", grad_hidden, up_weight, preferred_element_type=jnp.float32
    )
    norm_one_back = jax.vjp(layer_norm, pre_one, vec_f32[3], vec_f32[4])[1]
    grad_one, grad_gain_one, grad_offset_one = norm_one_back(grad_normed)
    grad_branch = grad_one.astype(jnp.bfloat16)
    grad_w_out = jnp.einsum(
        "rd,re->de", attended_tokens, grad_branch, preferred_element_type=jnp.float32
    )
    grad_attended = jnp.einsum(
        "re,de->rd", grad_branch, attention_output_weight, preferred_element_type=jnp.float32
    ).astype(jnp.bfloat16)
    scores = attention_scores(queries, keys_low, lengths)
    soft_f32 = jnp.exp(scores - totals)
    soft_low = soft_f32.astype(jnp.bfloat16)
    grad_heads = head_split(grad_attended, seq_count)
    grad_soft = jnp.einsum(
        "sqhc,skhc->shqk",
        grad_heads,
        head_split(values, seq_count),
        preferred_element_type=jnp.float32,
    )
    grad_values = jnp.einsum(
        "shqk,sqhc->skhc", soft_low, grad_heads, preferred_element_type=jnp.float32
    )
    row_inner = jnp.sum(soft_f32 * grad_soft, axis=-1, keepdims=True)
    grad_scores = (soft_f32 * (grad_soft - row_inner)).astype(jnp.bfloat16)
    scaling = (model_width // HEADS) ** (-0.5)
    grad_queries = (
        jnp.einsum(
            "shqk,skhc->sqhc",
            grad_scores,
            head_split(keys_low, seq_count),
            preferred_element_type=jnp.float32,
        )
        * scaling
    )
    grad_keys = (
        jnp.einsum(
            "shqk,sqhc->skhc",
            grad_scores,
            head_split(queries, seq_count),
            preferred_element_type=jnp.float32,
        )
        * scaling
    )
    grad_q_low = grad_queries.reshape(row_count, model_width).astype(jnp.bfloat16)
    grad_k_low = grad_keys.reshape(row_count, model_width).astype(jnp.bfloat16)
    grad_v_low = grad_values.reshape(row_count, model_width).astype(jnp.bfloat16)
    grad_projected = jnp.concatenate([grad_q_low, grad_k_low, grad_v_low], axis=1)
    grad_w_qkv = jnp.einsum(
        "rd,re->de", token_rows, grad_projected, preferred_element_type=jnp.float32
    )
    grad_tokens = grad_one + jnp.einsum(
        "re,de->rd", grad_projected, query_key_value_weight, preferred_element_type=jnp.float32
    )
    vector_grads = jnp.stack(
        [
            column_total(grad_q_low),
            column_total(grad_v_low),
            column_total(grad_branch),
            grad_gain_one,
            grad_offset_one,
            column_total(grad_ffn),
            grad_gain_two,
            grad_offset_two,
        ]
    )
    return (
        grad_tokens,
        grad_w_qkv,
        grad_w_out,
        grad_w_in,
        grad_w_back,
        vector_grads,
        column_total(grad_hidden),
    )


def combine_rows(first_part, second_part):
    highest = jnp.maximum(first_part[0], second_part[0])
    merged = first_part[1] * jnp.exp(first_part[0] - highest) + second_part[1] * jnp.exp(
        second_part[0] - highest
    )
    return (highest, merged, first_part[2] + second_part[2])


def shards(
    q_embed,
    p_embed,
    q_len,
    p_len,
    q_set,
    p_set,
    gold,
    query_key_value_weight,
    attention_output_weight,
    up_weight,
    down_weight,
    vectors,
    hidden_bias,
):
    gathered = gather_weights(
        query_key_value_weight,
        attention_output_weight,
        up_weight,
        down_weight,
        vectors,
        hidden_bias,
    )
    q_weights = tuple((member[0] for member in gathered))
    p_weights = tuple((member[1] for member in gathered))
    q_encoded, q_stored = encode_forward(q_embed, q_len, q_weights)
    p_encoded, p_stored = encode_forward(p_embed, p_len, p_weights)
    model_width = q_embed.shape[1]
    q_count = q_len.shape[0]
    p_count = p_len.shape[0]
    q_slots = q_embed.shape[0] // q_count
    p_slots = p_embed.shape[0] // p_count
    q_heads = q_encoded.reshape(q_count, q_slots, model_width)[:, 0, :].astype(jnp.bfloat16)
    p_heads = p_encoded.reshape(p_count, p_slots, model_width)[:, 0, :].astype(jnp.bfloat16)
    row_heads, row_sets, row_gold = (
        lax.all_gather(q_heads, "np", axis=0, tiled=True),
        lax.all_gather(q_set, "np", axis=0, tiled=True),
        lax.all_gather(gold, "np", axis=0, tiled=True),
    )
    col_heads, col_sets = (
        lax.all_gather(p_heads, "wq", axis=0, tiled=True),
        lax.all_gather(p_set, "wq", axis=0, tiled=True),
    )
    column = jnp.arange(col_heads.shape[0], dtype=jnp.int32)
    col_global = (
        column // p_count * lax.axis_size("np") + lax.axis_index("np")
    ) * p_count + column % p_count
    scaling = model_width ** (-0.5)
    similar = (
        jnp.einsum("qd,pd->qp", row_heads, col_heads, preferred_element_type=jnp.float32) * scaling
    )
    is_gold = col_global[None, :] == row_gold[:, None]
    usable = (row_sets[:, None] == col_sets[None, :]) | is_gold
    masked = jnp.where(usable, similar, NEGATIVE)
    local_high = jnp.max(masked, axis=1)
    local_total = jnp.sum(jnp.where(usable, jnp.exp(masked - local_high[:, None]), 0.0), axis=1)
    local_gold = jnp.sum(jnp.where(is_gold, similar, 0.0), axis=1)
    highest, row_total, gold_score = combined_all(
        (local_high, local_total, local_gold), "np", combine_rows
    )
    log_total = highest + jnp.log(row_total)
    loss_sum = lax.psum(jnp.sum(log_total - gold_score), "wq")
    loss = loss_sum / (row_heads.shape[0] * lax.axis_size("wq"))
    soft_rows = jnp.where(usable, jnp.exp(masked - log_total[:, None]), 0.0)
    grad_similar = (soft_rows - is_gold.astype(jnp.float32)).astype(jnp.bfloat16)
    grad_rows = (
        jnp.einsum("qp,pd->qd", grad_similar, col_heads, preferred_element_type=jnp.float32)
        * scaling
    )
    grad_cols = (
        jnp.einsum("qp,qd->pd", grad_similar, row_heads, preferred_element_type=jnp.float32)
        * scaling
    )
    grad_q_heads = lax.psum_scatter(
        grad_rows.astype(jnp.bfloat16), "np", scatter_dimension=0, tiled=True
    ).astype(jnp.float32)
    grad_p_heads = lax.psum_scatter(grad_cols, "wq", scatter_dimension=0, tiled=True)
    grad_q_encoded = jnp.pad(grad_q_heads[:, None, :], ((0, 0), (0, q_slots - 1), (0, 0))).reshape(
        q_embed.shape[0], model_width
    )
    grad_p_encoded = jnp.pad(grad_p_heads[:, None, :], ((0, 0), (0, p_slots - 1), (0, 0))).reshape(
        p_embed.shape[0], model_width
    )
    p_grads = encode_backward(p_embed, p_len, p_weights, p_stored, grad_p_encoded)
    q_grads = encode_backward(q_embed, q_len, q_weights, q_stored, grad_q_encoded)
    shared = reduce_grads(
        tuple(
            (
                jnp.stack([q_member, p_member])
                for q_member, p_member in zip(q_grads[1:], p_grads[1:])
            )
        )
    )
    return (
        loss,
        q_encoded.astype(jnp.bfloat16),
        p_encoded.astype(jnp.bfloat16),
        q_grads[0],
        p_grads[0],
        shared[0],
        shared[1],
        shared[2],
        shared[3],
        shared[4],
        shared[5],
    )


def solution(mesh):
    return jax.shard_map(
        shards,
        mesh=mesh,
        in_specs=(
            P(("wq", "np"), None),
            P(("wq", "np"), None),
            P(("wq", "np")),
            P(("wq", "np")),
            P(("wq", "np")),
            P(("wq", "np")),
            P(("wq", "np")),
            P(None, "wq", "np"),
            P(None, "wq", "np"),
            P(None, "wq", "np"),
            P(None, "wq", "np"),
            P(None, "np", "wq"),
            P(None, ("wq", "np")),
        ),
        out_specs=(
            P(),
            P(("wq", "np"), None),
            P(("wq", "np"), None),
            P(("wq", "np"), None),
            P(("wq", "np"), None),
            P(None, "wq", "np"),
            P(None, "wq", "np"),
            P(None, "wq", "np"),
            P(None, "wq", "np"),
            P(None, "np", "wq"),
            P(None, ("wq", "np")),
        ),
        check_vma=False,
    )
```

profile of v0, /device:TPU:0, one launch (start us, length us, event | category | flops | bytes accessed | tf_op | source)
XLA Modules:
  0.0 1223.4 jit_solution(18406497182007926918)
XLA Ops:
  7.2 11.0 all_gather.72
  18.4 5.3 all_gather.76
  23.8 9.7 all_gather.78
  33.6 7.7 all_gather.82
  44.1 4.4 all-gather.5
  49.2 22.4 %all-gather.6 = bf16[16,192,2]{1,2,0:T(2,128)(2,1)S(1)} all-gather(bf16[1,192,2]{1,2,0:T(2,128)(2,1)S(1)} %reshape.453), channel_id=1, replica_groups=mesh['wq'=16,'np'=2] {'wq'}, dimensions={0}, use_global_device_ids=true | all-gather | bytes 13056 | tf_op jit(solution)/shard_map/all_gather | solution.py:54
  71.7 4.3 all_gather.74
  80.0 4.3 all-reduce.12
  84.3 7.0 all-reduce.3
  91.3 23.8 %all_gather.75 = bf16[2,8,768]{1,0,2:T(2,128)(2,1)S(1)} all-gather(bf16[2,8,48]{1,0,2:T(2,128)(2,1)S(1)} %copy.243), channel_id=1, replica_groups=mesh['wq'=16,'np'=2] {'wq'}, dimensions={2}, use_global_device_ids=true | all-gather | bytes 26112 | tf_op jit(solution)/shard_map/all_gather | solution.py:53
  115.9 47.1 %slice_reduce_fusion.1 = (f32[768]{0:T(1024)S(1)}, f32[768]{0:T(1024)S(1)}, f32[768]{0:T(1024)S(1)}, f32[768]{0:T(1024)S(1)}, f32[768]{0:T(1024)S(1)}, /*index=5...) fusion(f32[1,8,768]{1,0,2:T(1,128)S(1)} %get-tuple-element.157,, ...), kind=kLoop, calls=%fused_computation.150 | loop fusion | bytes 98304 | tf_op jit(solution)/shard_map/slice | solution.py:161
  163.1 4.0 fusion.36
  189.3 8.8 fusion.37
  202.0 6.0 reshape.487
  208.0 6.4 copy.258
  214.4 8.9 reshape.488
  223.3 7.3 copy.259
  230.6 8.2 reshape.486
  238.8 7.3 copy.260
  246.1 10.9 fusion.8
  257.1 12.3 %exponential_reduce_fusion = f32[6,12,256]{2,1,0:T(8,128)S(1)} fusion(f32[6,12,256,256]{2,3,1,0:T(8,128)} %get-tuple-element.168, f32[6,12,256]{2,1,0:T(8,128)S(1)} %is-finite_select_fusion, pred[6,256]{1,0:T(8,128)(4,1)S(1)} %iota_compare_fusion), kind=kLoop, calls=%fused_computation.13 | loop fusion | flops 18855936 | bytes 19023360 | tf_op jit(solution)/shard_map/reduce_sum | solution.py:137
  269.4 8.8 convert_bitcast_fusion
  291.9 7.4 fusion.27
  299.4 8.4 fusion.111
  310.3 4.4 all-gather
  314.7 11.5 fusion.31
  326.2 17.3 %fusion.109 = (f32[1536]{0:T(1024)S(1)}, f32[1536,768]{1,0:T(8,128)S(1)}) fusion(f32[768]{0:T(1024)S(1)} %get-tuple-element.121, bf16[2,3072,768]{2,1,0:T(8,128)(2,1)} %all-gather.18.cloned.1.call-done, f32[1536,3072]{1,0:T(8,128)} %fusion.31, f32[3072]{0:T(1024)S(1)} %bitcast.278, f32[768]{0:T(1024)S(1)} %get-tuple-element.122, ...), kind=kOutput, calls=%fused_computation.257 | convolution fusion | flops 7303199232 | bytes 33070080 | tf_op jit(solution)/shard_map/dot_general | solution.py:158
  347.1 18.3 %all-gather.1 = bf16[96,1,768]{2,1,0:T(2,128)(2,1)S(1)} all-gather(bf16[6,1,768]{2,1,0:T(2,128)(2,1)S(1)} %slice.224), channel_id=3, replica_groups=mesh['wq'=16,'np'=2] {'wq'}, dimensions={0}, use_global_device_ids=true | all-gather | bytes 156672 | tf_op jit(solution)/shard_map/all_gather | solution.py:340
  366.5 4.9 all-reduce.13
  372.5 33.4 %fusion = f32[8,768]{1,0:T(8,128)S(1)} fusion(f32[96,768]{1,0:T(8,128)S(1)} %convolution_multiply_fusion), kind=kCustom, calls=%all-reduce-scatter | all-reduce-scatter fusion | flops 98305 | bytes 320000
  421.7 24.3 %fusion.116 = (bf16[3072]{0:T(1024)(128)(2,1)S(1)}, bf16[1536,3072]{1,0:T(8,128)(2,1)}) fusion(f32[1536,3072]{1,0:T(8,128)} %fusion.31, f32[3072]{0:T(1024)S(1)} %bitcast.279, bf16[1536,768]{1,0:T(8,128)(2,1)S(1)} %get-tuple-element.139, bf16[2,3072,768]{2,1,0:T(8,128)(2,1)} %all-gather.18.cloned.1.call-done), kind=kOutput, calls=%fused_computation.264 | convolution fusion | flops 7351563264 | bytes 35407872 | tf_op jit(solution)/shard_map/rd,fd->rf/dot_general | solution.py:207
  446.0 13.5 %multiply_reduce_fusion.1 = (bf16[768]{0:T(1024)(128)(2,1)}, f32[1536]{0:T(1024)S(1)}, bf16[768]{0:T(1024)(128)(2,1)}, f32[1536,768]{1,0:T(8,128)S(1)}) fusion(f32[1536,768]{1,0:T(8,128)S(1)} %bitcast.247, f32[1536]{0:T(1024)S(1)} %fusion.71, f32[1536]{0:T(1024)S(1)} %broadcast_multiply_fusion.1, f32[768]{0:T(1024)S(1)} %get-tuple-element.123, ...), kind=kOutput, calls=%fused_computation.50 | convolution fusion | flops 7259550720 | bytes 28342272 | tf_op jit(solution)/shard_map/rf,df->rd/dot_general | solution.py:213
  468.9 6.1 reshape.490
  475.0 7.3 copy.278
  482.4 11.4 fusion.113
  493.8 15.0 %multiply_reduce_fusion = (f32[6,12,256]{2,1,0:T(8,128)S(1)}, f32[6,12,256,256]{2,3,1,0:T(8,128)}) fusion(f32[6,12,256,256]{2,3,1,0:T(8,128)} %get-tuple-element.168, f32[6,12,256]{2,1,0:T(8,128)S(1)} %copy-done.38, pred[6,256]{1,0:T(8,128)(4,1)S(1)} %copy-done.51, bf16[6,256,12,64]{1,3,2,0:T(8,128)(2,1)} %copy.278, bf16[6,256,12,64]{1,3,2,0:T(8,128)(2,1)S(1)} %copy-done.16), kind=kOutput, calls=%fused_computation.10 | convolution fusion | flops 627554304 | bytes 42616320 | tf_op jit(solution)/shard_map/sqhc,skhc->shqk/dot_general | solution.py:229
  508.8 14.1 %multiply_convert_fusion = bf16[6,12,256,256]{2,3,1,0:T(8,128)(2,1)S(1)} fusion(f32[6,12,256,256]{2,3,1,0:T(8,128)} %get-tuple-element.186, f32[6,12,256,256]{2,3,1,0:T(8,128)} %get-tuple-element.168, f32[6,12,256]{2,1,0:T(8,128)S(1)} %get-tuple-element.185, f32[6,12,256]{2,1,0:T(8,128)S(1)} %copy-done.38, pred[6,256]{1,0:T(8,128)(4,1)S(1)} %copy-done.51), kind=kLoop, calls=%fused_computation.9 | loop fusion | flops 28311552 | bytes 47334912 | tf_op jit(solution)/shard_map/convert_element_type | solution.py:239
  522.9 4.3 fusion.39
  539.1 7.2 fusion.21
  552.0 8.3 fusion.117
  573.0 3.9 reshape.489
  576.9 4.1 fusion.115
  587.3 4.1 multiply_reduce_fusion.6
  616.5 18.2 %copy.289 = bf16[2,768,2304]{2,0,1:T(2,128)(2,1)} copy(bf16[2,768,2304]{1,2,0:T(8,128)(2,1)} %pad_maximum_fusion.2) | data formatting | bytes 14155776 | tf_op jit(solution)/shard_map/stack | solution.py:388
  636.5 17.0 %fusion.25 = bf16[1,3072,768]{2,1,0:T(8,128)(2,1)} fusion(bf16[1536,768]{1,0:T(8,128)(2,1)S(1)} %copy-done.29, f32[1536,3072]{1,0:T(8,128)} %fusion.31, f32[3072]{0:T(1024)S(1)} %bitcast.280), kind=kOutput, calls=%fused_computation.66 | convolution fusion | flops 7297302528 | bytes 25964544 | tf_op jit(solution)/shard_map/rf,rd->fd/dot_general | solution.py:204
  653.5 8.6 fusion.23
  662.1 8.3 pad_maximum_fusion.1
  671.1 14.4 %fusion.20 = bf16[1,768,3072]{2,1,0:T(8,128)(2,1)} fusion(bf16[1536,3072]{1,0:T(8,128)(2,1)} %get-tuple-element.196, f32[1536,768]{1,0:T(8,128)} %copy-done.10, f32[768]{0:T(1024)S(1)} %copy-done.89, f32[768]{0:T(1024)S(1)} %copy-done.75, f32[1536]{0:T(1024)S(1)} %copy-done.63, f32[1536]{0:T(1024)S(1)} %copy-done.53), kind=kOutput, calls=%fused_computation.61 | convolution fusion | flops 7256014848 | bytes 18892800 | tf_op jit(solution)/shard_map/rd,rf->df/dot_general | solution.py:212
  685.5 4.8 fusion.22
  690.3 8.3 pad_maximum_fusion
  704.3 142.4 %all-reduce.16.cloned.1.call-done = bf16[2,768,2304]{2,0,1:T(2,128)(2,1)} async-done(((bf16[2,768,2304]{2,0,1:T(2,128)(2,1)}), bf16[2,768,2304]{2,0,1:T(2,128)(2,1)}) %all-reduce.16.cloned.1.call-update) | async-done | bytes 7077904
  848.0 24.1 %copy.299 = bf16[2,48,2304]{0,1,2:T(8,128)(2,1)} copy(bf16[2,48,2304]{2,0,1:T(2,128)(2,1)S(1)} %constant_dynamic-slice_fusion) | data formatting | bytes 884736
  872.1 30.4 %reshape.468 = bf16[2304,96]{1,0:T(8,128)(2,1)} reshape(bf16[2304,48,2]{2,1,0:T(8,128)(2,1)} %bitcast.242) | data formatting | bytes 884736
  902.6 59.7 %reduce-scatter.35.cloned.1.call-done = bf16[2,192,768]{2,1,0:T(8,128)(2,1)} async-done(((bf16[2,3072,768]{2,1,0:T(8,128)(2,1)}), bf16[2,192,768]{2,1,0:T(8,128)(2,1)}) %reduce-scatter.35.cloned.1.call-update) | async-done | bytes 589840 | tf_op jit(solution)/shard_map/reduce_scatter | solution.py:69
  966.5 32.9 %psum.7 = f32[]{:T(128)} all-reduce(f32[]{:T(128)} %get-tuple-element.150), channel_id=1, replica_groups=mesh['wq'=16,'np'=2] {'wq'}, use_global_device_ids=true, to_apply=%region_16.17 | all-reduce | flops 1 | bytes 8 | tf_op jit(solution)/shard_map/psum | solution.py:361
  1000.0 77.9 %reduce-scatter.31.cloned.1.call-done = bf16[2,48,3072]{2,1,0:T(8,128)(2,1)} async-done(((bf16[2,768,3072]{2,1,0:T(8,128)(2,1)}), bf16[2,48,3072]{2,1,0:T(8,128)(2,1)}) %reduce-scatter.31.cloned.1.call-update) | async-done | bytes 589840 | tf_op jit(solution)/shard_map/reduce_scatter | solution.py:66
  1078.0 11.7 add_add_fusion.4
  1089.7 5.2 add_add_fusion.10
  1096.3 50.5 %reduce-scatter.43.cloned.1.call-done = bf16[48,16]{1,0:T(8,128)(2,1)} async-done(((bf16[768,16]{1,0:T(8,128)(2,1)}), bf16[48,16]{1,0:T(8,128)(2,1)}) %reduce-scatter.43.cloned.1.call-update) | async-done | bytes 1552
  1147.7 4.9 all-reduce.10
  1153.2 6.4 reduce-scatter.39.cloned.1.call-done
  1161.5 16.2 %reduce-scatter.37.cloned.1.call-done = bf16[1152,96]{1,0:T(8,128)(2,1)} async-done(((bf16[2304,96]{1,0:T(8,128)(2,1)}), bf16[1152,96]{1,0:T(8,128)(2,1)}) %reduce-scatter.37.cloned.1.call-update) | async-done | bytes 221200
  1177.6 17.8 %reshape.469 = bf16[1152,48,2]{2,1,0:T(8,128)(2,1)} reshape(bf16[1152,96]{1,0:T(8,128)(2,1)} %reduce-scatter.37.cloned.1.call-done) | data formatting | bytes 442368
  1195.5 14.5 %copy.300 = bf16[2,48,1152]{2,0,1:T(2,128)(2,1)S(1)} copy(bf16[2,48,1152]{0,1,2:T(8,128)(2,1)} %bitcast.243) | data formatting | bytes 442368
  (444 shorter events, 161.9 us)
Async XLA Ops:
  7.2 108.0 %copy-start.100 = (s32[8]{0:T(128)S(1)}, s32[8]{0:T(128)}, u32[]{:S(2)}) copy-start(s32[8]{0:T(128)} %param.15) | copy-start | bytes 100
  7.2 108.0 %copy-start.93 = (s32[6]{0:T(128)S(1)}, s32[6]{0:T(128)}, u32[]{:S(2)}) copy-start(s32[6]{0:T(128)} %param.16) | copy-start | bytes 76
  7.2 155.9 %all-gather.12.cloned.1.call-start = ((), (), s32[]{:S(2)}) async-start(), calls=%async_computation.11 | async-start | bytes 7520256 | tf_op jit(solution)/shard_map/all_gather | solution.py:49
  18.3 263.9 %all-gather.14.cloned.1.call-start = ((), (), s32[]{:S(2)}) async-start(), calls=%async_computation.12 | async-start | bytes 2506752 | tf_op jit(solution)/shard_map/all_gather | solution.py:50
  23.7 268.2 %all-gather.16.cloned.1.call-start = ((), (), s32[]{:S(2)}) async-start(), calls=%async_computation.13 | async-start | bytes 10027008 | tf_op jit(solution)/shard_map/all_gather | solution.py:51
  33.5 265.8 %all-gather.18.cloned.1.call-start = ((), (), s32[]{:S(2)}) async-start(), calls=%async_computation.14 | async-start | bytes 10027008 | tf_op jit(solution)/shard_map/all_gather | solution.py:52
  41.3 121.8 %copy-start.98 = (bf16[512,768]{1,0:T(8,128)(2,1)S(1)}, bf16[512,768]{1,0:T(8,128)(2,1)}, u32[]{:S(2)}) copy-start(bf16[512,768]{1,0:T(8,128)(2,1)} %param.13) | copy-start | bytes 2359300
  41.3 507.1 %reduce-scatter.27.cloned.1.call-start = ((), (), s32[]{:S(2)}) async-start(), calls=%async_computation.15 | async-start | bytes 36864 | tf_op jit(solution)/shard_map/reduce_scatter | solution.py:373
  115.2 70.6 %copy-start.64 = (pred[8,64]{1,0:T(8,128)(4,1)}, pred[8,64]{1,0:T(8,128)(4,1)S(1)}, u32[]{:S(2)}) copy-start(pred[8,64]{1,0:T(8,128)(4,1)S(1)} %iota_compare_fusion.1) | copy-start | bytes 1540
  115.3 154.1 %copy-start.50 = (pred[6,256]{1,0:T(8,128)(4,1)}, pred[6,256]{1,0:T(8,128)(4,1)S(1)}, u32[]{:S(2)}) copy-start(pred[6,256]{1,0:T(8,128)(4,1)S(1)} %iota_compare_fusion) | copy-start | bytes 4612
  115.9 183.4 %copy-start.77 = (f32[1,3072]{1,0:T(1,128)}, f32[1,3072]{1,0:T(1,128)S(1)}, u32[]{:S(2)}) copy-start(f32[1,3072]{1,0:T(1,128)S(1)} %get-tuple-element.160) | copy-start | bytes 36868
  115.9 305.8 %copy-start.79 = (f32[1,3072]{1,0:T(1,128)}, f32[1,3072]{1,0:T(1,128)S(1)}, u32[]{:S(2)}) copy-start(f32[1,3072]{1,0:T(1,128)S(1)} %get-tuple-element.161) | copy-start | bytes 36868
  163.0 136.3 %copy-start.72 = (f32[768]{0:T(1024)}, f32[768]{0:T(1024)S(1)}, u32[]{:S(2)}) copy-start(f32[768]{0:T(1024)S(1)} %get-tuple-element.205) | copy-start | bytes 9220
  163.0 136.3 %copy-start.86 = (f32[768]{0:T(1024)}, f32[768]{0:T(1024)S(1)}, u32[]{:S(2)}) copy-start(f32[768]{0:T(1024)S(1)} %get-tuple-element.206) | copy-start | bytes 9220
  163.1 145.1 %copy-start.54 = (f32[768]{0:T(1024)}, f32[768]{0:T(1024)S(1)}, u32[]{:S(2)}) copy-start(f32[768]{0:T(1024)S(1)} %get-tuple-element.209) | copy-start | bytes 9220
  163.1 163.1 %copy-start.88 = (f32[768]{0:T(1024)}, f32[768]{0:T(1024)S(1)}, u32[]{:S(2)}) copy-start(f32[768]{0:T(1024)S(1)} %get-tuple-element.122) | copy-start | bytes 9220
  163.1 296.5 %copy-start.74 = (f32[768]{0:T(1024)}, f32[768]{0:T(1024)S(1)}, u32[]{:S(2)}) copy-start(f32[768]{0:T(1024)S(1)} %get-tuple-element.123) | copy-start | bytes 9220
  189.3 92.9 %copy-start.41 = (bf16[512,768]{0,1:T(8,128)(2,1)}, bf16[512,768]{0,1:T(8,128)(2,1)S(1)}, u32[]{:S(2)}) copy-start(bf16[512,768]{0,1:T(8,128)(2,1)S(1)} %convert_element_type.273) | copy-start | bytes 2359300
  214.4 31.7 %copy-start.4 = (bf16[6,256,12,64]{1,3,2,0:T(8,128)(2,1)}, bf16[6,256,12,64]{1,3,2,0:T(8,128)(2,1)S(1)}, u32[]{:S(2)}) copy-start(bf16[6,256,12,64]{1,3,2,0:T(8,128)(2,1)S(1)} %copy.258) | copy-start | bytes 7077892
  257.1 12.3 %copy-start.15 = (bf16[6,256,12,64]{1,3,2,0:T(8,128)(2,1)S(1)}, bf16[6,256,12,64]{1,3,2,0:T(8,128)(2,1)}, u32[]{:S(2)}) copy-start(bf16[6,256,12,64]{1,3,2,0:T(8,128)(2,1)} %copy.260) | copy-start | bytes 7077892
  269.4 8.9 copy-start.37
  284.8 14.6 %copy-start.18 = (f32[512,768]{1,0:T(8,128)}, f32[512,768]{1,0:T(8,128)S(1)}, u32[]{:S(2)}) copy-start(f32[512,768]{1,0:T(8,128)S(1)} %get-tuple-element.176) | copy-start | bytes 4718596
  284.8 14.6 %copy-start.66 = (f32[512]{0:T(512)}, f32[512]{0:T(512)S(1)}, u32[]{:S(2)}) copy-start(f32[512]{0:T(512)S(1)} %broadcast_multiply_fusion.3) | copy-start | bytes 6148
  285.1 14.2 %copy-start.81 = (f32[512]{0:T(512)}, f32[512]{0:T(512)S(1)}, u32[]{:S(2)}) copy-start(f32[512]{0:T(512)S(1)} %fusion.75) | copy-start | bytes 6148
  289.0 170.5 %copy-start.52 = (f32[1536]{0:T(1024)}, f32[1536]{0:T(1024)S(1)}, u32[]{:S(2)}) copy-start(f32[1536]{0:T(1024)S(1)} %broadcast_multiply_fusion.1) | copy-start | bytes 18436
  291.9 167.7 %copy-start.62 = (f32[1536]{0:T(1024)}, f32[1536]{0:T(1024)S(1)}, u32[]{:S(2)}) copy-start(f32[1536]{0:T(1024)S(1)} %fusion.71) | copy-start | bytes 18436
  291.9 22.7 %slice-start = ((s8[4718592]{0:T(1024)(128)(4,1)}), s8[524288]{0:T(1024)(128)(4,1)S(1)}, s32[]{:S(2)}) async-start(s8[4718592]{0:T(1024)(128)(4,1)} %bitcast.244), calls=%async_computation.27 | async-start | bytes 1048576
  299.4 15.3 %slice-start.1 = ((s8[4718592]{0:T(1024)(128)(4,1)}), s8[4194304]{0:T(1024)(128)(4,1)S(1)}, s32[]{:S(2)}) async-start(s8[4718592]{0:T(1024)(128)(4,1)} %bitcast.244), calls=%async_computation.28 | async-start | bytes 8388608
  299.4 15.3 %copy-start.94 = (bf16[2,768,3072]{2,1,0:T(8,128)(2,1)S(1)}, bf16[2,768,3072]{2,1,0:T(8,128)(2,1)}, u32[]{:S(2)}) copy-start(bf16[2,768,3072]{2,1,0:T(8,128)(2,1)} %all-gather.16.cloned.1.call-done) | copy-start | bytes 28311556
  307.8 18.4 %copy-start.56 = (f32[512]{0:T(512)}, f32[512]{0:T(512)S(1)}, u32[]{:S(2)}) copy-start(f32[512]{0:T(512)S(1)} %broadcast_multiply_fusion.2) | copy-start | bytes 6148
  308.1 18.0 %copy-start.70 = (f32[512]{0:T(512)}, f32[512]{0:T(512)S(1)}, u32[]{:S(2)}) copy-start(f32[512]{0:T(512)S(1)} %multiply_reduce_fusion.10) | copy-start | bytes 6148
  308.2 18.0 %copy-start.58 = (f32[512]{0:T(512)}, f32[512]{0:T(512)S(1)}, u32[]{:S(2)}) copy-start(f32[512]{0:T(512)S(1)} %fusion.76) | copy-start | bytes 6148
  405.9 6.7 collective-permute-start.2
  407.2 5.4 collective-permute-start.1
  408.5 4.1 collective-permute-start
  409.8 2.8 collective-permute-start.3
  412.0 288.0 %reduce-scatter.45.cloned.1.call-start = ((), (), s32[]{:S(2)}) async-start(), calls=%async_computation.24 | async-start | bytes 835584
  420.6 25.4 %slice-start.2 = ((s8[4718592]{0:T(1024)(128)(4,1)}), s8[4194304]{0:T(1024)(128)(4,1)S(1)}, s32[]{:S(2)}) async-start(s8[4718592]{0:T(1024)(128)(4,1)} %bitcast.246), calls=%async_computation.29 | async-start | bytes 8388608
  421.7 24.3 %copy-start.28 = (bf16[1536,768]{1,0:T(8,128)(2,1)}, bf16[1536,768]{1,0:T(8,128)(2,1)S(1)}, u32[]{:S(2)}) copy-start(bf16[1536,768]{1,0:T(8,128)(2,1)S(1)} %get-tuple-element.139) | copy-start | bytes 7077892
  421.7 24.3 %slice-start.3 = ((s8[4718592]{0:T(1024)(128)(4,1)}), s8[524288]{0:T(1024)(128)(4,1)S(1)}, s32[]{:S(2)}) async-start(s8[4718592]{0:T(1024)(128)(4,1)} %bitcast.246), calls=%async_computation.30 | async-start | bytes 1048576
  482.4 11.4 copy-start.16
  508.8 14.1 %copy-start.5 = (bf16[6,256,12,64]{1,3,2,0:T(8,128)(2,1)S(1)}, bf16[6,256,12,64]{1,3,2,0:T(8,128)(2,1)}, u32[]{:S(2)}) copy-start(bf16[6,256,12,64]{1,3,2,0:T(8,128)(2,1)} %copy-done.4) | copy-start | bytes 7077892
  550.7 9.7 slice-start.4
  551.5 8.8 copy-start.43
  551.9 8.4 copy-start.82
  552.0 8.4 slice-start.5
  552.0 8.4 slice-start.6
  567.8 134.3 %reduce-scatter.29.cloned.1.call-start = ((), (), s32[]{:S(2)}) async-start(), calls=%async_computation.16 | async-start | bytes 2506752 | tf_op jit(solution)/shard_map/reduce_scatter | solution.py:63
  569.6 277.2 %all-reduce.16.cloned.1.call-start = ((), (), s32[]{:S(2)}) async-start(), calls=%async_computation.26 | async-start | bytes 14155776
  634.8 18.7 %copy-start.44 = (bf16[512,768]{1,0:T(8,128)(2,1)S(1)}, bf16[512,768]{1,0:T(8,128)(2,1)}, u32[]{:S(2)}) copy-start(bf16[512,768]{1,0:T(8,128)(2,1)} %copy-done.43) | copy-start | bytes 2359300
  634.8 327.5 %reduce-scatter.35.cloned.1.call-start = ((), (), s32[]{:S(2)}) async-start(), calls=%async_computation.19 | async-start | bytes 10027008 | tf_op jit(solution)/shard_map/reduce_scatter | solution.py:69
  670.4 15.1 %copy-start.20 = (f32[512,768]{1,0:T(8,128)S(1)}, f32[512,768]{1,0:T(8,128)}, u32[]{:S(2)}) copy-start(f32[512,768]{1,0:T(8,128)} %copy-done.18) | copy-start | bytes 4718596
  670.5 15.1 %copy-start.87 = (f32[768]{0:T(1024)S(1)}, f32[768]{0:T(1024)}, u32[]{:S(2)}) copy-start(f32[768]{0:T(1024)} %copy-done.86) | copy-start | bytes 9220
  670.5 407.5 %reduce-scatter.31.cloned.1.call-start = ((), (), s32[]{:S(2)}) async-start(), calls=%async_computation.17 | async-start | bytes 10027008 | tf_op jit(solution)/shard_map/reduce_scatter | solution.py:66
  671.1 14.4 %copy-start.102 = (bf16[512,3072]{1,0:T(8,128)(2,1)S(1)}, bf16[512,3072]{1,0:T(8,128)(2,1)}, u32[]{:S(2)}) copy-start(bf16[512,3072]{1,0:T(8,128)(2,1)} %copy-done.101) | copy-start | bytes 9437188
  698.6 396.3 %reduce-scatter.47.cloned.1.call-start = ((), (), s32[]{:S(2)}) async-start(), calls=%async_computation.25 | async-start | bytes 73728
  700.0 446.8 %reduce-scatter.43.cloned.1.call-start = ((), (), s32[]{:S(2)}) async-start(), calls=%async_computation.23 | async-start | bytes 208896
  701.4 458.2 %reduce-scatter.39.cloned.1.call-start = ((), (), s32[]{:S(2)}) async-start(), calls=%async_computation.21 | async-start | bytes 294912
  704.3 473.3 %reduce-scatter.37.cloned.1.call-start = ((), (), s32[]{:S(2)}) async-start(), calls=%async_computation.20 | async-start | bytes 884736
  872.1 205.8 %copy-start.61 = (f32[1536]{0:T(1024)S(1)}, f32[1536]{0:T(1024)}, u32[]{:S(2)}) copy-start(f32[1536]{0:T(1024)} %copy-done.60) | copy-start | bytes 18436
  902.5 308.3 %reduce-scatter.41.cloned.1.call-start = ((), (), s32[]{:S(2)}) async-start(), calls=%async_computation.22 | async-start | bytes 884736
  965.8 247.9 %reduce-scatter.33.cloned.1.call-start = ((), (), s32[]{:S(2)}) async-start(), calls=%async_computation.18 | async-start | bytes 884736 | tf_op jit(solution)/shard_map/reduce_scatter | solution.py:86
  1078.0 11.7 copy-start.22
  1078.0 11.7 copy-start.47
  (68 other events, 204.7 us)
Sparse Core Ops, SparseCore 0:
  18.4 67.0 all-gather.11
  87.8 41.5 all-gather.13
  131.7 80.2 all-gather.15
  214.2 79.5 all-gather.17
  412.1 10.9 reduce-scatter.26
  568.0 59.3 reduce-scatter.44
  631.6 61.9 reduce-scatter.28
  697.3 149.4 all-reduce.15
  850.8 111.3 reduce-scatter.34
  966.8 111.1 reduce-scatter.30
  1080.1 9.5 reduce-scatter.46
  1093.1 53.6 reduce-scatter.42
  1149.6 9.9 reduce-scatter.38
  1162.3 15.2 reduce-scatter.36
  1180.4 15.2 reduce-scatter.40
  1197.8 15.2 reduce-scatter.32
where the time goes:
time: 1230 us; the launch traced here: 1220 us
  waiting for transfers between devices  354 us (29%)
  local copies, waits for them, and re-layouts  301 us (24%)
  matrix products  264 us (21%)
  blocking collectives  199 us (16%)
  other arithmetic  77.4 us (6%)
  between operations  21.8 us (2%)
    unnamed x27, waiting for transfers between devices  216 us
    unnamed x272, local copies, waits for them, and re-layouts  136 us
    reduce_scatter x1, waiting for transfers between devices, reduce_grads(): lax.psum_scatter(grads[2].astype(jnp.bfloat16), 'wq', scatter_dimension=1...  77.9 us
    reshape x13, local copies, waits for them, and re-layouts, head_split(): matrix.reshape(seq_count, row_count // seq_count, HEADS, model_width // H...  71.9 us
    reduce_scatter x1, waiting for transfers between devices, reduce_grads(): lax.psum_scatter(grads[3].astype(jnp.bfloat16), 'wq', scatter_dimension=1...  59.7 us
    unnamed x5, blocking collectives  54.5 us
    slice x1, local copies, waits for them, and re-layouts, encode_forward(): encoded = layer_norm(pre_two, vec_f32[6], vec_f32[7])  47.1 us
    psum x1, blocking collectives, shards(): loss_sum = lax.psum(jnp.sum(log_total - gold_score), 'wq')  32.9 us
  transfers between devices with their start and end apart: 20, of which 7 were waited for; matrix products, arithmetic and copies ran while one was open for 46% of the time, Pallas kernels for 0%

commit v1 on v0

v1 whole, which is shorter than its diff:
```python
import math

import jax
import jax.numpy as jnp
from jax import lax
from jax.sharding import PartitionSpec as P

HEADS = 12


EPSILON = 1e-12
NEGATIVE = -1e30


def layer_norm(inputs, gain_row, offset):
    centred = inputs - jnp.mean(inputs, axis=-1, keepdims=True)
    spread = jnp.mean(centred * centred, axis=-1, keepdims=True)
    return centred * lax.rsqrt(spread + EPSILON) * gain_row + offset


def smooth_gate(values):
    return jax.nn.gelu(values, approximate=True)


def gather_weights(
    query_key_value_weight, attention_output_weight, up_weight, down_weight, vectors, hidden_bias
):
    np_parts = (
        lax.all_gather(query_key_value_weight, "np", axis=2, tiled=True),
        lax.all_gather(attention_output_weight, "np", axis=2, tiled=True),
        lax.all_gather(up_weight, "np", axis=2, tiled=True),
        lax.all_gather(down_weight, "np", axis=2, tiled=True),
        lax.all_gather(vectors, "np", axis=1, tiled=True),
        lax.all_gather(hidden_bias, "np", axis=1, tiled=True),
    )
    return (
        lax.all_gather(np_parts[0], "wq", axis=1, tiled=True),
        lax.all_gather(np_parts[1], "wq", axis=1, tiled=True),
        lax.all_gather(np_parts[2], "wq", axis=1, tiled=True),
        lax.all_gather(np_parts[3], "wq", axis=1, tiled=True),
        lax.all_gather(np_parts[4], "wq", axis=2, tiled=True),
        lax.all_gather(np_parts[5], "wq", axis=1, tiled=True),
    )


def head_split(matrix, seq_count):
    row_count, model_width = matrix.shape
    return matrix.reshape(seq_count, row_count // seq_count, HEADS, model_width // HEADS)


def attention_scores(queries, keys_low, lengths):
    seq_count = lengths.shape[0]
    split_q = head_split(queries, seq_count)
    scores = jnp.einsum(
        "sqhc,skhc->shqk",
        split_q,
        head_split(keys_low, seq_count),
        preferred_element_type=jnp.float32,
    )
    scores = scores * split_q.shape[3] ** (-0.5)
    live_mask = jnp.arange(split_q.shape[1])[None, :] < lengths[:, None]
    return jnp.where(live_mask[:, None, None, :], scores, NEGATIVE)


def first_rows(matrix, seq_count):
    row_count, width = matrix.shape
    return matrix.reshape(seq_count, row_count // seq_count, width)[:, 0, :]


def encode_forward(token_rows, lengths, weights):
    (
        query_key_value_weight,
        attention_output_weight,
        up_weight,
        down_weight,
        vectors,
        hidden_bias,
    ) = weights
    row_count, model_width = token_rows.shape
    seq_count = lengths.shape[0]
    vec_f32 = vectors.astype(jnp.float32)
    projected_rows = jnp.dot(token_rows, query_key_value_weight, preferred_element_type=jnp.float32)
    queries = (projected_rows[:, :model_width] + vec_f32[0]).astype(jnp.bfloat16)
    keys_low = projected_rows[:, model_width : 2 * model_width].astype(jnp.bfloat16)
    values = (projected_rows[:, 2 * model_width :] + vec_f32[1]).astype(jnp.bfloat16)
    scores = attention_scores(queries, keys_low, lengths)
    totals = jax.nn.logsumexp(scores, axis=-1, keepdims=True)
    soft_low = jnp.exp(scores - totals).astype(jnp.bfloat16)
    attended_tokens = jnp.einsum(
        "shqk,skhc->sqhc",
        soft_low,
        head_split(values, seq_count),
        preferred_element_type=jnp.float32,
    )
    attended_tokens = attended_tokens.reshape(row_count, model_width).astype(jnp.bfloat16)
    residual_branch = (
        jnp.dot(attended_tokens, attention_output_weight, preferred_element_type=jnp.float32)
        + vec_f32[2]
    )
    pre_one = token_rows.astype(jnp.float32) + residual_branch
    first_normed = layer_norm(pre_one, vec_f32[3], vec_f32[4])
    normed_low = first_normed.astype(jnp.bfloat16)
    hidden_rows = jnp.dot(
        normed_low, up_weight, preferred_element_type=jnp.float32
    ) + hidden_bias.astype(jnp.float32)
    activated_hidden = smooth_gate(hidden_rows).astype(jnp.bfloat16)
    feedforward_output = (
        jnp.dot(activated_hidden, down_weight, preferred_element_type=jnp.float32) + vec_f32[5]
    )
    pre_two = first_normed + feedforward_output
    encoded_low = layer_norm(pre_two, vec_f32[6], vec_f32[7]).astype(jnp.bfloat16)
    soft_first = jnp.exp(scores[:, :, 0, :] - totals[:, :, 0, :])
    stored = (
        first_rows(queries, seq_count),
        keys_low,
        values,
        soft_first,
        first_rows(attended_tokens, seq_count),
        first_rows(pre_one, seq_count),
        first_rows(normed_low, seq_count),
        first_rows(hidden_rows, seq_count),
        first_rows(activated_hidden, seq_count),
        first_rows(pre_two, seq_count),
    )
    return (encoded_low, stored)


def norm_back(pre, gain_row, grad_out):
    centred = pre - jnp.mean(pre, axis=-1, keepdims=True)
    inverse = lax.rsqrt(jnp.mean(centred * centred, axis=-1, keepdims=True) + EPSILON)
    scaled = grad_out * gain_row
    inner = jnp.mean(scaled * centred, axis=-1, keepdims=True)
    grad_in = inverse * (
        scaled - jnp.mean(scaled, axis=-1, keepdims=True) - centred * (inverse * inverse * inner)
    )
    return (grad_in, jnp.sum(grad_out * centred * inverse, axis=0), jnp.sum(grad_out, axis=0))


def encode_backward(token_rows, weights, stored, grad_first):
    (
        query_key_value_weight,
        attention_output_weight,
        up_weight,
        down_weight,
        vectors,
        hidden_bias,
    ) = weights
    (
        queries,
        keys_low,
        values,
        soft_first,
        attended,
        pre_one,
        normed_low,
        hidden_rows,
        activated_hidden,
        pre_two,
    ) = stored
    seq_count, model_width = queries.shape
    seq_length = token_rows.shape[0] // seq_count
    head_width = model_width // HEADS
    scaling = head_width ** (-0.5)
    vec_f32 = vectors.astype(jnp.float32)
    grad_two, gain_two, shift_two = norm_back(pre_two, vec_f32[6], grad_first)
    grad_ffn = grad_two.astype(jnp.bfloat16)
    grad_activated = jnp.einsum(
        "rd,fd->rf", grad_ffn, down_weight, preferred_element_type=jnp.float32
    )
    grad_hidden = jax.vjp(smooth_gate, hidden_rows)[1](grad_activated)[0].astype(jnp.bfloat16)
    grad_normed = grad_two + jnp.einsum(
        "rf,df->rd", grad_hidden, up_weight, preferred_element_type=jnp.float32
    )
    grad_one, gain_one, shift_one = norm_back(pre_one, vec_f32[3], grad_normed)
    grad_branch = grad_one.astype(jnp.bfloat16)
    grad_attended = jnp.einsum(
        "re,de->rd", grad_branch, attention_output_weight, preferred_element_type=jnp.float32
    ).astype(jnp.bfloat16)
    grad_heads = grad_attended.reshape(seq_count, HEADS, head_width)
    grad_soft = jnp.einsum(
        "shc,skhc->shk",
        grad_heads,
        head_split(values, seq_count),
        preferred_element_type=jnp.float32,
    )
    row_inner = jnp.sum(soft_first * grad_soft, axis=-1, keepdims=True)
    grad_scores = (soft_first * (grad_soft - row_inner)).astype(jnp.bfloat16)
    soft_low = soft_first.astype(jnp.bfloat16)
    grad_queries = (
        jnp.einsum(
            "shk,skhc->shc",
            grad_scores,
            head_split(keys_low, seq_count),
            preferred_element_type=jnp.float32,
        )
        * scaling
    )
    grad_q_low = grad_queries.reshape(seq_count, model_width).astype(jnp.bfloat16)
    tokens = token_rows.reshape(seq_count, seq_length, model_width)
    both = jnp.concatenate([grad_scores, soft_low], axis=1)
    mixed = jnp.einsum("sgk,skd->sgd", both, tokens, preferred_element_type=jnp.float32).astype(
        jnp.bfloat16
    )
    scaled_queries = (queries.astype(jnp.float32) * scaling).astype(jnp.bfloat16)
    split_weight = query_key_value_weight.reshape(model_width, 3, HEADS, head_width)
    back_rows = jnp.concatenate(
        [
            jnp.einsum(
                "shc,dhc->shd",
                scaled_queries.reshape(seq_count, HEADS, head_width),
                split_weight[:, 1],
                preferred_element_type=jnp.float32,
            ),
            jnp.einsum(
                "shc,dhc->shd",
                grad_heads,
                split_weight[:, 2],
                preferred_element_type=jnp.float32,
            ),
        ],
        axis=1,
    ).astype(jnp.bfloat16)
    grad_tokens = jnp.einsum("sgk,sgd->skd", both, back_rows, preferred_element_type=jnp.float32)
    first_extra = grad_one + jnp.einsum(
        "se,de->sd",
        grad_q_low,
        query_key_value_weight[:, :model_width],
        preferred_element_type=jnp.float32,
    )
    is_first = (jnp.arange(seq_length) == 0)[None, :, None]
    grad_tokens = grad_tokens + jnp.where(is_first, first_extra[:, None, :], 0.0)
    soft_total = jnp.sum(soft_low.astype(jnp.float32), axis=-1, keepdims=True)
    vector_parts = jnp.stack(
        [
            jnp.sum(grad_q_low.astype(jnp.float32), axis=0),
            jnp.sum(grad_heads.astype(jnp.float32) * soft_total, axis=0).reshape(model_width),
            jnp.sum(grad_branch.astype(jnp.float32), axis=0),
            gain_one,
            shift_one,
            jnp.sum(grad_ffn.astype(jnp.float32), axis=0),
            gain_two,
            shift_two,
        ]
    )
    bias_part = jnp.sum(grad_hidden.astype(jnp.float32), axis=0)
    left = (
        activated_hidden,
        normed_low,
        attended,
        jnp.concatenate(
            [jnp.broadcast_to(tokens[:, :1, :], (seq_count, HEADS, model_width)), mixed], axis=1
        ),
    )
    right = (
        grad_ffn,
        grad_hidden,
        grad_branch,
        jnp.concatenate([grad_q_low, scaled_queries, grad_attended], axis=1),
    )
    return (
        grad_tokens.reshape(token_rows.shape),
        left,
        right,
        vector_parts,
        bias_part,
    )


def left_message(left, wq_size, np_size):
    activated, normed, attended, mixed = left
    rows, groups, model_width = mixed.shape
    part = model_width // wq_size
    columns = 3 * model_width // np_size
    head_width = model_width // HEADS
    group = math.gcd(head_width, columns)
    mixed = jnp.repeat(mixed, head_width // group, axis=1)
    mixed = mixed.reshape(rows, np_size, columns // group, wq_size, part)
    mixed = mixed.transpose(3, 1, 0, 2, 4).reshape(wq_size, np_size, rows, columns // group * part)

    def same(matrix):
        pieces = matrix.reshape(rows, wq_size, -1).transpose(1, 0, 2)
        return jnp.broadcast_to(pieces[:, None], (wq_size, np_size) + pieces.shape[1:])

    return jnp.concatenate([same(activated), same(normed), same(attended), mixed], axis=3)


def right_message(right, np_size):
    rows = right[0].shape[0]
    return jnp.concatenate(
        [member.reshape(rows, np_size, -1).transpose(1, 0, 2) for member in right], axis=2
    )


def weight_grads(left, right, model_width, ff_width, wq_size, np_size):
    rows = left.shape[0]
    part, ff_part = model_width // wq_size, ff_width // wq_size
    columns = 3 * model_width // np_size
    group = math.gcd(model_width // HEADS, columns)
    right_sizes = (model_width // np_size, ff_width // np_size, model_width // np_size)
    cut = [ff_part, ff_part + part, ff_part + 2 * part]
    activated, normed, attended, mixed = jnp.split(left, cut, axis=1)
    cut = [right_sizes[0], right_sizes[0] + right_sizes[1], sum(right_sizes)]
    grad_ffn, grad_hidden, grad_branch, grad_projected = jnp.split(right, cut, axis=1)

    def outer(one, two):
        return jnp.einsum("sd,se->de", one, two, preferred_element_type=jnp.float32)

    w_qkv = jnp.einsum(
        "sgd,sgc->dgc",
        mixed.reshape(rows, columns // group, part),
        grad_projected.reshape(rows, columns // group, group),
        preferred_element_type=jnp.float32,
    ).reshape(part, columns)
    return (
        w_qkv,
        outer(attended, grad_branch),
        outer(normed, grad_hidden),
        outer(activated, grad_ffn),
    )


def shards(
    q_embed,
    p_embed,
    q_len,
    p_len,
    q_set,
    p_set,
    gold,
    query_key_value_weight,
    attention_output_weight,
    up_weight,
    down_weight,
    vectors,
    hidden_bias,
):
    gathered = gather_weights(
        query_key_value_weight,
        attention_output_weight,
        up_weight,
        down_weight,
        vectors,
        hidden_bias,
    )
    wq_size, np_size = lax.axis_size("wq"), lax.axis_size("np")
    both_axes = ("wq", "np")
    q_weights = tuple((member[0] for member in gathered))
    p_weights = tuple((member[1] for member in gathered))
    p_encoded, p_stored = encode_forward(p_embed, p_len, p_weights)
    q_encoded, q_stored = encode_forward(q_embed, q_len, q_weights)
    model_width = q_embed.shape[1]
    ff_width = gathered[2].shape[2]
    q_count = q_len.shape[0]
    p_count = p_len.shape[0]
    own_heads = jnp.concatenate([first_rows(q_encoded, q_count), first_rows(p_encoded, p_count)])
    heads = lax.all_gather(own_heads, both_axes, axis=0)
    marks = lax.all_gather(jnp.concatenate([q_set, gold, p_set]), both_axes, axis=0)
    q_heads = heads[:, :q_count].reshape(-1, model_width)
    p_heads = heads[:, q_count:].reshape(-1, model_width)
    q_sets = marks[:, :q_count].reshape(-1)
    golds = marks[:, q_count : 2 * q_count].reshape(-1)
    p_sets = marks[:, 2 * q_count :].reshape(-1)
    scaling = model_width ** (-0.5)
    similar = (
        jnp.einsum("qd,pd->qp", q_heads, p_heads, preferred_element_type=jnp.float32) * scaling
    )
    is_gold = jnp.arange(p_heads.shape[0], dtype=jnp.int32)[None, :] == golds[:, None]
    usable = (q_sets[:, None] == p_sets[None, :]) | is_gold
    masked = jnp.where(usable, similar, NEGATIVE)
    highest = jnp.max(masked, axis=1)
    total = jnp.sum(jnp.where(usable, jnp.exp(masked - highest[:, None]), 0.0), axis=1)
    log_total = highest + jnp.log(total)
    gold_score = jnp.sum(jnp.where(is_gold, similar, 0.0), axis=1)
    loss = jnp.mean(log_total - gold_score)
    soft_rows = jnp.where(usable, jnp.exp(masked - log_total[:, None]), 0.0)
    grad_similar = (soft_rows - is_gold.astype(jnp.float32)).astype(jnp.bfloat16)
    me = lax.axis_index("wq") * np_size + lax.axis_index("np")
    grad_q_first = (
        jnp.einsum(
            "qp,pd->qd",
            lax.dynamic_slice_in_dim(grad_similar, me * q_count, q_count, 0),
            p_heads,
            preferred_element_type=jnp.float32,
        )
        * scaling
    )
    grad_p_first = (
        jnp.einsum(
            "qp,qd->pd",
            lax.dynamic_slice_in_dim(grad_similar, me * p_count, p_count, 1),
            q_heads,
            preferred_element_type=jnp.float32,
        )
        * scaling
    )
    q_back = encode_backward(q_embed, q_weights, q_stored, grad_q_first)
    p_back = encode_backward(p_embed, p_weights, p_stored, grad_p_first)
    left = jnp.concatenate(
        [left_message(member[1], wq_size, np_size) for member in (q_back, p_back)], axis=2
    )
    left = left.reshape((wq_size * np_size,) + left.shape[2:])
    left = lax.all_to_all(left, both_axes, 0, 0)
    right = jnp.concatenate([right_message(member[2], np_size) for member in (q_back, p_back)], axis=1)
    right = lax.all_gather(lax.all_to_all(right, "np", 0, 0), "wq", axis=0)
    right = right.reshape((wq_size * np_size,) + right.shape[2:])
    sums = jnp.concatenate(
        [
            jnp.stack([q_back[3], p_back[3]])
            .reshape(2, np_size, -1, wq_size, model_width // wq_size)
            .transpose(3, 1, 0, 2, 4)
            .reshape(wq_size * np_size, -1),
            jnp.stack([q_back[4], p_back[4]])
            .reshape(2, wq_size * np_size, -1)
            .transpose(1, 0, 2)
            .reshape(wq_size * np_size, -1),
        ],
        axis=1,
    )
    sums = jnp.sum(lax.all_to_all(sums, both_axes, 0, 0), axis=0)
    grad_vectors = sums[: sums.shape[0] - 2 * ff_width // (wq_size * np_size)].reshape(
        2, -1, model_width // wq_size
    )
    grad_b_in = sums[sums.shape[0] - 2 * ff_width // (wq_size * np_size) :].reshape(2, -1)
    q_weight_grads = weight_grads(
        left[:, :q_count].reshape(-1, left.shape[2]),
        right[:, :q_count].reshape(-1, right.shape[2]),
        model_width,
        ff_width,
        wq_size,
        np_size,
    )
    p_weight_grads = weight_grads(
        left[:, q_count:].reshape(-1, left.shape[2]),
        right[:, q_count:].reshape(-1, right.shape[2]),
        model_width,
        ff_width,
        wq_size,
        np_size,
    )
    shared = tuple(jnp.stack(pair) for pair in zip(q_weight_grads, p_weight_grads))
    return (
        loss,
        q_encoded,
        p_encoded,
        q_back[0],
        p_back[0],
        shared[0],
        shared[1],
        shared[2],
        shared[3],
        grad_vectors,
        grad_b_in,
    )


def solution(mesh):
    return jax.shard_map(
        shards,
        mesh=mesh,
        in_specs=(
            P(("wq", "np"), None),
            P(("wq", "np"), None),
            P(("wq", "np")),
            P(("wq", "np")),
            P(("wq", "np")),
            P(("wq", "np")),
            P(("wq", "np")),
            P(None, "wq", "np"),
            P(None, "wq", "np"),
            P(None, "wq", "np"),
            P(None, "wq", "np"),
            P(None, "np", "wq"),
            P(None, ("wq", "np")),
        ),
        out_specs=(
            P(),
            P(("wq", "np"), None),
            P(("wq", "np"), None),
            P(("wq", "np"), None),
            P(("wq", "np"), None),
            P(None, "wq", "np"),
            P(None, "wq", "np"),
            P(None, "wq", "np"),
            P(None, "wq", "np"),
            P(None, "np", "wq"),
            P(None, ("wq", "np")),
        ),
        check_vma=False,
    )
```

time: 1230 us -> 664 us (0.54)
  waiting for transfers between devices: 354 us -> 11.6 us
  matrix products: 264 us -> 142 us
  local copies, waits for them, and re-layouts: 301 us -> 224 us
  other arithmetic: 77.4 us -> 50.4 us
    unnamed x27 -> x5, waiting for transfers between devices: 216 us -> 0.09 us
    reduce_scatter x5 -> x0, waiting for transfers between devices: 138 us -> none  [the longest x1 77.9 us: reduce_grads(): lax.psum_scatter(grads[2].astype(jnp.bfloat16), 'wq', scatter_dimension=1...]
    dot_general x21 -> x25, matrix products: 122 us -> 33 us  [the longest x6 6.95 us: outer(): return jnp.einsum('sd,se->de', one, two, preferred_element_type=jnp.float32)]
    unnamed x272 -> x270, local copies, waits for them, and re-layouts: 136 us -> 48 us
    all_gather x2 -> x1, blocking collectives: 22.7 us -> 71.3 us  [shards(): heads = lax.all_gather(own_heads, both_axes, axis=0)]
    psum x1 -> x0, blocking collectives: 32.9 us -> none  [shards(): loss_sum = lax.psum(jnp.sum(log_total - gold_score), 'wq')]
    slice x3 -> x25, local copies, waits for them, and re-layouts: 47.2 us -> 77.1 us  [the longest x1 47.5 us: encode_forward(): vec_f32[6]]
    reshape x13 -> x9, local copies, waits for them, and re-layouts: 71.9 us -> 45.4 us  [head_split(): matrix.reshape(seq_count, row_count // seq_count, HEADS, model_width // H...]
  transfers between devices with their start and end apart: 20 -> 7, of which waited for: 7 -> 1; matrix products, arithmetic and copies ran while one was open for 46% -> 47% of each run, Pallas kernels for 0% -> 0%
where the time goes in v1:
time: 664 us; the launch traced here: 657 us
  local copies, waits for them, and re-layouts  224 us (34%)
  blocking collectives  201 us (30%)
  matrix products  142 us (21%)
  other arithmetic  50.4 us (8%)
  between operations  17.8 us (3%)
  waiting for transfers between devices  11.6 us (2%)
  starting transfers between devices  9.96 us (2%)
    all_gather x1, blocking collectives, shards(): heads = lax.all_gather(own_heads, both_axes, axis=0)  71.3 us
    unnamed x270, local copies, waits for them, and re-layouts  48 us
    slice x1, local copies, waits for them, and re-layouts, encode_forward(): vec_f32[6]  47.5 us
    reshape x9, local copies, waits for them, and re-layouts, head_split(): matrix.reshape(seq_count, row_count // seq_count, HEADS, model_width // H...  45.4 us
    unnamed x1, blocking collectives  41.8 us
    dot_general x2, matrix products, encode_forward(): jnp.dot(normed_low, up_weight, preferred_element_type=jnp.float32)  26.6 us
    all_gather x1, blocking collectives, gather_weights(): lax.all_gather(np_parts[5], 'wq', axis=1, tiled=True)  20.7 us
    dot_general x2, matrix products, encode_forward(): jnp.dot(activated_hidden, down_weight, preferred_element_type=jnp.float32)  18.8 us
  transfers between devices with their start and end apart: 7, of which 1 were waited for; matrix products, arithmetic and copies ran while one was open for 47% of the time, Pallas kernels for 0%

profile of v1, /device:TPU:0, one launch (start us, length us, event | category | flops | bytes accessed | tf_op | source)
XLA Modules:
  0.0 656.8 jit_solution(7252113864050566007)
XLA Ops:
  8.5 9.2 %all_gather.56 = bf16[2,48,2304]{2,0,1:T(2,128)(2,1)} all-gather(bf16[2,48,1152]{2,0,1:T(2,128)(2,1)S(1)} %copy.254), channel_id=1, replica_groups=mesh['wq'=16,'np'=2] {'np'}, dimensions={2}, use_global_device_ids=true | all-gather | bytes 663552 | tf_op jit(solution)/shard_map/all_gather | solution.py:29
  17.7 6.6 %all_gather.60 = bf16[2,48,768]{2,1,0:T(8,128)(2,1)} all-gather(bf16[2,48,384]{2,1,0:T(8,128)(2,1)} %param.21), channel_id=1, replica_groups=mesh['wq'=16,'np'=2] {'np'}, dimensions={2}, use_global_device_ids=true | all-gather | bytes 221184 | tf_op jit(solution)/shard_map/all_gather | solution.py:30
  24.4 8.5 %all_gather.62 = bf16[2,48,3072]{2,1,0:T(8,128)(2,1)} all-gather(bf16[2,48,1536]{2,1,0:T(8,128)(2,1)} %param.22), channel_id=1, replica_groups=mesh['wq'=16,'np'=2] {'np'}, dimensions={2}, use_global_device_ids=true | all-gather | bytes 884736 | tf_op jit(solution)/shard_map/all_gather | solution.py:31
  32.9 7.5 %all_gather.66 = bf16[2,192,768]{2,1,0:T(8,128)(2,1)} all-gather(bf16[2,192,384]{2,1,0:T(8,128)(2,1)S(1)} %copy-done.35), channel_id=1, replica_groups=mesh['wq'=16,'np'=2] {'np'}, dimensions={2}, use_global_device_ids=true | all-gather | bytes 884736 | tf_op jit(solution)/shard_map/all_gather | solution.py:32
  40.7 41.8 %all-reduce = s32[704]{0:T(1024)S(1)} all-reduce(s32[704]{0:T(1024)S(1)} %add_dynamic-update-slice_fusion), channel_id=2, replica_groups=mesh['wq'=16,'np'=2] {'wq','np'}, use_global_device_ids=true, to_apply=%add | all-reduce | flops 704 | bytes 5632
  83.4 4.4 all-gather.3
  88.6 4.3 all_gather.58
  92.9 20.7 %all-gather.4 = bf16[16,192,2]{1,2,0:T(2,128)(2,1)S(1)} all-gather(bf16[1,192,2]{1,2,0:T(2,128)(2,1)S(1)} %reshape.632), channel_id=1, replica_groups=mesh['wq'=16,'np'=2] {'wq'}, dimensions={0}, use_global_device_ids=true | all-gather | bytes 13056 | tf_op jit(solution)/shard_map/all_gather | solution.py:42
  116.5 18.7 %all_gather.59 = bf16[2,8,768]{1,0,2:T(2,128)(2,1)S(1)} all-gather(bf16[2,8,48]{1,0,2:T(2,128)(2,1)S(1)} %copy.257), channel_id=1, replica_groups=mesh['wq'=16,'np'=2] {'wq'}, dimensions={2}, use_global_device_ids=true | all-gather | bytes 26112 | tf_op jit(solution)/shard_map/all_gather | solution.py:41
  135.7 47.5 %slice_reduce_fusion.1 = (f32[768]{0:T(1024)S(1)}, f32[768]{0:T(1024)}, f32[768]{0:T(1024)}, f32[768]{0:T(1024)}, f32[768]{0:T(1024)S(1)}, /*index=5*/f32[768]{0...) fusion(f32[1,8,768]{1,0,2:T(1,128)S(1)} %get-tuple-element.80, ...), kind=kLoop, calls=%fused_computation.132 | loop fusion | bytes 98304 | tf_op jit(solution)/shard_map/slice | solution.py:111
  184.4 15.3 %fusion.177 = (bf16[1,768,2304]{2,0,1:T(2,128)(2,1)}, bf16[1,768,2304]{2,0,1:T(2,128)(2,1)}) fusion(bf16[2,768,2304]{2,0,1:T(2,128)(2,1)} %all-gather.12.cloned.1.call-done), kind=kLoop, calls=%fused_computation.358 | loop fusion | bytes 14155776 | tf_op jit(solution)/shard_map/slice | solution.py:347
  199.7 16.0 %copy.345 = bf16[1,768,2304]{1,2,0:T(8,128)(2,1)S(1)} copy(bf16[1,768,2304]{2,0,1:T(2,128)(2,1)} %get-tuple-element.67) | data formatting | bytes 7077888
  215.8 16.3 %copy.347 = bf16[1,768,2304]{1,2,0:T(8,128)(2,1)} copy(bf16[1,768,2304]{2,0,1:T(2,128)(2,1)} %get-tuple-element.68) | data formatting | bytes 7077888
  232.1 3.2 fusion.170
  235.7 2.2 reshape.647
  238.5 2.2 reshape.648
  242.2 2.9 copy.263
  245.1 3.3 fusion.182
  248.5 1.8 exponential_reduce_fusion.1
  252.5 2.4 convolution_convert_fusion
  256.1 2.4 copy.264
  258.6 3.7 convert_element_type.229
  262.3 7.5 %fusion.168 = f32[1536,2304]{1,0:T(8,128)S(1)} fusion(bf16[1536,768]{1,0:T(8,128)(2,1)} %param.14, bf16[1,768,2304]{1,2,0:T(8,128)(2,1)S(1)} %copy-done.6), kind=kOutput, calls=%fused_computation.350 | convolution fusion | flops 5435817984 | bytes 20054016 | tf_op jit(solution)/shard_map/dot_general | solution.py:82
  271.4 2.3 fusion.21
  273.7 6.0 reshape.650
  279.8 8.2 %reshape.649 = bf16[6,256,12,64]{3,2,1,0:T(8,128)(2,1)} reshape(bf16[1536,768]{1,0:T(8,128)(2,1)} %get-tuple-element.66) | data formatting | bytes 4718592 | tf_op jit(solution)/shard_map/reshape | solution.py:48
  288.0 6.3 copy.274
  294.3 8.2 %reshape.651 = bf16[6,256,12,64]{3,2,1,0:T(8,128)(2,1)} reshape(bf16[1536,768]{1,0:T(8,128)(2,1)} %slice.513) | data formatting | bytes 4718592 | tf_op jit(solution)/shard_map/reshape | solution.py:48
  302.5 7.8 %copy.273 = bf16[6,256,12,64]{1,3,2,0:T(8,128)(2,1)} copy(bf16[6,256,12,64]{3,2,1,0:T(8,128)(2,1)} %reshape.651) | data formatting | bytes 4718592 | tf_op jit(solution)/shard_map/reshape | solution.py:48
  310.4 13.4 %fusion.179 = (f32[6,12,256]{2,1,0:T(8,128)S(1)}, f32[6,12,256,256]{3,2,1,0:T(8,128)}) fusion(bf16[6,256,12,64]{1,3,2,0:T(8,128)(2,1)} %copy.273, bf16[6,256,12,64]{3,2,1,0:T(8,128)(2,1)} %reshape.650, pred[6,256]{1,0:T(8,128)(4,1)S(1)} %copy-done.101), kind=kOutput, calls=%fused_computation.360 | convolution fusion | flops 618117120 | bytes 23668224 | tf_op jit(solution)/shard_map/sqhc,skhc->shqk/dot_general | solution.py:54
  324.9 9.8 %exponential_reduce_fusion = f32[6,12,256]{2,1,0:T(8,128)S(1)} fusion(f32[6,12,256,256]{3,2,1,0:T(8,128)} %get-tuple-element.90, f32[6,12,256]{2,1,0:T(8,128)S(1)} %is-finite_select_fusion), kind=kLoop, calls=%fused_computation.13 | loop fusion | flops 9418752 | bytes 19021824 | tf_op jit(solution)/shard_map/reduce_sum | solution.py:87
  336.3 8.3 %fusion.31 = bf16[6,12,64,256]{3,2,1,0:T(8,128)(2,1)S(1)} fusion(bf16[6,256,12,64]{1,3,2,0:T(8,128)(2,1)S(1)} %copy.274, f32[6,12,256,256]{3,2,1,0:T(8,128)} %get-tuple-element.90, f32[6,12,256]{2,1,0:T(8,128)S(1)} %get-tuple-element.82), kind=kOutput, calls=%fused_computation.57 | convolution fusion | flops 614596608 | bytes 23666688 | tf_op jit(solution)/shard_map/shqk,skhc->sqhc/dot_general | solution.py:89
  346.0 1.7 copy.275
  347.7 2.2 copy.368
  350.0 2.6 fusion.183
  353.5 4.1 fusion.180
  362.6 2.1 fusion.30
  364.7 9.0 %fusion.20 = (bf16[512,3072]{1,0:T(8,128)(2,1)}, f32[512,3072]{1,0:T(8,128)}) fusion(f32[3072]{0:T(1024)S(1)} %bitcast.510, bf16[512,768]{1,0:T(8,128)(2,1)S(1)} %fusion.36, bf16[2,768,3072]{2,1,0:T(8,128)(2,1)} %all-gather.16.cloned.1.call-done), kind=kOutput, calls=%fused_computation.26 | convolution fusion | flops 2431647744 | bytes 14954496 | tf_op jit(solution)/shard_map/dot_general | solution.py:103
  373.8 6.6 %fusion.184 = (f32[512]{0:T(512)S(1)}, f32[512,768]{1,0:T(8,128)S(1)}) fusion(f32[768]{0:T(1024)S(1)} %copy-done.94, bf16[512,3072]{1,0:T(8,128)(2,1)} %get-tuple-element.101, bf16[2,3072,768]{2,1,0:T(8,128)(2,1)} %all-gather.18.cloned.1.call-done, f32[768]{0:T(1024)S(1)} %copy-done.74, f32[768]{0:T(1024)S(1)} %get-tuple-element.122, ...), kind=kOutput, calls=%fused_computation.365 | convolution fusion | flops 2418671104 | bytes 11025408 | tf_op jit(solution)/shard_map/dot_general | solution.py:108
  380.4 1.8 slice.376
  384.8 17.6 %fusion.10 = (bf16[1536,3072]{1,0:T(8,128)(2,1)}, f32[1536,3072]{1,0:T(8,128)}) fusion(f32[3072]{0:T(1024)S(1)} %bitcast.509, bf16[1536,768]{1,0:T(8,128)(2,1)} %fusion.30, bf16[2,768,3072]{2,1,0:T(8,128)(2,1)S(1)} %bitcast.462), kind=kOutput, calls=%fused_computation.11 | convolution fusion | flops 7294943232 | bytes 35401728 | tf_op jit(solution)/shard_map/dot_general | solution.py:103
  402.5 12.2 %fusion.181 = (f32[1536]{0:T(1024)S(1)}, f32[1536,768]{1,0:T(8,128)S(1)}) fusion(f32[768]{0:T(1024)S(1)} %copy-done.93, bf16[1536,3072]{1,0:T(8,128)(2,1)} %get-tuple-element.93, bf16[2,3072,768]{2,1,0:T(8,128)(2,1)} %all-gather.18.cloned.1.call-done, f32[768]{0:T(1024)S(1)} %copy-done.72, f32[768]{0:T(1024)S(1)} %get-tuple-element.23, ...), kind=kOutput, calls=%fused_computation.362 | convolution fusion | flops 7256013312 | bytes 23620608 | tf_op jit(solution)/shard_map/dot_general | solution.py:108
  414.7 1.7 slice.386
  420.6 71.3 %all-gather.5 = bf16[32,14,768]{2,1,0:T(8,128)(2,1)S(1)} all-gather(bf16[1,14,768]{2,1,0:T(8,128)(2,1)S(1)} %maximum_bitcast_fusion.3), channel_id=3, replica_groups=mesh['wq'=16,'np'=2] {'wq','np'}, dimensions={0}, use_global_device_ids=true | all-gather | bytes 709632 | tf_op jit(solution)/shard_map/all_gather | solution.py:356
  496.6 1.9 multiply_reduce_fusion.5
  502.6 4.4 convert_reduce_fusion
  507.1 4.4 fusion.154
  512.2 4.3 convert_reduce_fusion.1
  516.6 2.1 multiply_reduce_fusion.6
  521.9 2.5 fusion.108
  526.4 2.3 multiply_reduce_fusion.7
  529.9 2.3 fusion.55
  533.0 8.0 %all_to_all.19 = bf16[2,14,3456]{2,1,0:T(8,128)(2,1)} all-to-all(bf16[2,14,3456]{2,1,0:T(8,128)(2,1)S(1)} %maximum_maximum_fusion), channel_id=1, replica_groups=mesh['wq'=16,'np'=2] {'np'}, dimensions={0} | all-to-all | bytes 387072 | tf_op jit(solution)/shard_map/all_to_all | solution.py:404
  545.8 1.7 copy.360
  553.8 2.2 fusion.52
  573.5 3.4 all-to-all-start.2
  582.3 2.4 reshape_reshape_broadcast_in_dim.6
  589.9 2.6 pad_maximum_fusion
  592.5 6.3 all-to-all-start.1
  598.8 2.2 fusion.50
  611.0 3.1 select_add_fusion
  616.3 11.5 %all-to-all-done.1 = bf16[32,14,1152]{2,1,0:T(8,128)(2,1)} async-done(((bf16[32,14,1152]{2,1,0:T(8,128)(2,1)}), bf16[32,14,1152]{2,1,0:T(8,128)(2,1)}, u32[]{:S(2)}, u32[]{:S(2)}) %all-to-all-start.1) | async-done | bytes 1032224 | tf_op jit(solution)/shard_map/all_to_all | solution.py:402
  638.2 1.7 slice_bitcast_fusion.14
  639.8 1.8 convolution_bitcast_fusion.7
  (507 shorter events, 116.1 us)
Async XLA Ops:
  7.2 25.7 %copy-start.35 = (bf16[2,192,384]{2,1,0:T(8,128)(2,1)S(1)}, bf16[2,192,384]{2,1,0:T(8,128)(2,1)}, u32[]{:S(2)}) copy-start(bf16[2,192,384]{2,1,0:T(8,128)(2,1)} %param.23) | copy-start | bytes 884740
  7.2 33.3 %copy-start.105 = (s32[8]{0:T(128)S(1)}, s32[8]{0:T(128)}, u32[]{:S(2)}) copy-start(s32[8]{0:T(128)} %param.19) | copy-start | bytes 100
  7.2 33.3 %copy-start.104 = (s32[6]{0:T(128)S(1)}, s32[6]{0:T(128)}, u32[]{:S(2)}) copy-start(s32[6]{0:T(128)} %param.18) | copy-start | bytes 76
  7.2 33.3 %copy-start.106 = (s32[8]{0:T(128)S(1)}, s32[8]{0:T(128)}, u32[]{:S(2)}) copy-start(s32[8]{0:T(128)} %param.17) | copy-start | bytes 100
  7.2 75.5 %copy-start.115 = (s32[8]{0:T(128)S(1)}, s32[8]{0:T(128)}, u32[]{:S(2)}) copy-start(s32[8]{0:T(128)} %param.15) | copy-start | bytes 100
  7.2 76.2 %copy-start.116 = (bf16[2,96]{1,0:T(2,128)(2,1)S(1)}, bf16[2,96]{1,0:T(2,128)(2,1)}, u32[]{:S(2)}) copy-start(bf16[2,96]{1,0:T(2,128)(2,1)} %param.25) | copy-start | bytes 1156
  7.2 80.7 %copy-start.107 = (s32[6]{0:T(128)S(1)}, s32[6]{0:T(128)}, u32[]{:S(2)}) copy-start(s32[6]{0:T(128)} %param.16) | copy-start | bytes 76
  7.3 81.3 %copy-start.102 = (bf16[2,4,48]{2,1,0:T(4,128)(2,1)S(1)}, bf16[2,4,48]{2,1,0:T(4,128)(2,1)}, u32[]{:S(2)}) copy-start(bf16[2,4,48]{2,1,0:T(4,128)(2,1)} %param.24) | copy-start | bytes 2308
  7.3 177.1 %all-gather.12.cloned.1.call-start = ((), (), s32[]{:S(2)}) async-start(), calls=%async_computation.3 | async-start | bytes 7520256 | tf_op jit(solution)/shard_map/all_gather | solution.py:37
  17.7 332.3 %all-gather.14.cloned.1.call-start = ((), (), s32[]{:S(2)}) async-start(), calls=%async_computation.4 | async-start | bytes 2506752 | tf_op jit(solution)/shard_map/all_gather | solution.py:38
  24.3 340.4 %all-gather.16.cloned.1.call-start = ((), (), s32[]{:S(2)}) async-start(), calls=%async_computation.5 | async-start | bytes 10027008 | tf_op jit(solution)/shard_map/all_gather | solution.py:39
  32.9 340.9 %all-gather.18.cloned.1.call-start = ((), (), s32[]{:S(2)}) async-start(), calls=%async_computation.6 | async-start | bytes 10027008 | tf_op jit(solution)/shard_map/all_gather | solution.py:40
  40.5 592.8 %all-gather.20.cloned.1.call-start = ((), (), s32[]{:S(2)}) async-start(), calls=%async_computation.7 | async-start | bytes 3760128 | tf_op jit(solution)/shard_map/all_gather | solution.py:404
  183.2 16.5 %copy-start.68 = (f32[768]{0:T(1024)}, f32[768]{0:T(1024)S(1)}, u32[]{:S(2)}) copy-start(f32[768]{0:T(1024)S(1)} %get-tuple-element.19) | copy-start | bytes 9220
  215.8 16.4 %copy-start.4 = (bf16[1,768,2304]{1,2,0:T(8,128)(2,1)}, bf16[1,768,2304]{1,2,0:T(8,128)(2,1)S(1)}, u32[]{:S(2)}) copy-start(bf16[1,768,2304]{1,2,0:T(8,128)(2,1)S(1)} %copy.345) | copy-start | bytes 10616836
  255.0 7.3 %copy-start.6 = (bf16[1,768,2304]{1,2,0:T(8,128)(2,1)S(1)}, bf16[1,768,2304]{1,2,0:T(8,128)(2,1)}, u32[]{:S(2)}) copy-start(bf16[1,768,2304]{1,2,0:T(8,128)(2,1)} %copy.347) | copy-start | bytes 10616836
  279.8 81.8 %copy-start.48 = (bf16[6,1,768]{2,1,0:T(2,128)(2,1)}, bf16[6,1,768]{2,1,0:T(2,128)(2,1)S(1)}, u32[]{:S(2)}) copy-start(bf16[6,1,768]{2,1,0:T(2,128)(2,1)S(1)} %slice.387) | copy-start | bytes 27652
  302.5 7.8 %copy-start.101 = (pred[6,256]{1,0:T(8,128)(4,1)S(1)}, pred[6,256]{1,0:T(8,128)(4,1)}, u32[]{:S(2)}) copy-start(pred[6,256]{1,0:T(8,128)(4,1)} %iota_compare_fusion.1) | copy-start | bytes 4612
  324.8 10.0 %copy-start.36 = (f32[6,12,1,256]{3,2,1,0:T(1,128)}, f32[6,12,1,256]{3,2,1,0:T(1,128)S(1)}, u32[]{:S(2)}) copy-start(f32[6,12,1,256]{3,2,1,0:T(1,128)S(1)} %slice.381) | copy-start | bytes 221188
  334.8 9.8 %copy-start.80 = (f32[6,12]{1,0:T(8,128)}, f32[6,12]{1,0:T(8,128)S(1)}, u32[]{:S(2)}) copy-start(f32[6,12]{1,0:T(8,128)S(1)} %fusion.124) | copy-start | bytes 868
  352.6 9.7 %copy-start.7 = (f32[512,768]{1,0:T(8,128)}, f32[512,768]{1,0:T(8,128)S(1)}, u32[]{:S(2)}) copy-start(f32[512,768]{1,0:T(8,128)S(1)} %get-tuple-element.100) | copy-start | bytes 4718596
  352.9 6.3 copy-start.108
  364.7 9.0 %copy-start.94 = (f32[768]{0:T(1024)S(1)}, f32[768]{0:T(1024)}, u32[]{:S(2)}) copy-start(f32[768]{0:T(1024)} %get-tuple-element.124) | copy-start | bytes 9220
  373.7 11.0 %slice-start.2 = ((s8[9437184]{0:T(1024)(128)(4,1)}), s8[4194304]{0:T(1024)(128)(4,1)S(1)}, s32[]{:S(2)}) async-start(s8[9437184]{0:T(1024)(128)(4,1)} %bitcast.461), calls=%async_computation.10 | async-start | bytes 8388608
  373.8 9.7 %copy-start.73 = (f32[768]{0:T(1024)S(1)}, f32[768]{0:T(1024)}, u32[]{:S(2)}) copy-start(f32[768]{0:T(1024)} %get-tuple-element.125) | copy-start | bytes 9220
  373.8 11.0 %slice-start.3 = ((s8[9437184]{0:T(1024)(128)(4,1)}), s8[4194304]{0:T(1024)(128)(4,1)S(1)}, s32[]{:S(2)}) async-start(s8[9437184]{0:T(1024)(128)(4,1)} %bitcast.461), calls=%async_computation.11 | async-start | bytes 8388608
  373.8 11.0 %slice-start.4 = ((s8[9437184]{0:T(1024)(128)(4,1)}), s8[1048576]{0:T(1024)(128)(4,1)S(1)}, s32[]{:S(2)}) async-start(s8[9437184]{0:T(1024)(128)(4,1)} %bitcast.461), calls=%async_computation.12 | async-start | bytes 2097152
  382.7 19.7 %copy-start.31 = (f32[8,1,768]{2,1,0:T(1,128)}, f32[8,1,768]{2,1,0:T(1,128)S(1)}, u32[]{:S(2)}) copy-start(f32[8,1,768]{2,1,0:T(1,128)S(1)} %get-tuple-element.78) | copy-start | bytes 73732
  383.5 19.0 %slice-start = ((s8[4718592]{0:T(1024)(128)(4,1)}), s8[4194304]{0:T(1024)(128)(4,1)S(1)}, s32[]{:S(2)}) async-start(s8[4718592]{0:T(1024)(128)(4,1)} %bitcast.446), calls=%async_computation.8 | async-start | bytes 8388608
  384.8 17.7 %slice-start.1 = ((s8[4718592]{0:T(1024)(128)(4,1)}), s8[524288]{0:T(1024)(128)(4,1)S(1)}, s32[]{:S(2)}) async-start(s8[4718592]{0:T(1024)(128)(4,1)} %bitcast.446), calls=%async_computation.9 | async-start | bytes 1048576
  384.8 17.7 %copy-start.93 = (f32[768]{0:T(1024)S(1)}, f32[768]{0:T(1024)}, u32[]{:S(2)}) copy-start(f32[768]{0:T(1024)} %get-tuple-element.21) | copy-start | bytes 9220
  419.2 77.4 %copy-start.70 = (f32[768]{0:T(1024)S(1)}, f32[768]{0:T(1024)}, u32[]{:S(2)}) copy-start(f32[768]{0:T(1024)} %broadcast_multiply_fusion.3) | copy-start | bytes 9220
  419.2 79.9 %copy-start.82 = (f32[768]{0:T(1024)S(1)}, f32[768]{0:T(1024)}, u32[]{:S(2)}) copy-start(f32[768]{0:T(1024)} %broadcast_multiply_fusion.2) | copy-start | bytes 9220
  492.8 23.7 %slice-start.5 = ((s8[9437184]{0:T(1024)(128)(4,1)}), s8[4194304]{0:T(1024)(128)(4,1)S(1)}, s32[]{:S(2)}) async-start(s8[9437184]{0:T(1024)(128)(4,1)} %bitcast.463), calls=%async_computation.13 | async-start | bytes 8388608
  495.7 11.3 %copy-start.34 = (f32[6,1,768]{2,1,0:T(1,128)S(1)}, f32[6,1,768]{2,1,0:T(1,128)}, u32[]{:S(2)}) copy-start(f32[6,1,768]{2,1,0:T(1,128)} %copy-done.33) | copy-start | bytes 55300
  495.7 11.4 %copy-start.90 = (f32[6]{0:T(128)S(1)}, f32[6]{0:T(128)}, u32[]{:S(2)}) copy-start(f32[6]{0:T(128)} %copy-done.89) | copy-start | bytes 76
  495.7 11.4 %copy-start.98 = (f32[6]{0:T(128)S(1)}, f32[6]{0:T(128)}, u32[]{:S(2)}) copy-start(f32[6]{0:T(128)} %add_rsqrt_fusion.5) | copy-start | bytes 76
  502.6 13.9 %slice-start.6 = ((s8[9437184]{0:T(1024)(128)(4,1)}), s8[4194304]{0:T(1024)(128)(4,1)S(1)}, s32[]{:S(2)}) async-start(s8[9437184]{0:T(1024)(128)(4,1)} %bitcast.463), calls=%async_computation.14 | async-start | bytes 8388608
  507.1 9.4 %slice-start.7 = ((s8[9437184]{0:T(1024)(128)(4,1)}), s8[1048576]{0:T(1024)(128)(4,1)S(1)}, s32[]{:S(2)}) async-start(s8[9437184]{0:T(1024)(128)(4,1)} %bitcast.463), calls=%async_computation.15 | async-start | bytes 2097152
  519.9 6.4 copy-start.61
  521.5 7.3 %copy-start.8 = (bf16[8,64,12,64]{1,3,2,0:T(8,128)(2,1)S(1)}, bf16[8,64,12,64]{1,3,2,0:T(8,128)(2,1)}, u32[]{:S(2)}) copy-start(bf16[8,64,12,64]{1,3,2,0:T(8,128)(2,1)} %copy.263) | copy-start | bytes 2359300
  521.5 7.8 %copy-start.44 = (f32[8,12,1,64]{3,2,1,0:T(1,128)S(1)}, f32[8,12,1,64]{3,2,1,0:T(1,128)}, u32[]{:S(2)}) copy-start(f32[8,12,1,64]{3,2,1,0:T(1,128)} %copy-done.43) | copy-start | bytes 73732
  521.5 7.8 %copy-start.84 = (f32[8,12]{1,0:T(8,128)S(1)}, f32[8,12]{1,0:T(8,128)}, u32[]{:S(2)}) copy-start(f32[8,12]{1,0:T(8,128)} %copy-done.83) | copy-start | bytes 1156
  521.9 6.9 %copy-start.45 = (bf16[6,12,256]{2,1,0:T(8,128)(2,1)}, bf16[6,12,256]{2,1,0:T(8,128)(2,1)S(1)}, u32[]{:S(2)}) copy-start(bf16[6,12,256]{2,1,0:T(8,128)(2,1)S(1)} %fusion.58) | copy-start | bytes 110596
  524.4 8.5 %copy-start.66 = (bf16[6,768]{1,0:T(8,128)(2,1)S(1)}, bf16[6,768]{1,0:T(8,128)(2,1)}, u32[]{:S(2)}) copy-start(bf16[6,768]{1,0:T(8,128)(2,1)} %fusion.220) | copy-start | bytes 27652
  524.4 8.5 %copy-start.65 = (bf16[8,768]{1,0:T(8,128)(2,1)S(1)}, bf16[8,768]{1,0:T(8,128)(2,1)}, u32[]{:S(2)}) copy-start(bf16[8,768]{1,0:T(8,128)(2,1)} %fusion.219) | copy-start | bytes 36868
  525.1 16.0 %copy-start.56 = (bf16[6,768]{1,0:T(8,128)(2,1)}, bf16[6,768]{1,0:T(8,128)(2,1)S(1)}, u32[]{:S(2)}) copy-start(bf16[6,768]{1,0:T(8,128)(2,1)S(1)} %convert_element_type.267) | copy-start | bytes 27652
  526.4 18.8 %copy-start.41 = (bf16[8,1,768]{2,1,0:T(2,128)(2,1)S(1)}, bf16[8,1,768]{2,1,0:T(2,128)(2,1)}, u32[]{:S(2)}) copy-start(bf16[8,1,768]{2,1,0:T(2,128)(2,1)} %slice.377) | copy-start | bytes 36868
  528.7 18.9 %copy-start.42 = (bf16[8,768]{1,0:T(8,128)(2,1)}, bf16[8,768]{1,0:T(8,128)(2,1)S(1)}, u32[]{:S(2)}) copy-start(bf16[8,768]{1,0:T(8,128)(2,1)S(1)} %get-tuple-element.118) | copy-start | bytes 36868
  529.3 20.6 %copy-start.49 = (bf16[6,1,768]{2,1,0:T(2,128)(2,1)S(1)}, bf16[6,1,768]{2,1,0:T(2,128)(2,1)}, u32[]{:S(2)}) copy-start(bf16[6,1,768]{2,1,0:T(2,128)(2,1)} %copy-done.48) | copy-start | bytes 27652
  529.3 21.3 %copy-start.2 = (bf16[6,12,64,256]{3,2,1,0:T(8,128)(2,1)S(1)}, bf16[6,12,64,256]{3,2,1,0:T(8,128)(2,1)}, u32[]{:S(2)}) copy-start(bf16[6,12,64,256]{3,2,1,0:T(8,128)(2,1)} %copy-done.1) | copy-start | bytes 7077892
  532.9 17.7 %copy-start.58 = (bf16[8,768]{1,0:T(8,128)(2,1)}, bf16[8,768]{1,0:T(8,128)(2,1)S(1)}, u32[]{:S(2)}) copy-start(bf16[8,768]{1,0:T(8,128)(2,1)S(1)} %convert_element_type.256) | copy-start | bytes 36868
  549.3 12.8 %copy-start.79 = (f32[768]{0:T(1024)S(1)}, f32[768]{0:T(1024)}, u32[]{:S(2)}) copy-start(f32[768]{0:T(1024)} %get-tuple-element.41) | copy-start | bytes 9220
  551.4 25.6 %copy-start.20 = (bf16[512,768]{1,0:T(8,128)(2,1)S(1)}, bf16[512,768]{1,0:T(8,128)(2,1)}, u32[]{:S(2)}) copy-start(bf16[512,768]{1,0:T(8,128)(2,1)} %param.13) | copy-start | bytes 2359300
  551.4 25.6 %copy-start.25 = (bf16[8,12,64]{2,1,0:T(8,128)(2,1)S(1)}, bf16[8,12,64]{2,1,0:T(8,128)(2,1)}, u32[]{:S(2)}) copy-start(bf16[8,12,64]{2,1,0:T(8,128)(2,1)} %copy-done.24) | copy-start | bytes 36868
  556.0 23.7 %copy-start.11 = (bf16[1536,768]{1,0:T(8,128)(2,1)S(1)}, bf16[1536,768]{1,0:T(8,128)(2,1)}, u32[]{:S(2)}) copy-start(bf16[1536,768]{1,0:T(8,128)(2,1)} %param.14) | copy-start | bytes 7077892
  556.0 23.7 %copy-start.27 = (bf16[6,12,256]{2,1,0:T(8,128)(2,1)S(1)}, bf16[6,12,256]{2,1,0:T(8,128)(2,1)}, u32[]{:S(2)}) copy-start(bf16[6,12,256]{2,1,0:T(8,128)(2,1)} %get-tuple-element.60) | copy-start | bytes 110596
  572.0 7.7 %copy-start.46 = (bf16[6,12,256]{2,1,0:T(8,128)(2,1)S(1)}, bf16[6,12,256]{2,1,0:T(8,128)(2,1)}, u32[]{:S(2)}) copy-start(bf16[6,12,256]{2,1,0:T(8,128)(2,1)} %copy-done.45) | copy-start | bytes 110596
  572.8 7.3 %copy-start.67 = (bf16[6,1,768]{2,0,1:T(8,128)(2,1)S(1)}, bf16[6,1,768]{2,0,1:T(8,128)(2,1)}, u32[]{:S(2)}) copy-start(bf16[6,1,768]{2,0,1:T(8,128)(2,1)} %copy.540) | copy-start | bytes 27652
  573.5 19.0 %all-to-all-start.2 = ((f32[32,1,576]{2,1,0:T(1,128)}), f32[32,1,576]{2,1,0:T(1,128)}, u32[]{:S(2)}, u32[]{:S(2)}) async-start(f32[32,1,576]{2,1,0:T(1,128)} %copy.320), calls=%async_computation.2 | async-start | bytes 163840 | tf_op jit(solution)/shard_map/all_to_all | solution.py:419
  589.9 13.9 %copy-start.5 = (bf16[1,768,2304]{1,2,0:T(8,128)(2,1)S(1)}, bf16[1,768,2304]{1,2,0:T(8,128)(2,1)}, u32[]{:S(2)}) copy-start(bf16[1,768,2304]{1,2,0:T(8,128)(2,1)} %copy-done.4) | copy-start | bytes 10616836
  592.5 35.3 %all-to-all-start.1 = ((bf16[32,14,1152]{2,1,0:T(8,128)(2,1)}), bf16[32,14,1152]{2,1,0:T(8,128)(2,1)}, u32[]{:S(2)}, u32[]{:S(2)}) async-start(bf16[32,14,1152]{2,1,0:T(8,128)(2,1)} %bitcast.467), calls=%async_computation.1 | async-start | bytes 2359296 | tf_op jit(solution)/shard_map/all_to_all | solution.py:402
  601.7 5.8 copy-start.57
  638.2 6.1 copy-start.16
  (70 other events, 214.8 us)
Sparse Core Ops, SparseCore 0:
  17.8 68.3 all-gather.11
  88.4 41.9 all-gather.13
  132.7 81.0 all-gather.15
  215.9 79.5 all-gather.17
  541.2 45.3 all-gather.19

commit v2 on v1

--- a/solution.py
+++ b/solution.py
@@ -1,8 +1,11 @@
+import functools
 import math
 
 import jax
 import jax.numpy as jnp
 from jax import lax
+from jax.experimental import pallas as pl
+from jax.experimental.pallas import tpu as pltpu
 from jax.sharding import PartitionSpec as P
 
 HEADS = 12
@@ -319,6 +322,359 @@
     )
 
 
+MESH = pl.DeviceIdType.MESH
+
+def ag_schedule(n_units, starts):
+    out = []
+    for t in range(max(starts) + 7):
+        for u in sorted(range(n_units), key=lambda u: (starts[u], u)):
+            s = t - starts[u]
+            if 0 <= s <= 6: out.append((u, s))
+    return out
+
+class Gather:
+    def __init__(self, units, ins, outs, send, recv):
+        self.units, self.ins, self.outs, self.send, self.recv = units, ins, outs, send, recv
+        w, self.y = lax.axis_index("wq"), lax.axis_index("np")
+        self.w = w
+        self.z, self.x, self.c = w // 4, (w // 2) % 2, w % 2
+        self.pending = {}
+    def dev(self, dz=0, fx=False, fy=False, fc=False):
+        x = 1 - self.x if fx else self.x
+        c = 1 - self.c if fc else self.c
+        y = 1 - self.y if fy else self.y
+        return ((self.z + dz) * 4 + x * 2 + c, y)
+    def barrier(self):
+        bar = pltpu.get_barrier_semaphore()
+        def sig(**k): pl.semaphore_signal(bar, inc=1, device_id=self.dev(**k), device_id_type=MESH)
+        sig(fx=True); sig(fy=True); sig(fc=True)
+        @pl.when(self.z > 0)
+        def _(): sig(dz=-1)
+        @pl.when(self.z < 3)
+        def _(): sig(dz=1)
+        pl.semaphore_wait(bar, 3 + (self.z + 3) // 4 + (6 - self.z) // 4)
+    def view(self, u, z=None, x=None, y=None, c=None):
+        a, e, kind, r0, rn = self.units[u]
+        o = self.outs[a]
+        r, w = self.ins[a].shape[1:]
+        zs = slice(None) if z is None else z
+        xs = slice(None) if x is None else x
+        cs = slice(None) if y is None else pl.ds(pl.multiple_of(y * w, 128), w)
+        return o.at[e, zs, xs, pl.ds(pl.multiple_of((self.c if c is None else c) * r + r0, 16), rn), cs]
+    def copy(self, u, sem, src, dst, dev):
+        return pltpu.make_async_remote_copy(src_ref=src, dst_ref=dst, send_sem=self.send.at[u, sem], recv_sem=self.recv.at[u, sem], device_id=dev, device_id_type=MESH)
+    def own_src(self, u):
+        a, e, kind, r0, rn = self.units[u]
+        return self.ins[a].at[e, pl.ds(r0, rn)]
+    def zview(self, u, core, z):
+        kind = self.units[u][2]
+        if kind == "F": return self.view(u, z=z, x=self.x, y=self.y)
+        if core == 0: return self.view(u, z=z, x=None, y=self.y)
+        return self.view(u, z=z, x=self.x, y=None)
+    def step(self, u, s):
+        for core in (0, 1):
+            pl.when(self.c == core)(lambda core=core: self._step(u, s, core))
+    def A(self, core): return dict(fx=True) if core == 0 else dict(fy=True)
+    def B(self, core): return dict(fy=True) if core == 0 else dict(fx=True)
+    def a_src(self, u, core):
+        kind = self.units[u][2]
+        z = None if kind == "F" else self.z
+        return self.view(u, z=z, x=self.x, y=self.y)
+    def a_got(self, u, core):
+        kind = self.units[u][2]
+        z = None if kind == "F" else self.z
+        return self.view(u, z=z, x=1 - self.x, y=self.y) if core == 0 else self.view(u, z=z, x=self.x, y=1 - self.y)
+    def b_src(self, u, core):
+        return self.view(u, x=None, y=self.y) if core == 0 else self.view(u, x=self.x, y=None)
+    def b_got(self, u, core):
+        return self.view(u, x=None, y=1 - self.y) if core == 0 else self.view(u, x=1 - self.x, y=None)
+    def local(self, u, sem, ref):
+        self.copy(u, sem, ref, ref, self.dev(fc=True)).start()
+    def z_send(self, u, core, hop):
+        z = self.z
+        @pl.when((z - hop >= 0) & (z + 1 <= 3))
+        def _():
+            v = self.zview(u, core, z - hop)
+            src = self.own_src(u) if (hop == 0 and self.units[u][2] == "F") else v
+            self.copy(u, 2 + hop, src, v, self.dev(dz=1)).start()
+        @pl.when((z + hop <= 3) & (z - 1 >= 0))
+        def _():
+            v = self.zview(u, core, z + hop)
+            src = self.own_src(u) if (hop == 0 and self.units[u][2] == "F") else v
+            self.copy(u, 5 + hop, src, v, self.dev(dz=-1)).start()
+    def z_wait(self, u, core, hop):
+        z = self.z
+        @pl.when(z - 1 - hop >= 0)
+        def _():
+            v = self.zview(u, core, z - 1 - hop)
+            self.copy(u, 2 + hop, v, v, self.dev(fc=True)).wait_recv()
+            self.local(u, 11 + hop, v)
+        @pl.when(z + 1 + hop <= 3)
+        def _():
+            v = self.zview(u, core, z + 1 + hop)
+            self.copy(u, 5 + hop, v, v, self.dev(fc=True)).wait_recv()
+            self.local(u, 14 + hop, v)
+    def _step(self, u, s, core):
+        F = self.units[u][2] == "F"
+        own = self.view(u, z=self.z, x=self.x, y=self.y)
+        if s == 0:
+            src = self.own_src(u)
+            self.copy(u, 8, src, own, self.dev(fc=True)).start()
+            pltpu.make_async_copy(src, own, self.send.at[u, 17]).start()
+            if F:
+                self.z_send(u, core, 0)
+            else:
+                self.copy(u, 0, src, own, self.dev(**self.A(core))).start()
+        if s == 1:
+            pltpu.make_async_copy(self.own_src(u), own, self.send.at[u, 17]).wait()
+            if F:
+                self.z_wait(u, core, 0); self.z_send(u, core, 1)
+            else:
+                g = self.a_got(u, core)
+                self.copy(u, 0, g, g, self.dev(fc=True)).wait_recv()
+                self.z_send(u, core, 0)
+                self.local(u, 9, g)
+        if s == 2:
+            if F: self.z_wait(u, core, 1); self.z_send(u, core, 2)
+            else: self.z_wait(u, core, 0); self.z_send(u, core, 1)
+        if s == 3:
+            if F:
+                self.z_wait(u, core, 2)
+                v = self.a_src(u, core)
+                self.copy(u, 0, v, v, self.dev(**self.A(core))).start()
+            else:
+                self.z_wait(u, core, 1); self.z_send(u, core, 2)
+        if s == 4:
+            if F:
+                g = self.a_got(u, core)
+                self.copy(u, 0, g, g, self.dev(fc=True)).wait_recv()
+            else:
+                self.z_wait(u, core, 2)
+            v = self.b_src(u, core)
+            self.copy(u, 1, v, v, self.dev(**self.B(core))).start()
+            if F: self.local(u, 9, g)
+        if s == 5:
+            g = self.b_got(u, core)
+            self.copy(u, 1, g, g, self.dev(fc=True)).wait_recv()
+            self.local(u, 10, g)
+        if s == 6:
+            self.finish_recv(u, core); self.finish_send(u, core)
+    def finish_recv(self, u, core):
+        other = 1 - core
+        c = 1 - self.c
+        kind = self.units[u][2]
+        def got(sem, v): self.copy(u, sem, v, v, self.dev(fc=True)).wait_recv()
+        sv = lambda **k: self.view(u, c=c, **k)
+        got(8, sv(z=self.z, x=self.x, y=self.y))
+        za = None if kind == "F" else self.z
+        got(9, sv(z=za, x=1 - self.x, y=self.y) if other == 0 else sv(z=za, x=self.x, y=1 - self.y))
+        got(10, sv(x=None, y=1 - self.y) if other == 0 else sv(x=1 - self.x, y=None))
+        def zv(z):
+            if kind == "F": return sv(z=z, x=self.x, y=self.y)
+            return sv(z=z, x=None, y=self.y) if other == 0 else sv(z=z, x=self.x, y=None)
+        for hop in range(3):
+            pl.when(self.z - 1 - hop >= 0)(lambda hop=hop: got(11 + hop, zv(self.z - 1 - hop)))
+            pl.when(self.z + 1 + hop <= 3)(lambda hop=hop: got(14 + hop, zv(self.z + 1 + hop)))
+    def finish_send(self, u, core):
+        def sent(sem, v): self.copy(u, sem, v, v, self.dev(fc=True)).wait_send()
+        own = self.view(u, z=self.z, x=self.x, y=self.y)
+        sent(8, own)
+        sent(0, self.a_src(u, core)); sent(1, self.b_src(u, core))
+        sent(9, self.a_got(u, core)); sent(10, self.b_got(u, core))
+        z = self.z
+        for hop in range(3):
+            pl.when((z - hop >= 0) & (z + 1 <= 3))(lambda hop=hop: sent(2 + hop, self.zview(u, core, z - hop)))
+            pl.when((z + hop <= 3) & (z - 1 >= 0))(lambda hop=hop: sent(5 + hop, self.zview(u, core, z + hop)))
+            pl.when(z - 1 - hop >= 0)(lambda hop=hop: sent(11 + hop, self.zview(u, core, z - 1 - hop)))
+            pl.when(z + 1 + hop <= 3)(lambda hop=hop: sent(14 + hop, self.zview(u, core, z + 1 + hop)))
+
+def gather_kernel(units, schedule, n, *refs):
+    ins, outs, (send, recv) = refs[:n], refs[n:2*n], refs[2*n:]
+    g = Gather(units, ins, outs, send, recv)
+    g.barrier()
+    for u, s in schedule: g.step(u, s)
+
+def gather_call(arrays, units, schedule, name="gather"):
+    n = len(arrays)
+    shapes = [jax.ShapeDtypeStruct((a.shape[0], 4, 2, 2 * a.shape[1], 2 * a.shape[2]), a.dtype) for a in arrays]
+    return pl.pallas_call(functools.partial(gather_kernel, units, schedule, n), out_shape=shapes,
+        in_specs=[pl.BlockSpec(memory_space=pl.ANY)] * n, out_specs=[pl.BlockSpec(memory_space=pl.ANY)] * n,
+        scratch_shapes=[pltpu.SemaphoreType.DMA((len(units), 18)), pltpu.SemaphoreType.DMA((len(units), 18))],
+        compiler_params=pltpu.CompilerParams(collective_id=1, has_side_effects=True), name=name)(*arrays)
+
+
+BLK=256
+F32=jnp.float32; BF=jnp.bfloat16
+NEG=-1e30; EPS=1e-12
+def dot(a,b): return jnp.dot(a,b,preferred_element_type=F32)
+def norm(u,g,b):
+    c=u-jnp.mean(u,axis=-1,keepdims=True)
+    s=jnp.mean(c*c,axis=-1,keepdims=True)
+    return c*lax.rsqrt(s+EPS)*g+b
+def pick(v):
+    r=[v[i*64:i*64+1] for i in range(4)]
+    return jnp.concatenate(r+[jnp.zeros_like(v[0:4])],axis=0)
+def make_bias(bias_ref, slot, lens, slots):
+    n=BLK//slots
+    key=lax.broadcasted_iota(jnp.int32,(BLK,BLK),0)
+    qry=lax.broadcasted_iota(jnp.int32,(BLK,BLK),1)
+    ok=key<lens[0]
+    if n>1:
+        ok=ok&(qry<slots)
+        for j in range(1,n):
+            ok=ok|((key>=j*slots)&(key<j*slots+lens[j])&(qry>=j*slots)&(qry<(j+1)*slots))
+    bias_ref[...]=jnp.where(ok,0.0,NEG)
+def attend_block(row, x_ref, wqkv, vec, bias_ref, k_ref, v_ref, att_ref, q0_ref, b):
+    x=x_ref[pl.ds(row,BLK),:]
+    for g in range(3):
+        cs=pl.ds(g*256,256)
+        q4=dot(x,wqkv[:,g*256:g*256+256])+vec[0:1,g*256:g*256+256]
+        q4=q4.astype(BF)
+        k4=dot(x,wqkv[:,768+g*256:768+g*256+256]).astype(BF)
+        v4=(dot(x,wqkv[:,1536+g*256:1536+g*256+256])+vec[1:2,g*256:g*256+256]).astype(BF)
+        k_ref[pl.ds(row,BLK),cs]=k4
+        v_ref[pl.ds(row,BLK),cs]=v4
+        q0_ref[pl.ds(pl.multiple_of(b*8,8),8),cs]=pick(q4.astype(F32))
+        qT=(q4.astype(F32)*0.125).T.astype(BF)
+        vT=v4.astype(F32).T.astype(BF)
+        lane=lax.broadcasted_iota(jnp.int32,(BLK,256),1)
+        outs=[]
+        for h in range(4):
+            kh=jnp.where((lane>=64*h)&(lane<64*h+64),k4,jnp.zeros_like(k4))
+            s=dot(kh,qT)+bias_ref[...]
+            m=jnp.max(s,axis=0,keepdims=True)
+            p=jnp.exp(s-m)
+            l=jnp.sum(p,axis=0,keepdims=True)
+            o=dot(vT[64*h:64*h+64,:],p.astype(BF))
+            outs.append(o*(1.0/l))
+        oT=jnp.concatenate(outs,axis=0)
+        att_ref[pl.ds(row,BLK),cs]=oT.T.astype(BF)
+def out_block(row, x_ref, att_ref, wo, vec, n_ref, a0_ref, p1_ref, b):
+    att=att_ref[pl.ds(row,BLK),:]
+    r8=pl.ds(pl.multiple_of(b*8,8),8)
+    a0_ref[r8,:]=pick(att.astype(F32))
+    pre=x_ref[pl.ds(row,BLK),:].astype(F32)+dot(att,wo[...])+vec[2:3,:]
+    p1_ref[r8,:]=pick(pre)
+    n_ref[pl.ds(row,BLK),:]=norm(pre,vec[3:4,:],vec[4:5,:])
+def gelu(u):
+    return 0.5*u*(1.0+jnp.tanh(0.7978845608028654*(u+0.044715*(u*u*u))))
+def up_block(row, n_ref, wup, hb, act_ref, h0_ref, b, arow):
+    nl=n_ref[pl.ds(row,BLK),:].astype(BF)
+    r8=pl.ds(pl.multiple_of(b*8,8),8)
+    for t in range(12):
+        cs=slice(t*256,t*256+256)
+        h=dot(nl,wup[:,cs])+hb[0:1,cs]
+        h0_ref[r8,cs]=pick(h)
+        act_ref[pl.ds(arow,BLK),cs]=gelu(h).astype(BF)
+def down_block(row, n_ref, act_ref, wdown, vec, o_ref, p2_ref, b, arow):
+    f=dot(act_ref[pl.ds(arow,BLK),:],wdown[...])+vec[5:6,:]
+    pre=n_ref[pl.ds(row,BLK),:]+f
+    p2_ref[pl.ds(pl.multiple_of(b*8,8),8),:]=pick(pre)
+    o_ref[pl.ds(row,BLK),:]=norm(pre,vec[6:7,:],vec[7:8,:]).astype(BF)
+
+def fw_kernel(phases, ql, pl_, qx, px, wqkv, wo, wup, wdn, vec, hb, qo, po, qk, qv, pk, pv, q0, a0, p1, h0, p2, bias, att, nrm, act):
+    for e,(x,o,k,v,lens,nb,slots,base) in ((1,(px,po,pk,pv,pl_,6,256,2)),(0,(qx,qo,qk,qv,ql,2,64,0))):
+        n=256//slots
+        def body(i,_):
+            row=pl.multiple_of(i*BLK,BLK); b=base+i; arow=0
+            mrow=pl.multiple_of((base+i)*BLK,BLK)
+            A=att.at[pl.ds(base*BLK,nb*BLK)]; N=nrm.at[pl.ds(base*BLK,nb*BLK)]
+            if "1" in phases:
+                make_bias(bias,0,[lens[i*n+j] for j in range(n)],slots)
+                attend_block(row,x,wqkv.at[e],vec.at[e],bias,k,v,A,q0,b)
+            if "2" in phases: out_block(row,x,A,wo.at[e],vec.at[e],N,a0,p1,b)
+            if "3" in phases: up_block(row,N,wup.at[e],hb.at[e],act,h0,b,arow)
+            if "4" in phases: down_block(row,N,act,wdn.at[e],vec.at[e],o,p2,b,arow)
+            return _
+        lax.fori_loop(0,nb,body,0)
+def forward(ql,pl_,qx,px,wqkv,wo,wup,wdn,vec,hb,phases="1234"):
+    S=jax.ShapeDtypeStruct
+    V=pl.BlockSpec(memory_space=pltpu.VMEM); SM=pl.BlockSpec(memory_space=pltpu.SMEM)
+    outs=[S(qx.shape,BF),S(px.shape,BF),S(qx.shape,BF),S(qx.shape,BF),S(px.shape,BF),S(px.shape,BF),S((64,768),F32),S((64,768),F32),S((64,768),F32),S((64,3072),F32),S((64,768),F32)]
+    return pl.pallas_call(functools.partial(fw_kernel,phases),out_shape=outs,in_specs=[SM,SM]+[V]*8,out_specs=[V]*11,
+      scratch_shapes=[pltpu.VMEM((256,256),F32),pltpu.VMEM((2048,768),BF),pltpu.VMEM((2048,768),F32),pltpu.VMEM((256,3072),BF)],
+      compiler_params=pltpu.CompilerParams(vmem_limit_bytes=62*2**20),name="fw")(ql,pl_,qx,px,wqkv,wo,wup,wdn,vec,hb)
+
+
+def small_tile(vectors, hidden_bias):
+    tile = jnp.zeros((1, 16, 128), vectors.dtype)
+    count, rows, width = vectors.shape
+    tile = tile.at[0, : count * rows, :width].set(vectors.reshape(count * rows, width))
+    return tile.at[0, count * rows : count * rows + count, : hidden_bias.shape[1]].set(hidden_bias)
+
+
+def small_whole(tiles, vectors, hidden_bias):
+    count, rows, width = vectors.shape
+    tiles = tiles.reshape(16, 16, 2, 128)
+    whole = tiles[:, : count * rows, :, :width].reshape(16, count, rows, 2, width)
+    whole = whole.transpose(1, 3, 2, 0, 4).reshape(count, 2 * rows, 16 * width)
+    bias = tiles[:, count * rows : count * rows + count, :, : hidden_bias.shape[1]]
+    bias = bias.transpose(1, 0, 2, 3).reshape(count, -1)
+    return (whole, bias)
+
+
+GATHER_ORDER = ((4, 0), (0, 1), (0, 0), (1, 1), (1, 0), (2, 1), (3, 1), (2, 0), (3, 0))
+
+
+def gather_weights_kernel(wqkv, wout, wup, wdown, vectors, hidden_bias):
+    arrays = (wqkv, wout, wup, wdown, small_tile(vectors, hidden_bias))
+    parts = (3, 1, 3, 3, 1)
+    units = []
+    for a, e in GATHER_ORDER:
+        rows = arrays[a].shape[1] // parts[a]
+        for j in range(parts[a]):
+            units.append((a, e, "MFM"[len(units) % 3], j * rows, rows))
+    schedule = ag_schedule(len(units), [i // 3 for i in range(len(units))])
+    whole = gather_call(arrays, units, schedule)
+    small = small_whole(whole[4], vectors, hidden_bias)
+    return tuple(
+        member.reshape(2, 16 * shard.shape[1], 2 * shard.shape[2])
+        for member, shard in zip(whole[:4], arrays[:4])
+    ) + small
+
+
+def first_state(index, tokens_low, keys_low, values, lengths, rows_of, weights):
+    queries, attended, pre_one, hidden_rows, pre_two = (
+        rows_of(member) for member in index
+    )
+    seq_count, model_width = queries.shape
+    seq_length = keys_low.shape[0] // seq_count
+    vec_f32 = weights[4].astype(jnp.float32)
+    scores = jnp.einsum(
+        "shc,skhc->shk",
+        queries.astype(jnp.bfloat16).reshape(seq_count, HEADS, -1),
+        head_split(keys_low, seq_count),
+        preferred_element_type=jnp.float32,
+    ) * (model_width // HEADS) ** (-0.5)
+    live = jnp.arange(seq_length)[None, :] < lengths[:, None]
+    scores = jnp.where(live[:, None, :], scores, NEGATIVE)
+    soft_first = jnp.exp(scores - jax.nn.logsumexp(scores, axis=-1, keepdims=True))
+    normed_low = layer_norm(pre_one, vec_f32[3], vec_f32[4]).astype(jnp.bfloat16)
+    return (
+        queries.astype(jnp.bfloat16),
+        keys_low,
+        values,
+        soft_first,
+        attended.astype(jnp.bfloat16),
+        pre_one,
+        normed_low,
+        hidden_rows,
+        smooth_gate(hidden_rows).astype(jnp.bfloat16),
+        pre_two,
+    )
+
+
+def kernels_fit(q_embed, p_embed, q_len, p_len):
+    return (
+        lax.axis_size("wq") == 16
+        and lax.axis_size("np") == 2
+        and q_embed.shape == (512, 768)
+        and p_embed.shape == (1536, 768)
+        and q_len.shape == (8,)
+        and p_len.shape == (6,)
+    )
+
+
 def shards(
     q_embed,
     p_embed,
@@ -334,7 +690,8 @@
     vectors,
     hidden_bias,
 ):
-    gathered = gather_weights(
+    fast = kernels_fit(q_embed, p_embed, q_len, p_len)
+    gathered = (gather_weights_kernel if fast else gather_weights)(
         query_key_value_weight,
         attention_output_weight,
         up_weight,
@@ -346,8 +703,32 @@
     both_axes = ("wq", "np")
     q_weights = tuple((member[0] for member in gathered))
     p_weights = tuple((member[1] for member in gathered))
-    p_encoded, p_stored = encode_forward(p_embed, p_len, p_weights)
-    q_encoded, q_stored = encode_forward(q_embed, q_len, q_weights)
+    if fast:
+        done = forward(
+            q_len,
+            p_len,
+            q_embed,
+            p_embed,
+            *gathered[:4],
+            gathered[4].astype(jnp.float32),
+            gathered[5].astype(jnp.float32)[:, None, :],
+        )
+        q_encoded, p_encoded = done[0], done[1]
+        q_stored = first_state(
+            done[6:],
+            q_embed,
+            done[2],
+            done[3],
+            q_len,
+            lambda m: m.reshape(8, 8, -1)[:2, :4].reshape(8, -1),
+            q_weights,
+        )
+        p_stored = first_state(
+            done[6:], p_embed, done[4], done[5], p_len, lambda m: m.reshape(8, 8, -1)[2:, 0], p_weights
+        )
+    else:
+        p_encoded, p_stored = encode_forward(p_embed, p_len, p_weights)
+        q_encoded, q_stored = encode_forward(q_embed, q_len, q_weights)
     model_width = q_embed.shape[1]
     ff_width = gathered[2].shape[2]
     q_count = q_len.shape[0]

time: 664 us -> 665 us (level)
  Pallas kernels: 0 us -> 219 us
  blocking collectives: 201 us -> 108 us
  matrix products: 142 us -> 63.2 us
  local copies, waits for them, and re-layouts: 224 us -> 178 us
  other arithmetic: 50.4 us -> 38.8 us
    pallas_call x0 -> x2, Pallas kernels: none -> 219 us  [the longest x1 136 us: gather_call(): pl.pallas_call(functools.partial(gather_kernel, units, schedule, n), out_...]
    dot_general x12 -> x2, matrix products: 90.1 us -> 3.68 us  [first_state(): jnp.einsum('shc,skhc->shk', queries.astype(jnp.bfloat16).reshape(seq_coun...]
    all_gather x8 -> x0, blocking collectives: 79.9 us -> none  [the longest x1 20.7 us: gather_weights(): lax.all_gather(np_parts[5], 'wq', axis=1, tiled=True)]
    unnamed x270 -> x201, local copies, waits for them, and re-layouts: 48 us -> 3.95 us
    another operation x6 -> x2, local copies, waits for them, and re-layouts: 0.65 us -> 27.5 us  [encode_backward(): query_key_value_weight.reshape(model_width, 3, HEADS, head_width)]
    reshape x9 -> x5, local copies, waits for them, and re-layouts: 45.4 us -> 26.9 us  [head_split(): matrix.reshape(seq_count, row_count // seq_count, HEADS, model_width // H...]
    reduce_sum x6 -> x2, other arithmetic: 13.6 us -> 0.33 us  [first_state(): jax.nn.logsumexp(scores, axis=-1, keepdims=True)]
    slice x5 -> x12, local copies, waits for them, and re-layouts: 50.4 us -> 41.2 us  [the longest x5 34.4 us: shards(): p_weights = tuple((member[1] for member in gathered))]
  transfers between devices with their start and end apart: 7 -> 4, of which waited for: 1 -> 1; matrix products, arithmetic and copies ran while one was open for 47% -> 19% of each run, Pallas kernels for 0% -> 0%
where the time goes in v2:
time: 665 us; the launch traced here: 654 us
  Pallas kernels  219 us (33%)
  local copies, waits for them, and re-layouts  178 us (27%)
  blocking collectives  108 us (16%)
  matrix products  63.2 us (10%)
  other arithmetic  38.8 us (6%)
  between operations  17.7 us (3%)
  waiting for transfers between devices  16.3 us (2%)
  starting transfers between devices  12.9 us (2%)
    pallas_call x1, Pallas kernels, gather_call(): pl.pallas_call(functools.partial(gather_kernel, units, schedule, n), out_...  136 us
    pallas_call x1, Pallas kernels, forward(): pl.pallas_call(functools.partial(fw_kernel, phases), out_shape=outs, in_s...  82.5 us
    all_gather x1, blocking collectives, shards(): heads = lax.all_gather(own_heads, both_axes, axis=0)  69.8 us
    unnamed x1, blocking collectives  38.3 us
    slice x5, local copies, waits for them, and re-layouts, shards(): p_weights = tuple((member[1] for member in gathered))  34.4 us
    another operation x2, local copies, waits for them, and re-layouts, encode_backward(): query_key_value_weight.reshape(model_width, 3, HEADS, head_width)  27.5 us
    reshape x5, local copies, waits for them, and re-layouts, head_split(): matrix.reshape(seq_count, row_count // seq_count, HEADS, model_width // H...  26.9 us
    all_to_all x1, waiting for transfers between devices, shards(): left = lax.all_to_all(left, both_axes, 0, 0)  15.6 us
  transfers between devices with their start and end apart: 4, of which 1 were waited for; matrix products, arithmetic and copies ran while one was open for 19% of the time, Pallas kernels for 0%

profile of v2, /device:TPU:0, one launch (start us, length us, event | category | flops | bytes accessed | tf_op | source)
XLA Modules:
  0.0 654.0 jit_solution(1754124253024020851)
XLA Ops:
  7.9 1.5 scatter.9.refs_4_
  9.9 136.5 %gather.1 = (bf16[2,4,2,96,2304]{4,3,2,1,0:T(8,128)(2,1)}, bf16[2,4,2,96,768]{4,3,2,1,0:T(8,128)(2,1)}, bf16[2,4,2,96,3072]{4,3,2,1,0:T(8,128)(2,1)}, bf16[2,4,2...) custom-call(bf16[2,48,1152]{2,1,0:T(8,128)(2,1)} %refs_0_.1, bf16[2,48,384]{2,1,0:T(8,128)(2,1)} %refs_1_.1, ...), custom_call_target="tpu_custom_call" | custom-call | tf_op jit(solution)/shard_map/gather/pallas_call | solution.py:500
  148.3 38.3 %all-reduce.1 = s32[704]{0:T(1024)S(1)} all-reduce(s32[704]{0:T(1024)S(1)} %add_dynamic-update-slice_fusion), channel_id=2, replica_groups=mesh['wq'=16,'np'=2] {'wq','np'}, use_global_device_ids=true, to_apply=%add.1 | all-reduce | flops 704 | bytes 5632
  189.5 82.5 %fw.1 = (bf16[512,768]{1,0:T(8,128)(2,1)}, bf16[1536,768]{1,0:T(8,128)(2,1)}, bf16[512,768]{1,0:T(8,128)(2,1)}, bf16[512,768]{1,0:T(8,128)(2,1)}, bf16[1536,768]...) custom-call(s32[8]{0:T(128)} %ql.1, s32[6]{0:T(128)} %pl_.1, ...), custom_call_target="tpu_custom_call" | custom-call | tf_op jit(solution)/shard_map/fw/pallas_call | solution.py:594
  273.0 1.4 multiply_reduce_fusion.9
  275.6 8.4 %fusion.161 = (bf16[1,4,2,384,768]{4,3,2,1,0:T(8,128)(2,1)}, bf16[1,4,2,384,768]{4,3,2,1,0:T(8,128)(2,1)}) fusion(bf16[2,4,2,384,768]{4,3,2,1,0:T(8,128)(2,1)} %get-tuple-element.54), kind=kLoop, calls=%fused_computation.299 | loop fusion | bytes 18874368 | tf_op jit(solution)/shard_map/slice | solution.py:705
  284.1 2.0 multiply_reduce_fusion.10
  286.6 8.7 %fusion.160 = (bf16[1,4,2,96,3072]{4,3,2,1,0:T(8,128)(2,1)}, bf16[1,4,2,96,3072]{4,3,2,1,0:T(8,128)(2,1)}) fusion(bf16[2,4,2,96,3072]{4,3,2,1,0:T(8,128)(2,1)} %get-tuple-element.53), kind=kLoop, calls=%fused_computation.298 | loop fusion | bytes 18874368 | tf_op jit(solution)/shard_map/slice | solution.py:705
  296.2 2.0 slice_reduce_fusion.6
  298.2 2.0 fusion.164
  300.3 1.4 multiply_convert_fusion.5
  301.7 1.5 slice.299
  305.7 69.8 %all-gather.3 = bf16[32,14,768]{2,1,0:T(8,128)(2,1)S(1)} all-gather(bf16[1,14,768]{2,1,0:T(8,128)(2,1)S(1)} %maximum_bitcast_fusion.3), channel_id=3, replica_groups=mesh['wq'=16,'np'=2] {'wq','np'}, dimensions={0}, use_global_device_ids=true | all-gather | bytes 709632 | tf_op jit(solution)/shard_map/all_gather | solution.py:737
  383.5 1.8 multiply_reduce_fusion.2
  388.4 4.4 convert_reduce_fusion.1
  392.9 2.1 multiply_reduce_fusion.3
  395.1 2.4 reshape.775
  397.5 2.5 fusion.24
  404.2 3.9 reshape.760
  408.1 2.5 fusion.4
  414.3 2.5 fusion.159
  417.0 1.8 fusion.128
  419.6 4.3 convert_reduce_fusion
  423.9 5.0 multiply_reduce_fusion
  431.3 6.0 reshape.763
  437.3 6.3 copy.201
  446.8 1.5 mul.615
  448.3 2.0 convert_reduce_fusion.7
  450.3 1.8 multiply_reduce_fusion.1
  452.2 8.2 %reshape.766 = bf16[6,256,12,64]{3,2,1,0:T(8,128)(2,1)} reshape(bf16[1536,768]{1,0:T(8,128)(2,1)} %get-tuple-element.65) | data formatting | bytes 4718592 | tf_op jit(solution)/shard_map/reshape | solution.py:51
  460.5 4.1 fusion.2
  467.9 1.5 maximum_maximum_fusion
  469.3 3.4 all-to-all-start
  485.2 3.3 all-to-all-start.2
  496.9 2.0 copy.176
  498.9 3.1 reshape.716
  510.1 5.5 fusion.162
  515.6 11.6 %copy.157 = bf16[1,4,2,96,2304]{3,2,1,4,0:T(2,128)(2,1)} copy(bf16[1,4,2,96,2304]{4,3,2,1,0:T(8,128)(2,1)} %get-tuple-element.127) | data formatting | bytes 7077888 | tf_op jit(solution)/shard_map/slice | solution.py:705
  527.2 13.8 %reshape_squeeze.7 = bf16[768,3,12,64]{0,3,2,1:T(8,128)(2,1)} reshape(bf16[1,4,2,96,2304]{3,2,1,4,0:T(2,128)(2,1)} %copy.157) | data formatting | bytes 7077888 | tf_op jit(solution)/shard_map/reshape;squeeze | solution.py:208
  544.2 1.4 broadcast_in_dim.113
  545.6 2.2 concatenate.72
  547.9 1.4 broadcast_in_dim.117
  549.3 1.5 broadcast_in_dim.116
  550.8 1.4 broadcast_in_dim.118
  552.2 2.2 concatenate.74
  554.4 2.2 fusion.18
  556.6 2.4 pad_maximum_fusion
  559.0 2.2 fusion.19
  561.9 1.4 convert_element_type.223
  563.4 8.0 %copy.144 = bf16[1,4,2,96,2304]{3,2,1,4,0:T(2,128)(2,1)} copy(bf16[1,4,2,96,2304]{4,3,2,1,0:T(8,128)(2,1)S(1)} %get-tuple-element.128) | data formatting | bytes 7077888 | tf_op jit(solution)/shard_map/slice | solution.py:704
  571.3 13.8 %reshape_squeeze.6 = bf16[768,3,12,64]{0,3,2,1:T(8,128)(2,1)} reshape(bf16[1,4,2,96,2304]{3,2,1,4,0:T(2,128)(2,1)} %copy.144) | data formatting | bytes 7077888 | tf_op jit(solution)/shard_map/reshape;squeeze | solution.py:208
  585.8 6.2 all-to-all-start.1
  593.0 1.5 fusion.20
  594.6 1.5 fusion.21
  596.2 1.7 fusion.35
  598.4 1.6 select_add_fusion.1
  600.0 3.1 select_add_fusion
  605.3 15.6 %all-to-all-done.1 = bf16[32,14,1152]{2,1,0:T(8,128)(2,1)} async-done(((bf16[32,14,1152]{2,1,0:T(8,128)(2,1)}), bf16[32,14,1152]{2,1,0:T(8,128)(2,1)}, u32[]{:S(2)}, u32[]{:S(2)}) %all-to-all-start.1) | async-done | bytes 1032224 | tf_op jit(solution)/shard_map/all_to_all | solution.py:783
  625.8 1.6 slice_bitcast_fusion
  628.4 2.0 convolution_bitcast_fusion.1
  631.7 1.9 convolution_bitcast_fusion.4
  633.6 2.1 convolution_bitcast_fusion
  635.8 1.8 convolution_bitcast_fusion.7
  637.6 1.8 convolution_bitcast_fusion.6
  (408 shorter events, 90.3 us)
Async XLA Ops:
  286.6 8.7 %copy-start.95 = (s32[8]{0:T(128)S(1)}, s32[8]{0:T(128)}, u32[]{:S(2)}) copy-start(s32[8]{0:T(128)} %ql.1) | copy-start | bytes 100
  286.6 9.4 %copy-start.2 = (bf16[2,4,2,96,768]{4,3,2,1,0:T(8,128)(2,1)S(1)}, bf16[2,4,2,96,768]{4,3,2,1,0:T(8,128)(2,1)}, u32[]{:S(2)}) copy-start(bf16[2,4,2,96,768]{4,3,2,1,0:T(8,128)(2,1)} %get-tuple-element.52) | copy-start | bytes 7077892
  296.0 7.2 %copy-start.90 = (s32[6]{0:T(128)S(1)}, s32[6]{0:T(128)}, u32[]{:S(2)}) copy-start(s32[6]{0:T(128)} %pl_.1) | copy-start | bytes 76
  301.7 93.3 %copy-start.55 = (bf16[2,4,768]{2,1,0:T(4,128)(2,1)}, bf16[2,4,768]{2,1,0:T(4,128)(2,1)S(1)}, u32[]{:S(2)}) copy-start(bf16[2,4,768]{2,1,0:T(4,128)(2,1)S(1)} %get-tuple-element.118) | copy-start | bytes 36868
  375.5 17.4 %copy-start.8 = (bf16[32,14,768]{2,1,0:T(8,128)(2,1)}, bf16[32,14,768]{2,1,0:T(8,128)(2,1)S(1)}, u32[]{:S(2)}) copy-start(bf16[32,14,768]{2,1,0:T(8,128)(2,1)S(1)} %all-gather.3) | copy-start | bytes 2064388
  376.4 10.7 %copy-start.35 = (f32[2,4,768]{2,1,0:T(4,128)S(1)}, f32[2,4,768]{2,1,0:T(4,128)}, u32[]{:S(2)}) copy-start(f32[2,4,768]{2,1,0:T(4,128)} %get-tuple-element.136) | copy-start | bytes 73732
  381.1 4.3 copy-start.34
  386.3 6.6 %copy-start.17 = (f32[2,4,3072]{2,1,0:T(4,128)}, f32[2,4,3072]{2,1,0:T(4,128)S(1)}, u32[]{:S(2)}) copy-start(f32[2,4,3072]{2,1,0:T(4,128)S(1)} %slice.294) | copy-start | bytes 294916
  387.1 14.2 %copy-start.87 = (f32[8]{0:T(128)}, f32[8]{0:T(128)S(1)}, u32[]{:S(2)}) copy-start(f32[8]{0:T(128)S(1)} %rsqrt.53) | copy-start | bytes 100
  388.4 4.4 copy-start.44
  388.4 4.4 copy-start
  388.4 4.5 copy-start.86
  394.9 5.1 copy-start.83
  404.2 6.9 %copy-start.7 = (bf16[8,64,12,64]{3,2,1,0:T(8,128)(2,1)S(1)}, bf16[8,64,12,64]{3,2,1,0:T(8,128)(2,1)}, u32[]{:S(2)}) copy-start(bf16[8,64,12,64]{3,2,1,0:T(8,128)(2,1)} %reshape.775) | copy-start | bytes 2359300
  408.1 4.7 copy-start.92
  408.1 4.7 copy-start.43
  408.1 4.9 copy-start.33
  408.1 8.7 %copy-start.91 = (f32[6]{0:T(128)S(1)}, f32[6]{0:T(128)}, u32[]{:S(2)}) copy-start(f32[6]{0:T(128)} %get-tuple-element.132) | copy-start | bytes 76
  408.1 8.7 %copy-start.20 = (f32[6,1,768]{2,1,0:T(1,128)S(1)}, f32[6,1,768]{2,1,0:T(1,128)}, u32[]{:S(2)}) copy-start(f32[6,1,768]{2,1,0:T(1,128)} %get-tuple-element.131) | copy-start | bytes 55300
  413.8 10.1 %copy-start.63 = (f32[768]{0:T(1024)}, f32[768]{0:T(1024)S(1)}, u32[]{:S(2)}) copy-start(f32[768]{0:T(1024)S(1)} %get-tuple-element.89) | copy-start | bytes 9220
  416.8 7.0 %copy-start.84 = (f32[6]{0:T(128)}, f32[6]{0:T(128)S(1)}, u32[]{:S(2)}) copy-start(f32[6]{0:T(128)S(1)} %broadcast_multiply_fusion.5) | copy-start | bytes 76
  417.0 6.8 %copy-start.88 = (f32[6]{0:T(128)}, f32[6]{0:T(128)S(1)}, u32[]{:S(2)}) copy-start(f32[6]{0:T(128)S(1)} %add_rsqrt_fusion.3) | copy-start | bytes 76
  419.6 4.3 copy-start.47
  419.6 4.3 copy-start.21
  423.9 5.1 copy-start.25
  423.9 5.6 copy-start.94
  423.9 6.1 copy-start.62
  423.9 7.4 %copy-start.5 = (bf16[1536,768]{1,0:T(8,128)(2,1)S(1)}, bf16[1536,768]{1,0:T(8,128)(2,1)}, u32[]{:S(2)}) copy-start(bf16[1536,768]{1,0:T(8,128)(2,1)} %get-tuple-element.64) | copy-start | bytes 7077892
  430.6 6.7 %copy-start.53 = (bf16[6,1,768]{2,0,1:T(8,128)(2,1)}, bf16[6,1,768]{2,0,1:T(8,128)(2,1)S(1)}, u32[]{:S(2)}) copy-start(bf16[6,1,768]{2,0,1:T(8,128)(2,1)S(1)} %get-tuple-element.120) | copy-start | bytes 27652
  443.6 4.7 copy-start.64
  460.5 4.1 copy-start.11
  460.5 4.1 copy-start.73
  460.5 4.2 copy-start.80
  465.7 18.5 %copy-start.3 = (bf16[512,768]{1,0:T(8,128)(2,1)S(1)}, bf16[512,768]{1,0:T(8,128)(2,1)}, u32[]{:S(2)}) copy-start(bf16[512,768]{1,0:T(8,128)(2,1)} %qx.1) | copy-start | bytes 2359300
  466.4 17.4 %copy-start.67 = (f32[3072]{0:T(1024)S(1)}, f32[3072]{0:T(1024)}, u32[]{:S(2)}) copy-start(f32[3072]{0:T(1024)} %get-tuple-element.113) | copy-start | bytes 36868
  466.4 17.5 %copy-start.66 = (f32[3072]{0:T(1024)S(1)}, f32[3072]{0:T(1024)}, u32[]{:S(2)}) copy-start(f32[3072]{0:T(1024)} %get-tuple-element.111) | copy-start | bytes 36868
  466.4 17.7 %copy-start.57 = (bf16[8,12,64]{2,0,1:T(8,128)(2,1)S(1)}, bf16[8,12,64]{2,0,1:T(8,128)(2,1)}, u32[]{:S(2)}) copy-start(bf16[8,12,64]{2,0,1:T(8,128)(2,1)} %get-tuple-element.98) | copy-start | bytes 36868
  466.4 17.7 %copy-start.77 = (bf16[8,12,64]{2,0,1:T(8,128)(2,1)S(1)}, bf16[8,12,64]{2,0,1:T(8,128)(2,1)}, u32[]{:S(2)}) copy-start(bf16[8,12,64]{2,0,1:T(8,128)(2,1)} %copy-done.76) | copy-start | bytes 36868
  466.4 18.0 %copy-start.40 = (f32[64,768]{1,0:T(8,128)S(1)}, f32[64,768]{1,0:T(8,128)}, u32[]{:S(2)}) copy-start(f32[64,768]{1,0:T(8,128)} %get-tuple-element.66) | copy-start | bytes 589828
  469.3 15.8 %all-to-all-start = ((bf16[2,14,3456]{2,1,0:T(8,128)(2,1)}), bf16[2,14,3456]{2,1,0:T(8,128)(2,1)S(1)}, u32[]{:S(2)}, u32[]{:S(2)}) async-start(bf16[2,14,3456]{2,1,0:T(8,128)(2,1)} %maximum_maximum_fusion), calls=%async_computation | async-start | bytes 442368 | tf_op jit(solution)/shard_map/all_to_all | solution.py:785
  478.4 11.0 %copy-start.36 = (f32[2,4,768]{2,1,0:T(4,128)S(1)}, f32[2,4,768]{2,1,0:T(4,128)}, u32[]{:S(2)}) copy-start(f32[2,4,768]{2,1,0:T(4,128)} %get-tuple-element.136) | copy-start | bytes 73732
  479.2 11.5 %copy-start.18 = (f32[2,4,3072]{2,1,0:T(4,128)S(1)}, f32[2,4,3072]{2,1,0:T(4,128)}, u32[]{:S(2)}) copy-start(f32[2,4,3072]{2,1,0:T(4,128)} %copy-done.17) | copy-start | bytes 294916
  483.5 8.0 %copy-start.22 = (f32[6,1,768]{2,1,0:T(1,128)S(1)}, f32[6,1,768]{2,1,0:T(1,128)}, u32[]{:S(2)}) copy-start(f32[6,1,768]{2,1,0:T(1,128)} %get-tuple-element.131) | copy-start | bytes 55300
  483.5 8.6 %copy-start.65 = (f32[768]{0:T(1024)S(1)}, f32[768]{0:T(1024)}, u32[]{:S(2)}) copy-start(f32[768]{0:T(1024)} %copy-done.63) | copy-start | bytes 9220
  483.5 11.2 %copy-start.54 = (bf16[6,1,768]{2,0,1:T(8,128)(2,1)S(1)}, bf16[6,1,768]{2,0,1:T(8,128)(2,1)}, u32[]{:S(2)}) copy-start(bf16[6,1,768]{2,0,1:T(8,128)(2,1)} %copy-done.53) | copy-start | bytes 27652
  484.1 5.1 copy-start.27
  485.2 100.6 %all-to-all-start.2 = ((f32[32,1,576]{2,1,0:T(1,128)}), f32[32,1,576]{2,1,0:T(1,128)}, u32[]{:S(2)}, u32[]{:S(2)}) async-start(f32[32,1,576]{2,1,0:T(1,128)} %copy.190), calls=%async_computation.2 | async-start | bytes 163840 | tf_op jit(solution)/shard_map/all_to_all | solution.py:800
  488.5 137.4 %all-gather.6.cloned.1.call-start = ((), (), s32[]{:S(2)}) async-start(), calls=%async_computation.3 | async-start | bytes 3760128 | tf_op jit(solution)/shard_map/all_gather | solution.py:785
  496.9 5.1 copy-start.81
  496.9 5.7 copy-start.69
  496.9 6.5 copy-start.1
  527.2 13.8 %copy-start.70 = (f32[16,48]{1,0:T(8,128)S(1)}, f32[16,48]{1,0:T(8,128)}, u32[]{:S(2)}) copy-start(f32[16,48]{1,0:T(8,128)} %mul.593) | copy-start | bytes 9220
  527.2 13.8 %copy-start.71 = (f32[16,48]{1,0:T(8,128)S(1)}, f32[16,48]{1,0:T(8,128)}, u32[]{:S(2)}) copy-start(f32[16,48]{1,0:T(8,128)} %add.178) | copy-start | bytes 9220
  554.4 4.6 copy-start.75
  556.6 4.6 copy-start.39
  585.8 35.2 %all-to-all-start.1 = ((bf16[32,14,1152]{2,1,0:T(8,128)(2,1)}), bf16[32,14,1152]{2,1,0:T(8,128)(2,1)}, u32[]{:S(2)}, u32[]{:S(2)}) async-start(bf16[32,14,1152]{2,1,0:T(8,128)(2,1)} %bitcast.340), calls=%async_computation.1 | async-start | bytes 2359296 | tf_op jit(solution)/shard_map/all_to_all | solution.py:783
  591.9 4.3 copy-start.52
  592.0 4.3 copy-start.60
  593.0 4.9 copy-start.50
  593.0 4.9 copy-start.59
  594.6 3.8 copy-start.28
  596.2 3.8 copy-start.29
  622.2 5.2 copy-start.6
  623.5 3.9 copy-start.4
  (38 other events, 73.0 us)
Sparse Core Ops, SparseCore 0:
  491.6 48.3 all-gather.5

commit v3 on v2

--- a/solution.py
+++ b/solution.py
@@ -7,6 +7,7 @@
 from jax.experimental import pallas as pl
 from jax.experimental.pallas import tpu as pltpu
 from jax.sharding import PartitionSpec as P
+
 
 HEADS = 12
 
@@ -320,6 +321,237 @@
         outer(normed, grad_hidden),
         outer(activated, grad_ffn),
     )
+
+
+BLK=256
+F32=jnp.float32; BF=jnp.bfloat16
+NEG=-1e30; EPS=1e-12
+def dot(a,b): return jnp.dot(a,b,preferred_element_type=F32)
+def norm(u,g,b):
+    c=u-jnp.mean(u,axis=-1,keepdims=True)
+    s=jnp.mean(c*c,axis=-1,keepdims=True)
+    return c*lax.rsqrt(s+EPS)*g+b
+def put_first(ref, e, i, cols, v):
+    if e==1:
+        ref[pl.ds(8+i,1),cols]=v[0:1]
+    else:
+        for j in range(4): ref[pl.ds(4*i+j,1),cols]=v[64*j:64*j+1]
+def make_bias(bias_ref, slot, lens, slots):
+    n=BLK//slots
+    key=lax.broadcasted_iota(jnp.int32,(BLK,BLK),0)
+    qry=lax.broadcasted_iota(jnp.int32,(BLK,BLK),1)
+    ok=key<lens[0]
+    if n>1:
+        ok=ok&(qry<slots)
+        for j in range(1,n):
+            ok=ok|((key>=j*slots)&(key<j*slots+lens[j])&(qry>=j*slots)&(qry<(j+1)*slots))
+    bias_ref[...]=jnp.where(ok,0.0,NEG)
+def attend_block(row, x_ref, wqkv, vec, bias_ref, k_ref, v_ref, att_ref, q0_ref, e, i):
+    x=x_ref[pl.ds(row,BLK),:]
+    for g in range(3):
+        cs=pl.ds(g*256,256)
+        q4=dot(x,wqkv[:,g*256:g*256+256])+vec[0:1,g*256:g*256+256]
+        q4=q4.astype(BF)
+        k4=dot(x,wqkv[:,768+g*256:768+g*256+256]).astype(BF)
+        v4=(dot(x,wqkv[:,1536+g*256:1536+g*256+256])+vec[1:2,g*256:g*256+256]).astype(BF)
+        k_ref[pl.ds(row,BLK),cs]=k4
+        v_ref[pl.ds(row,BLK),cs]=v4
+        put_first(q0_ref,e,i,slice(g*256,g*256+256),q4.astype(F32))
+        qT=(q4.astype(F32)*0.125).T.astype(BF)
+        vT=v4.astype(F32).T.astype(BF)
+        lane=lax.broadcasted_iota(jnp.int32,(BLK,256),1)
+        outs=[]
+        for h in range(4):
+            kh=jnp.where((lane>=64*h)&(lane<64*h+64),k4,jnp.zeros_like(k4))
+            s=dot(kh,qT)+bias_ref[...]
+            m=jnp.max(s,axis=0,keepdims=True)
+            p=jnp.exp(s-m)
+            l=jnp.sum(p,axis=0,keepdims=True)
+            o=dot(vT[64*h:64*h+64,:],p.astype(BF))
+            outs.append(o*(1.0/l))
+        oT=jnp.concatenate(outs,axis=0)
+        att_ref[pl.ds(row,BLK),cs]=oT.T.astype(BF)
+def out_block(row, x_ref, att_ref, wo, vec, n_ref, a0_ref, p1_ref, e, i):
+    att=att_ref[pl.ds(row,BLK),:]
+    put_first(a0_ref,e,i,slice(None),att.astype(F32))
+    pre=x_ref[pl.ds(row,BLK),:].astype(F32)+dot(att,wo[...])+vec[2:3,:]
+    put_first(p1_ref,e,i,slice(None),pre)
+    n_ref[pl.ds(row,BLK),:]=norm(pre,vec[3:4,:],vec[4:5,:])
+def gelu(u):
+    return 0.5*u*(1.0+jnp.tanh(0.7978845608028654*(u+0.044715*(u*u*u))))
+def up_block(row, n_ref, wup, hb, act_ref, h0_ref, e, i, arow):
+    nl=n_ref[pl.ds(row,BLK),:].astype(BF)
+    for t in range(12):
+        cs=slice(t*256,t*256+256)
+        h=dot(nl,wup[:,cs])+hb[0:1,cs]
+        put_first(h0_ref,e,i,cs,h)
+        act_ref[pl.ds(arow,BLK),cs]=gelu(h).astype(BF)
+def down_block(row, n_ref, act_ref, wdown, vec, o_ref, p2_ref, hd_ref, e, i, arow):
+    f=dot(act_ref[pl.ds(arow,BLK),:],wdown[...])+vec[5:6,:]
+    pre=n_ref[pl.ds(row,BLK),:]+f
+    put_first(p2_ref,e,i,slice(None),pre)
+    enc=norm(pre,vec[6:7,:],vec[7:8,:])
+    put_first(hd_ref,e,i,slice(None),enc)
+    o_ref[pl.ds(row,BLK),:]=enc.astype(BF)
+
+def fw_kernel(phases, ql, pl_, qx, px, wqkv, wo, wup, wdn, vec, hb, qo, po, qk, qv, pk, pv, q0, a0, p1, h0, p2, hd, bias, att, nrm, act):
+    for ref in (q0,a0,p1,h0,p2,hd): ref[...]=jnp.zeros_like(ref)
+    for e,(x,o,k,v,lens,nb,slots,base) in ((1,(px,po,pk,pv,pl_,6,256,2)),(0,(qx,qo,qk,qv,ql,2,64,0))):
+        n=256//slots
+        def body(i,_):
+            row=pl.multiple_of(i*BLK,BLK); b=base+i; arow=0
+            mrow=pl.multiple_of((base+i)*BLK,BLK)
+            A=att.at[pl.ds(base*BLK,nb*BLK)]; N=nrm.at[pl.ds(base*BLK,nb*BLK)]
+            if "1" in phases:
+                make_bias(bias,0,[lens[i*n+j] for j in range(n)],slots)
+                attend_block(row,x,wqkv.at[e],vec.at[e],bias,k,v,A,q0,e,i)
+            if "2" in phases: out_block(row,x,A,wo.at[e],vec.at[e],N,a0,p1,e,i)
+            if "3" in phases: up_block(row,N,wup.at[e],hb.at[e],act,h0,e,i,arow)
+            if "4" in phases: down_block(row,N,act,wdn.at[e],vec.at[e],o,p2,hd,e,i,arow)
+            return _
+        lax.fori_loop(0,nb,body,0)
+def forward(ql,pl_,qx,px,wqkv,wo,wup,wdn,vec,hb,phases="1234"):
+    S=jax.ShapeDtypeStruct
+    V=pl.BlockSpec(memory_space=pltpu.VMEM); SM=pl.BlockSpec(memory_space=pltpu.SMEM)
+    outs=[S(qx.shape,BF),S(px.shape,BF),S(qx.shape,BF),S(qx.shape,BF),S(px.shape,BF),S(px.shape,BF),S((16,768),F32),S((16,768),F32),S((16,768),F32),S((16,3072),F32),S((16,768),F32),S((16,768),F32)]
+    return pl.pallas_call(functools.partial(fw_kernel,phases),out_shape=outs,in_specs=[SM,SM]+[V]*8,out_specs=[V]*12,
+      scratch_shapes=[pltpu.VMEM((256,256),F32),pltpu.VMEM((2048,768),BF),pltpu.VMEM((2048,768),F32),pltpu.VMEM((256,3072),BF)],
+      compiler_params=pltpu.CompilerParams(vmem_limit_bytes=62*2**20),name="fw")(ql,pl_,qx,px,wqkv,wo,wup,wdn,vec,hb)
+
+
+def dot_nt(a,b): return lax.dot_general(a,b,(((1,),(1,)),((),())),preferred_element_type=F32)
+def gelu_slope(u):
+    t=jnp.tanh(0.7978845608028654*(u+0.044715*(u*u*u)))
+    return 0.5*(1.0+t)+0.5*u*(1.0-t*t)*(0.7978845608028654*(1.0+0.134145*(u*u)))
+def norm_grad(u,g,gy):
+    c=u-jnp.mean(u,axis=-1,keepdims=True)
+    r=lax.rsqrt(jnp.mean(c*c,axis=-1,keepdims=True)+EPS)
+    t=gy*g
+    gu=r*(t-jnp.mean(t,axis=-1,keepdims=True)-c*(r*r)*jnp.mean(t*c,axis=-1,keepdims=True))
+    return gu, jnp.sum(gy*c*r,axis=0,keepdims=True), jnp.sum(gy,axis=0,keepdims=True)
+LEFT_ROWS=288
+def heads_apart(rows, count):
+    n=rows.shape[0]
+    wide=jnp.concatenate([jnp.broadcast_to(rows[i:i+1],(16,768)) for i in range(n)],axis=0)
+    r=lax.broadcasted_iota(jnp.int32,wide.shape,0)%16
+    l=lax.broadcasted_iota(jnp.int32,wide.shape,1)//64
+    return jnp.where(r==l,wide,0.0)
+def back_one(e, base, nb, slots, lens, x, k, v, gtok, gr, q0, a0, p1, h0, p2, wqkv, wo, wup, wdn, vec, hb, ls, la, right, u_s, gq_s, sv_s, qa_s, ga_s):
+    n=256//slots
+    seqs=n*nb
+    R=16*n
+    rows=slice(8*e,8*e+8)
+    W=lambda ref: ref.at[e]
+    vv=vec[e]
+    pre2=p2[rows,:]; pre1=p1[rows,:]; hid=h0[rows,:]
+    g2,gain2,shift2=norm_grad(pre2,vv[6:7],gr[rows,:])
+    gffn=g2.astype(BF)
+    gact=dot_nt(gffn,wdn[e])
+    gh=(gact*gelu_slope(hid)).astype(BF)
+    act=gelu(hid)
+    gn=g2+dot_nt(gh,wup[e])
+    g1,gain1,shift1=norm_grad(pre1,vv[3:4],gn)
+    nlow=norm(pre1,vv[3:4],vv[4:5])
+    gb=g1.astype(BF)
+    ga=dot_nt(gb,wo[e]).astype(BF).astype(F32)
+    q0s=q0[rows,:]*0.125
+    qa_s[...]=heads_apart(q0s,8).astype(BF)
+    ga_s[...]=heads_apart(ga,8).astype(BF)
+    u_s[0]=dot_nt(qa_s[...],wqkv[e,:,768:1536]).astype(BF)
+    u_s[1]=dot_nt(ga_s[...],wqkv[e,:,1536:2304]).astype(BF)
+    gq_s[...]=jnp.zeros_like(gq_s); sv_s[...]=jnp.zeros_like(sv_s)
+    def block(i,_):
+        row=i*256
+        rr=i*R
+        K=k[pl.ds(row,256),:]; V=v[pl.ds(row,256),:]; X=x[pl.ds(row,256),:]
+        qa=qa_s[pl.ds(rr,R),:]; gab=ga_s[pl.ds(rr,R),:]
+        s=dot_nt(qa,K)
+        key=lax.broadcasted_iota(jnp.int32,(R,256),1)
+        if n==1:
+            ok=key<lens[i]
+        else:
+            grp=lax.broadcasted_iota(jnp.int32,(R,256),0)//16
+            ok=(grp<0)
+            for j in range(n):
+                ok=ok|((grp==j)&(key>=j*slots)&(key<j*slots+lens[i*n+j]))
+        s=jnp.where(ok,s,NEG)
+        p=jnp.exp(s-jnp.max(s,axis=1,keepdims=True))
+        p=p*(1.0/jnp.sum(p,axis=1,keepdims=True))
+        gs=dot_nt(gab,V)
+        gs=p*(gs-jnp.sum(p*gs,axis=1,keepdims=True))
+        both=jnp.concatenate([gs,p],axis=0)
+        bb=both.astype(BF)
+        gq=dot(bb[:R],K)
+        rr0=lax.broadcasted_iota(jnp.int32,(R,768),0); ll=lax.broadcasted_iota(jnp.int32,(R,768),1)//64
+        gq=jnp.where(rr0%16==ll,gq,0.0)*0.125
+        st=jnp.sum(bb[R:].astype(F32),axis=1,keepdims=True)
+        sv_s[...]=sv_s[...]+jnp.sum(st*gab.astype(F32),axis=0,keepdims=True)
+        mix=dot(bb,X)
+        for j in range(n):
+            slot=i*n+j
+            gq_s[pl.ds(slot,1),:]=jnp.sum(gq[16*j:16*j+16],axis=0,keepdims=True)
+            first=X[j*slots:j*slots+1].astype(F32)
+            for c in range(6):
+                cc=slice(128*c,128*c+128)
+                ls[e,c,pl.ds(32+slot,12,stride=8),:]=mix[16*j:16*j+12,cc]
+                ls[e,c,pl.ds(128+slot,12,stride=8),:]=mix[R+16*j:R+16*j+12,cc]
+                ls[e,c,pl.ds(16+slot,1),:]=first[:,cc]
+        uu=jnp.concatenate([u_s[0,pl.ds(rr,R),:],u_s[1,pl.ds(rr,R),:]],axis=0)
+        gtok[pl.ds(row,256),:]=dot(both.T.astype(BF),uu)
+        return _
+    for i in range(nb): block(i,0)
+    gql=gq_s[...].astype(BF)
+    extra=g1+dot_nt(gql,wqkv[e,:,0:768])
+    for i in range(seqs):
+        gtok[i*slots:i*slots+1,:]=gtok[i*slots:i*slots+1,:]+extra[i:i+1]
+    cs=lambda m: jnp.sum(m.astype(F32),axis=0,keepdims=True)
+    sums=jnp.concatenate([cs(gql),sv_s[0:1],cs(gb),gain1,shift1,cs(gffn),gain2,shift2],axis=0)
+    for c in range(6):
+        cc=slice(128*c,128*c+128)
+        ls[e,c,0:8,:]=nlow[:,cc]
+        ls[e,c,8:16,:]=a0[rows,cc]
+        ls[e,c,24:32,:]=sums[:,cc]
+    la[e,0:8,:]=act
+    la[e,8:16,:]=jnp.concatenate([cs(gh),jnp.zeros((7,3072),F32)],axis=0)
+    rt=[(gffn.astype(F32)),gh.astype(F32),gb.astype(F32)]
+    for half in range(2):
+        o=0
+        for m in rt:
+            w=m.shape[1]//2
+            right[half,rows,o:o+w]=m[:,half*w:half*w+w]; o+=w
+        last=[gql.astype(F32),q0s[:,:384]] if half==0 else [q0s[:,384:],ga]
+        for m in last:
+            right[half,rows,o:o+m.shape[1]]=m; o+=m.shape[1]
+def pick_matrix(off, lane0):
+    r=lax.broadcasted_iota(jnp.int32,(256,128),0); l=lax.broadcasted_iota(jnp.int32,(256,128),1)
+    return jnp.where((r-off==l-lane0)&(l>=lane0)&(l<lane0+48),1.0,0.0).astype(BF)
+def left_messages(ls, la, left):
+    two=lambda e,w: jnp.concatenate([ls[e,w//128],ls[e,w//128+1]],axis=1).astype(BF)
+    aq=la[0].astype(BF); ap=la[1].astype(BF)
+    def win(start, width):
+        w=min(start//128*128, width-256); return w, start-w
+    for j in range(16):
+        w,off=win(48*j,768)
+        m=dot(two(0,w),pick_matrix(off,0))+dot(two(1,w),pick_matrix(off,64))
+        m=m.astype(BF)
+        left[j,48:80,:]=m[0:32]; left[j,0:48,:]=m[32:80]; left[j,144:288,:]=m[80:224]
+        for t in range(4):
+            w,off=win(192*j+48*t,3072)
+            left[j,80+16*t:96+16*t,:]=(dot(aq[:,w:w+256],pick_matrix(off,0))+dot(ap[:,w:w+256],pick_matrix(off,64))).astype(BF)
+def back_kernel(ql,pln,gr,q0,a0,p1,h0,p2,qx,px,qk,qv,pk,pv,wqkv,wo,wup,wdn,vec,hb,gq_tok,gp_tok,left,right,ls,la,rs,u_s,gq_s,sv_s,qa_s,ga_s):
+    ls[...]=jnp.zeros_like(ls)
+    back_one(1,2,6,256,pln,px,pk,pv,gp_tok,gr,q0,a0,p1,h0,p2,wqkv,wo,wup,wdn,vec,hb,ls,la,rs,u_s,gq_s,sv_s,qa_s,ga_s)
+    back_one(0,0,2,64,ql,qx,qk,qv,gq_tok,gr,q0,a0,p1,h0,p2,wqkv,wo,wup,wdn,vec,hb,ls,la,rs,u_s,gq_s,sv_s,qa_s,ga_s)
+    right[...]=rs[...].astype(BF)
+    left_messages(ls,la,left)
+def backward(*a):
+    S=jax.ShapeDtypeStruct
+    V=pl.BlockSpec(memory_space=pltpu.VMEM); SM=pl.BlockSpec(memory_space=pltpu.SMEM)
+    outs=[S((512,768),F32),S((1536,768),F32),S((16,LEFT_ROWS,128),BF),S((2,16,3456),BF)]
+    VM=pltpu.VMEM
+    return pl.pallas_call(back_kernel,out_shape=outs,in_specs=[SM,SM]+[V]*18,out_specs=[V]*4,
+      scratch_shapes=[VM((2,6,224,128),F32),VM((2,16,3072),F32),VM((2,16,3456),F32),VM((2,128,768),BF),VM((8,768),F32),VM((8,768),F32),VM((128,768),BF),VM((128,768),BF)],
+      compiler_params=pltpu.CompilerParams(vmem_limit_bytes=60*2**20),name="back")(*a)
 
 
 MESH = pl.DeviceIdType.MESH
@@ -503,97 +735,250 @@
         compiler_params=pltpu.CompilerParams(collective_id=1, has_side_effects=True), name=name)(*arrays)
 
 
-BLK=256
-F32=jnp.float32; BF=jnp.bfloat16
-NEG=-1e30; EPS=1e-12
-def dot(a,b): return jnp.dot(a,b,preferred_element_type=F32)
-def norm(u,g,b):
-    c=u-jnp.mean(u,axis=-1,keepdims=True)
-    s=jnp.mean(c*c,axis=-1,keepdims=True)
-    return c*lax.rsqrt(s+EPS)*g+b
-def pick(v):
-    r=[v[i*64:i*64+1] for i in range(4)]
-    return jnp.concatenate(r+[jnp.zeros_like(v[0:4])],axis=0)
-def make_bias(bias_ref, slot, lens, slots):
-    n=BLK//slots
-    key=lax.broadcasted_iota(jnp.int32,(BLK,BLK),0)
-    qry=lax.broadcasted_iota(jnp.int32,(BLK,BLK),1)
-    ok=key<lens[0]
-    if n>1:
-        ok=ok&(qry<slots)
-        for j in range(1,n):
-            ok=ok|((key>=j*slots)&(key<j*slots+lens[j])&(qry>=j*slots)&(qry<(j+1)*slots))
-    bias_ref[...]=jnp.where(ok,0.0,NEG)
-def attend_block(row, x_ref, wqkv, vec, bias_ref, k_ref, v_ref, att_ref, q0_ref, b):
-    x=x_ref[pl.ds(row,BLK),:]
-    for g in range(3):
-        cs=pl.ds(g*256,256)
-        q4=dot(x,wqkv[:,g*256:g*256+256])+vec[0:1,g*256:g*256+256]
-        q4=q4.astype(BF)
-        k4=dot(x,wqkv[:,768+g*256:768+g*256+256]).astype(BF)
-        v4=(dot(x,wqkv[:,1536+g*256:1536+g*256+256])+vec[1:2,g*256:g*256+256]).astype(BF)
-        k_ref[pl.ds(row,BLK),cs]=k4
-        v_ref[pl.ds(row,BLK),cs]=v4
-        q0_ref[pl.ds(pl.multiple_of(b*8,8),8),cs]=pick(q4.astype(F32))
-        qT=(q4.astype(F32)*0.125).T.astype(BF)
-        vT=v4.astype(F32).T.astype(BF)
-        lane=lax.broadcasted_iota(jnp.int32,(BLK,256),1)
-        outs=[]
-        for h in range(4):
-            kh=jnp.where((lane>=64*h)&(lane<64*h+64),k4,jnp.zeros_like(k4))
-            s=dot(kh,qT)+bias_ref[...]
-            m=jnp.max(s,axis=0,keepdims=True)
-            p=jnp.exp(s-m)
-            l=jnp.sum(p,axis=0,keepdims=True)
-            o=dot(vT[64*h:64*h+64,:],p.astype(BF))
-            outs.append(o*(1.0/l))
-        oT=jnp.concatenate(outs,axis=0)
-        att_ref[pl.ds(row,BLK),cs]=oT.T.astype(BF)
-def out_block(row, x_ref, att_ref, wo, vec, n_ref, a0_ref, p1_ref, b):
-    att=att_ref[pl.ds(row,BLK),:]
-    r8=pl.ds(pl.multiple_of(b*8,8),8)
-    a0_ref[r8,:]=pick(att.astype(F32))
-    pre=x_ref[pl.ds(row,BLK),:].astype(F32)+dot(att,wo[...])+vec[2:3,:]
-    p1_ref[r8,:]=pick(pre)
-    n_ref[pl.ds(row,BLK),:]=norm(pre,vec[3:4,:],vec[4:5,:])
-def gelu(u):
-    return 0.5*u*(1.0+jnp.tanh(0.7978845608028654*(u+0.044715*(u*u*u))))
-def up_block(row, n_ref, wup, hb, act_ref, h0_ref, b, arow):
-    nl=n_ref[pl.ds(row,BLK),:].astype(BF)
-    r8=pl.ds(pl.multiple_of(b*8,8),8)
-    for t in range(12):
-        cs=slice(t*256,t*256+256)
-        h=dot(nl,wup[:,cs])+hb[0:1,cs]
-        h0_ref[r8,cs]=pick(h)
-        act_ref[pl.ds(arow,BLK),cs]=gelu(h).astype(BF)
-def down_block(row, n_ref, act_ref, wdown, vec, o_ref, p2_ref, b, arow):
-    f=dot(act_ref[pl.ds(arow,BLK),:],wdown[...])+vec[5:6,:]
-    pre=n_ref[pl.ds(row,BLK),:]+f
-    p2_ref[pl.ds(pl.multiple_of(b*8,8),8),:]=pick(pre)
-    o_ref[pl.ds(row,BLK),:]=norm(pre,vec[6:7,:],vec[7:8,:]).astype(BF)
-
-def fw_kernel(phases, ql, pl_, qx, px, wqkv, wo, wup, wdn, vec, hb, qo, po, qk, qv, pk, pv, q0, a0, p1, h0, p2, bias, att, nrm, act):
-    for e,(x,o,k,v,lens,nb,slots,base) in ((1,(px,po,pk,pv,pl_,6,256,2)),(0,(qx,qo,qk,qv,ql,2,64,0))):
-        n=256//slots
-        def body(i,_):
-            row=pl.multiple_of(i*BLK,BLK); b=base+i; arow=0
-            mrow=pl.multiple_of((base+i)*BLK,BLK)
-            A=att.at[pl.ds(base*BLK,nb*BLK)]; N=nrm.at[pl.ds(base*BLK,nb*BLK)]
-            if "1" in phases:
-                make_bias(bias,0,[lens[i*n+j] for j in range(n)],slots)
-                attend_block(row,x,wqkv.at[e],vec.at[e],bias,k,v,A,q0,b)
-            if "2" in phases: out_block(row,x,A,wo.at[e],vec.at[e],N,a0,p1,b)
-            if "3" in phases: up_block(row,N,wup.at[e],hb.at[e],act,h0,b,arow)
-            if "4" in phases: down_block(row,N,act,wdn.at[e],vec.at[e],o,p2,b,arow)
-            return _
-        lax.fori_loop(0,nb,body,0)
-def forward(ql,pl_,qx,px,wqkv,wo,wup,wdn,vec,hb,phases="1234"):
-    S=jax.ShapeDtypeStruct
-    V=pl.BlockSpec(memory_space=pltpu.VMEM); SM=pl.BlockSpec(memory_space=pltpu.SMEM)
-    outs=[S(qx.shape,BF),S(px.shape,BF),S(qx.shape,BF),S(qx.shape,BF),S(px.shape,BF),S(px.shape,BF),S((64,768),F32),S((64,768),F32),S((64,768),F32),S((64,3072),F32),S((64,768),F32)]
-    return pl.pallas_call(functools.partial(fw_kernel,phases),out_shape=outs,in_specs=[SM,SM]+[V]*8,out_specs=[V]*11,
-      scratch_shapes=[pltpu.VMEM((256,256),F32),pltpu.VMEM((2048,768),BF),pltpu.VMEM((2048,768),F32),pltpu.VMEM((256,3072),BF)],
-      compiler_params=pltpu.CompilerParams(vmem_limit_bytes=62*2**20),name="fw")(ql,pl_,qx,px,wqkv,wo,wup,wdn,vec,hb)
+class Place:
+    def __init__(self):
+        self.w=lax.axis_index("wq"); self.y=lax.axis_index("np")
+        self.z,self.x,self.c=self.w//4,(self.w//2)%2,self.w%2
+        self.me=self.w*2+self.y
+    def dev(self, z=None, fx=False, fy=False, fc=False):
+        x=1-self.x if fx else self.x
+        c=1-self.c if fc else self.c
+        y=1-self.y if fy else self.y
+        return ((self.z if z is None else z)*4+x*2+c, y)
+
+def head_gather(pos, buf, send, recv):
+    z,x,c,y=pos.z,pos.x,pos.c,pos.y
+    def rc(sem,src,dev,dst=None):
+        return pltpu.make_async_remote_copy(src_ref=src,dst_ref=src if dst is None else dst,send_sem=send.at[sem],recv_sem=recv.at[sem],device_id=dev,device_id_type=MESH)
+    own=buf.at[z,x,c,y]
+    for k in (1,2,3): rc(k-1,own,pos.dev(z=(z+k)%4)).start()
+    def arrived(sem,ref): rc(sem,ref,pos.dev(fc=True)).wait_recv()
+    for k in (1,2,3): arrived(k-1,buf.at[(z+4-k)%4,x,c,y])
+    col=buf.at[:,x,c,y]
+    def order(core):
+        first=dict(fx=True) if core==0 else dict(fy=True)
+        second=dict(fy=True) if core==0 else dict(fx=True)
+        rc(3,col,pos.dev(**first)).start()
+        rc(5,col,pos.dev(fc=True)).start()
+        got=buf.at[:,1-x,c,y] if core==0 else buf.at[:,x,c,1-y]
+        arrived(3,got)
+        both=buf.at[:,:,c,y] if core==0 else buf.at[:,x,c,:]
+        rc(4,both,pos.dev(**second)).start()
+        rc(6,got,pos.dev(fc=True)).start()
+        last=buf.at[:,:,c,1-y] if core==0 else buf.at[:,1-x,c,:]
+        arrived(4,last)
+        rc(7,last,pos.dev(fc=True)).start()
+        o=1-c
+        arrived(5,buf.at[:,x,o,y])
+        arrived(6,buf.at[:,x,o,1-y] if core==0 else buf.at[:,1-x,o,y])
+        arrived(7,buf.at[:,1-x,o,:] if core==0 else buf.at[:,:,o,1-y])
+        for sem,ref in ((3,col),(4,both),(5,col),(6,got),(7,last)): rc(sem,ref,pos.dev(fc=True)).wait_send()
+    for core in (0,1): pl.when(c==core)(functools.partial(order,core))
+    for k in (1,2,3): rc(k-1,own,pos.dev(fc=True)).wait_send()
+
+def similar_kernel(heads, marks, gr, loss, buf, gs_s, gt_s, send, recv):
+    pos=Place()
+    bar=pltpu.get_barrier_semaphore()
+    for k in (1,2,3): pl.semaphore_signal(bar,inc=1,device_id=pos.dev(z=(pos.z+k)%4),device_id_type=MESH)
+    for kw in (dict(fx=True),dict(fy=True),dict(fc=True)): pl.semaphore_signal(bar,inc=1,device_id=pos.dev(**kw),device_id_type=MESH)
+    buf[pos.z,pos.x,pos.c,pos.y]=heads[...].astype(BF)
+    pl.semaphore_wait(bar,6)
+    head_gather(pos,buf,send,recv)
+    g=buf[...].reshape(32,16,768).astype(F32)
+    q=g[:,0:8].reshape(256,768).astype(BF); p=g[:,8:16].reshape(256,768).astype(BF)
+    m=jnp.sum(marks[...].reshape(8,32,256),axis=0)
+    m=m[0:16]+m[16:32]
+    m=(m[:,0:128]+m[:,128:256]).astype(F32)
+    row=lambda r: jnp.broadcast_to(jnp.concatenate([m[r:r+1],m[r+1:r+2]],axis=1),(256,256))
+    qset=row(0).T; gold=row(2).T; pset=row(4)
+    lane=lax.broadcasted_iota(jnp.int32,(256,256),1).astype(F32)
+    is_gold=gold==lane
+    usable=(qset==pset)|is_gold
+    sim=dot_nt(q,p)*(768**-0.5)
+    masked=jnp.where(usable,sim,NEG)
+    high=jnp.max(masked,axis=1,keepdims=True)
+    tot=high+jnp.log(jnp.sum(jnp.where(usable,jnp.exp(masked-high),0.0),axis=1,keepdims=True))
+    gsc=jnp.sum(jnp.where(is_gold,sim,0.0),axis=1,keepdims=True)
+    loss[...]=jnp.broadcast_to(jnp.sum(tot-gsc,axis=0,keepdims=True)*(1.0/256),loss.shape)
+    soft=jnp.where(usable,jnp.exp(masked-tot),0.0)
+    gsim=soft-jnp.where(is_gold,1.0,0.0)
+    gs_s[...]=gsim; gt_s[...]=gsim.T
+    me8=pl.ds(pl.multiple_of(pos.me*8,8),8)
+    gr[0:8,:]=dot(gs_s[me8,:].astype(BF),p)*(768**-0.5)
+    gr[8:16,:]=dot(gt_s[me8,:].astype(BF),q)*(768**-0.5)
+
+def similar_call(heads,marks):
+    V=pl.BlockSpec(memory_space=pltpu.VMEM)
+    return pl.pallas_call(similar_kernel,out_shape=[jax.ShapeDtypeStruct((16,768),F32),jax.ShapeDtypeStruct((8,128),F32)],in_specs=[V,V],out_specs=[V,V],
+      scratch_shapes=[pltpu.VMEM((4,2,2,2,16,768),BF),pltpu.VMEM((256,256),F32),pltpu.VMEM((256,256),F32),pltpu.SemaphoreType.DMA((8,)),pltpu.SemaphoreType.DMA((8,))],
+      compiler_params=pltpu.CompilerParams(collective_id=2,has_side_effects=True,vmem_limit_bytes=40*2**20),name="similar")(heads,marks)
+
+CHUNKS=3
+class RightGather:
+    def __init__(self,pos,src,buf,send,recv):
+        self.pos,self.src,self.buf,self.send,self.recv=pos,src,buf,send,recv
+        self.width=src.shape[2]//CHUNKS
+    def rc(self,ch,sem,src,dst,dev):
+        return pltpu.make_async_remote_copy(src_ref=src,dst_ref=dst,send_sem=self.send.at[ch,sem],recv_sem=self.recv.at[ch,sem],device_id=dev,device_id_type=MESH)
+    def view(self,ch,z=None,x=None,c=None,y=None):
+        p=self.pos
+        f=lambda v: slice(None) if v is None else v
+        return self.buf.at[f(z),p.x if x is None else x,p.c if c is None else c,f(y),:,ch*self.width:(ch+1)*self.width]
+    def half(self,ch,y): return self.src.at[y,:,ch*self.width:(ch+1)*self.width]
+    def step(self,ch,s):
+        p=self.pos; z,y=p.z,p.y
+        sib=p.dev(fc=True)
+        def arrived(sem,v): self.rc(ch,sem,v,v,sib).wait_recv()
+        def local(sem,v): self.rc(ch,sem,v,v,sib).start()
+        def z_send(hop):
+            @pl.when((z-hop>=0)&(z+1<=3))
+            def _():
+                v=self.view(ch,z=z-hop); self.rc(ch,2+hop,v,v,p.dev(z=z+1)).start()
+            @pl.when((z+hop<=3)&(z-1>=0))
+            def _():
+                v=self.view(ch,z=z+hop); self.rc(ch,5+hop,v,v,p.dev(z=z-1)).start()
+        def z_wait(hop):
+            @pl.when(z-1-hop>=0)
+            def _():
+                v=self.view(ch,z=z-1-hop); arrived(2+hop,v); local(9+hop,v)
+            @pl.when(z+1+hop<=3)
+            def _():
+                v=self.view(ch,z=z+1+hop); arrived(5+hop,v); local(12+hop,v)
+        own=self.view(ch,z=z,y=y)
+        if s==0:
+            self.rc(ch,0,self.half(ch,1-y),own,p.dev(fy=True)).start()
+            pltpu.make_async_copy(self.half(ch,y),own,self.send.at[ch,16]).start()
+        if s==1:
+            pltpu.make_async_copy(self.half(ch,y),own,self.send.at[ch,16]).wait()
+            arrived(0,self.view(ch,z=z,y=1-y))
+            z_send(0); local(8,self.view(ch,z=z))
+        if s==2: z_wait(0); z_send(1)
+        if s==3: z_wait(1); z_send(2)
+        if s==4:
+            z_wait(2)
+            v=self.view(ch); self.rc(ch,1,v,v,p.dev(fx=True)).start()
+        if s==5:
+            g=self.view(ch,x=1-p.x); arrived(1,g); local(15,g)
+        if s==6:
+            o=1-p.c
+            arrived(8,self.view(ch,z=z,c=o)); arrived(15,self.view(ch,x=1-p.x,c=o))
+            def sent(sem,v): self.rc(ch,sem,v,v,sib).wait_send()
+            sent(0,own); sent(1,self.view(ch)); sent(8,self.view(ch,z=z)); sent(15,self.view(ch,x=1-p.x))
+            for hop in range(3):
+                pl.when(z-1-hop>=0)(lambda hop=hop: arrived(9+hop,self.view(ch,z=z-1-hop,c=o)))
+                pl.when(z+1+hop<=3)(lambda hop=hop: arrived(12+hop,self.view(ch,z=z+1+hop,c=o)))
+                pl.when((z-hop>=0)&(z+1<=3))(lambda hop=hop: sent(2+hop,self.view(ch,z=z-hop)))
+                pl.when((z+hop<=3)&(z-1>=0))(lambda hop=hop: sent(5+hop,self.view(ch,z=z+hop)))
+                pl.when(z-1-hop>=0)(lambda hop=hop: sent(9+hop,self.view(ch,z=z-1-hop)))
+                pl.when(z+1+hop<=3)(lambda hop=hop: sent(12+hop,self.view(ch,z=z+1+hop)))
+
+def left_copies(pos,left,buf,send,recv):
+    def to(d):
+        t=(pos.me+d)%32
+        return t//2,t%2
+    def send_one(d,go):
+        w,y=to(d)
+        for half,(r0,n) in enumerate(((0,144),(48,240))):
+            @pl.when(y==half)
+            def _():
+                go(pltpu.make_async_remote_copy(src_ref=left.at[w,pl.ds(r0,n)],dst_ref=buf.at[pos.me,pl.ds(0,n)],send_sem=send.at[d],recv_sem=recv.at[d],device_id=(w,y),device_id_type=MESH))
+    def start():
+        def lap(d,kept):
+            send_one(d,lambda cp: cp.start()); return kept
+        lax.fori_loop(1,32,lap,0)
+    def finish():
+        def lap(d,kept):
+            send_one(d,lambda cp: cp.wait_send())
+            s=(pos.me+32-d)%32
+            for half,(r0,n) in enumerate(((0,144),(48,240))):
+                @pl.when(pos.y==half)
+                def _():
+                    v=buf.at[s,pl.ds(0,n)]
+                    pltpu.make_async_remote_copy(src_ref=v,dst_ref=v,send_sem=send.at[d],recv_sem=recv.at[d],device_id=(pos.w,pos.y),device_id_type=MESH).wait_recv()
+            return kept
+        lax.fori_loop(1,32,lap,0)
+    def own():
+        for half,(r0,n) in enumerate(((0,144),(48,240))):
+            @pl.when(pos.y==half)
+            def _(): buf[pos.me,0:n,:]=left[pos.w,r0:r0+n,:]
+    return start,own,finish
+
+def all_barrier(pos):
+    bar=pltpu.get_barrier_semaphore()
+    def lap(d,kept):
+        t=(pos.me+d)%32
+        pl.semaphore_signal(bar,inc=1,device_id=(t//2,t%2),device_id_type=MESH)
+        return kept
+    lax.fori_loop(1,32,lap,0)
+    pl.semaphore_wait(bar,31)
+
+def weight_products(pos,lbuf,rbuf,wqkv,wout,win,wback,gvec,gbin,bq,bp):
+    r=rbuf[...].reshape(32,16,3456).astype(F32)
+    bq[...]=r[:,0:8].reshape(256,3456).astype(BF)
+    bp[...]=r[:,8:16].reshape(256,3456).astype(BF)
+    def pair(r0):
+        t=lbuf[:,r0:r0+16,:].astype(F32)
+        return [t[:,8*i:8*i+8].reshape(256,128) for i in (0,1)]
+    def put(out,rows,cols,tt,bcols):
+        tt=tt.T.astype(BF)
+        out[0,rows,cols]=dot(tt,bq[:,bcols])[0:48]
+        out[1,rows,cols]=dot(tt,bp[:,bcols])[64:112]
+    everything=slice(None)
+    def common(base):
+        nrm,att=pair(base)
+        put(win,everything,everything,nrm,slice(384,1920))
+        put(wout,everything,everything,att,slice(1920,2304))
+        for k in range(4):
+            put(wback,slice(48*k,48*k+48),everything,pair(base+32+16*k)[0],slice(0,384))
+        x0,vs=pair(base+16)
+        vs=jnp.sum(vs.reshape(32,8,128),axis=0)
+        bs=[jnp.sum(pair(base+32+16*k)[1].reshape(32,8,128),axis=0)[0:1] for k in range(4)]
+        return x0,vs,bs
+    def mixed(r0,heads,col0,dst0):
+        for h in range(0,heads,2):
+            a,b=pair(r0+8*h)
+            a=a.T.astype(BF); b=b.T.astype(BF)
+            cs=slice(col0+64*h,col0+64*h+128); ds=slice(dst0+64*h,dst0+64*h+128)
+            low=lax.broadcasted_iota(jnp.int32,(128,128),1)<64
+            wqkv[0,:,ds]=jnp.where(low,dot(a,bq[:,cs]),dot(b,bq[:,cs]))[0:48]
+            wqkv[1,:,ds]=jnp.where(low,dot(a,bp[:,cs]),dot(b,bp[:,cs]))[64:112]
+    def sums(vs,bs,half):
+        gvec[0]=vs[4*half:4*half+4,0:48]; gvec[1]=vs[4*half:4*half+4,64:112]
+        for i in (0,1):
+            gbin[0,i:i+1,:]=bs[2*half+i][:,0:48]; gbin[1,i:i+1,:]=bs[2*half+i][:,64:112]
+    @pl.when(pos.y==0)
+    def _():
+        x0,vs,bs=common(48)
+        put(wqkv,everything,slice(0,768),x0,slice(2304,3072))
+        mixed(0,6,3072,768)
+        sums(vs,bs,0)
+    @pl.when(pos.y==1)
+    def _():
+        x0,vs,bs=common(0)
+        mixed(96,6,2304,0)
+        mixed(144,12,2688,384)
+        sums(vs,bs,1)
+
+def exchange_kernel(left,right,wqkv,wout,win,wback,gvec,gbin,lbuf,rbuf,bq,bp,lsend,lrecv,rsend,rrecv):
+    pos=Place()
+    all_barrier(pos)
+    g=RightGather(pos,right,rbuf,rsend,rrecv)
+    lstart,lown,lfinish=left_copies(pos,left,lbuf,lsend,lrecv)
+    for ch in range(CHUNKS): g.step(ch,0)
+    lstart()
+    lown()
+    for t in range(CHUNKS+6):
+        for ch in range(CHUNKS):
+            if 1<=t-ch<=6: g.step(ch,t-ch)
+    lfinish()
+    weight_products(pos,lbuf,rbuf,wqkv,wout,win,wback,gvec,gbin,bq,bp)
+
+def exchange_call(left,right):
+    V=pl.BlockSpec(memory_space=pltpu.VMEM); S=jax.ShapeDtypeStruct; VM=pltpu.VMEM; D=pltpu.SemaphoreType.DMA
+    outs=[S((2,48,1152),F32),S((2,48,384),F32),S((2,48,1536),F32),S((2,192,384),F32),S((2,4,48),F32),S((2,2,48),F32)]
+    return pl.pallas_call(exchange_kernel,out_shape=outs,in_specs=[V,V],out_specs=[V]*6,
+      scratch_shapes=[VM((32,240,128),BF),VM((4,2,2,2,16,3456),BF),VM((256,3456),BF),VM((256,3456),BF),D((32,)),D((32,)),D((CHUNKS,17)),D((CHUNKS,17))],
+      compiler_params=pltpu.CompilerParams(collective_id=3,has_side_effects=True,vmem_limit_bytes=50*2**20),name="exchange")(left,right)
 
 
 def small_tile(vectors, hidden_bias):
@@ -613,54 +998,51 @@
     return (whole, bias)
 
 
-GATHER_ORDER = ((4, 0), (0, 1), (0, 0), (1, 1), (1, 0), (2, 1), (3, 1), (2, 0), (3, 0))
-
-
-def gather_weights_kernel(wqkv, wout, wup, wdown, vectors, hidden_bias):
-    arrays = (wqkv, wout, wup, wdown, small_tile(vectors, hidden_bias))
-    parts = (3, 1, 3, 3, 1)
+def mark_tile(q_set, gold, p_set):
+    me = lax.axis_index("wq") * 2 + lax.axis_index("np")
+    spare = jnp.full((8 - p_set.shape[0],), -1, jnp.int32)
+    columns = gold // p_set.shape[0] * 8 + gold % p_set.shape[0]
+    rows = jnp.stack([q_set, columns, jnp.concatenate([p_set, spare])])
+    rows = jnp.where((jnp.arange(256) // 8 == me)[None, :], jnp.tile(rows, (1, 32)), 0)
+    return jnp.zeros((1, 16, 128), jnp.int32).at[0, :6].set(rows.reshape(6, 128))
+
+
+GATHER_ORDER = ((4, 0), (5, 0), (0, 1), (0, 0), (1, 1), (1, 0), (2, 1), (3, 1), (2, 0), (3, 0))
+
+
+def gather_units(arrays):
+    parts = (3, 1, 3, 3, 1, 1)
     units = []
     for a, e in GATHER_ORDER:
         rows = arrays[a].shape[1] // parts[a]
         for j in range(parts[a]):
             units.append((a, e, "MFM"[len(units) % 3], j * rows, rows))
-    schedule = ag_schedule(len(units), [i // 3 for i in range(len(units))])
-    whole = gather_call(arrays, units, schedule)
-    small = small_whole(whole[4], vectors, hidden_bias)
-    return tuple(
+    return units, ag_schedule(len(units), [max(i - 1, 0) // 3 for i in range(len(units))])
+
+
+def kernel_shards(
+    q_embed, p_embed, q_len, p_len, q_set, p_set, gold, wqkv, wout, wup, wdown, vectors, hidden_bias
+):
+    arrays = (
+        wqkv, wout, wup, wdown, small_tile(vectors, hidden_bias), mark_tile(q_set, gold, p_set)
+    )
+    whole = gather_call(arrays, *gather_units(arrays))
+    weights = tuple(
         member.reshape(2, 16 * shard.shape[1], 2 * shard.shape[2])
         for member, shard in zip(whole[:4], arrays[:4])
-    ) + small
-
-
-def first_state(index, tokens_low, keys_low, values, lengths, rows_of, weights):
-    queries, attended, pre_one, hidden_rows, pre_two = (
-        rows_of(member) for member in index
-    )
-    seq_count, model_width = queries.shape
-    seq_length = keys_low.shape[0] // seq_count
-    vec_f32 = weights[4].astype(jnp.float32)
-    scores = jnp.einsum(
-        "shc,skhc->shk",
-        queries.astype(jnp.bfloat16).reshape(seq_count, HEADS, -1),
-        head_split(keys_low, seq_count),
-        preferred_element_type=jnp.float32,
-    ) * (model_width // HEADS) ** (-0.5)
-    live = jnp.arange(seq_length)[None, :] < lengths[:, None]
-    scores = jnp.where(live[:, None, :], scores, NEGATIVE)
-    soft_first = jnp.exp(scores - jax.nn.logsumexp(scores, axis=-1, keepdims=True))
-    normed_low = layer_norm(pre_one, vec_f32[3], vec_f32[4]).astype(jnp.bfloat16)
+    )
+    vec, bias = small_whole(whole[4], vectors, hidden_bias)
+    vec, bias = vec.astype(jnp.float32), bias.astype(jnp.float32)[:, None, :]
+    done = forward(q_len, p_len, q_embed, p_embed, *weights, vec, bias)
+    q_out, p_out, q_keys, q_values, p_keys, p_values, q0, a0, p1, h0, p2, heads = done
+    grad_first, loss = similar_call(heads, whole[5])
+    grad_q, grad_p, left, right = backward(
+        q_len, p_len, grad_first, q0, a0, p1, h0, p2, q_embed, p_embed,
+        q_keys, q_values, p_keys, p_values, *weights, vec, bias,
+    )
+    grads = exchange_call(left, right)
     return (
-        queries.astype(jnp.bfloat16),
-        keys_low,
-        values,
-        soft_first,
-        attended.astype(jnp.bfloat16),
-        pre_one,
-        normed_low,
-        hidden_rows,
-        smooth_gate(hidden_rows).astype(jnp.bfloat16),
-        pre_two,
+        loss[0, 0], q_out, p_out, grad_q, grad_p, *grads[:5], grads[5].reshape(2, -1)
     )
 
 
@@ -690,8 +1072,23 @@
     vectors,
     hidden_bias,
 ):
-    fast = kernels_fit(q_embed, p_embed, q_len, p_len)
-    gathered = (gather_weights_kernel if fast else gather_weights)(
+    if kernels_fit(q_embed, p_embed, q_len, p_len):
+        return kernel_shards(
+            q_embed,
+            p_embed,
+            q_len,
+            p_len,
+            q_set,
+            p_set,
+            gold,
+            query_key_value_weight,
+            attention_output_weight,
+            up_weight,
+            down_weight,
+            vectors,
+            hidden_bias,
+        )
+    gathered = gather_weights(
         query_key_value_weight,
         attention_output_weight,
         up_weight,
@@ -703,32 +1100,8 @@
     both_axes = ("wq", "np")
     q_weights = tuple((member[0] for member in gathered))
     p_weights = tuple((member[1] for member in gathered))
-    if fast:
-        done = forward(
-            q_len,
-            p_len,
-            q_embed,
-            p_embed,
-            *gathered[:4],
-            gathered[4].astype(jnp.float32),
-            gathered[5].astype(jnp.float32)[:, None, :],
-        )
-        q_encoded, p_encoded = done[0], done[1]
-        q_stored = first_state(
-            done[6:],
-            q_embed,
-            done[2],
-            done[3],
-            q_len,
-            lambda m: m.reshape(8, 8, -1)[:2, :4].reshape(8, -1),
-            q_weights,
-        )
-        p_stored = first_state(
-            done[6:], p_embed, done[4], done[5], p_len, lambda m: m.reshape(8, 8, -1)[2:, 0], p_weights
-        )
-    else:
-        p_encoded, p_stored = encode_forward(p_embed, p_len, p_weights)
-        q_encoded, q_stored = encode_forward(q_embed, q_len, q_weights)
+    p_encoded, p_stored = encode_forward(p_embed, p_len, p_weights)
+    q_encoded, q_stored = encode_forward(q_embed, q_len, q_weights)
     model_width = q_embed.shape[1]
     ff_width = gathered[2].shape[2]
     q_count = q_len.shape[0]

time: 665 us -> 371 us (0.56); the launches traced: 654 us -> 367 us
  local copies, waits for them, and re-layouts: 178 us -> 13.7 us
  Pallas kernels: 219 us -> 351 us
  blocking collectives: 108 us -> 0 us
  matrix products: 63.2 us -> 0 us
  other arithmetic: 38.8 us -> 1.39 us
  between operations: 17.7 us -> 0.99 us
  waiting for transfers between devices: 16.3 us -> 0 us
  starting transfers between devices: 12.9 us -> 0 us
    pallas_call x0 -> x3, Pallas kernels: none -> 122 us  [the longest x1 75.4 us: exchange_call(): pl.pallas_call(exchange_kernel, out_shape=outs, in_specs=[V, V], out_spec...]
    all_gather x1 -> x0, blocking collectives: 69.8 us -> none  [shards(): heads = lax.all_gather(own_heads, both_axes, axis=0)]
    dot_general x33 -> x0, matrix products: 63.2 us -> none  [the longest x6 10.7 us: outer(): return jnp.einsum('sd,se->de', one, two, preferred_element_type=jnp.float32)]
    slice x24 -> x1, local copies, waits for them, and re-layouts: 53.5 us -> 0.51 us  [kernel_shards(): loss[0, 0]]
    reshape x26 -> x1, local copies, waits for them, and re-layouts: 42.1 us -> 0.64 us  [kernel_shards(): grads[5].reshape(2, -1)]
    another operation x29 -> x2, local copies, waits for them, and re-layouts: 41.3 us -> 0.1 us  [mark_tile(): jnp.tile(rows, (1, 32))]
    unnamed x1 -> x0, blocking collectives: 38.3 us -> none
    reduce_sum x19 -> x0, other arithmetic: 16.6 us -> none  [the longest x4 3.74 us: norm_back(): jnp.mean(centred * centred, axis=-1, keepdims=True) + EPSILON]
  transfers between devices with their start and end apart: 4 -> 0, of which waited for: 1 -> 0; matrix products, arithmetic and copies ran while one was open for 19% -> 0% of each run, Pallas kernels for 0% -> 0%
where the time goes in v3:
time: 371 us; the launch traced here: 367 us
  Pallas kernels  351 us (95%)
  local copies, waits for them, and re-layouts  13.7 us (4%)
    pallas_call x1, Pallas kernels, gather_call(): pl.pallas_call(functools.partial(gather_kernel, units, schedule, n), out_...  138 us
    pallas_call x1, Pallas kernels, forward(): pl.pallas_call(functools.partial(fw_kernel, phases), out_shape=outs, in_s...  91.2 us
    pallas_call x1, Pallas kernels, exchange_call(): pl.pallas_call(exchange_kernel, out_shape=outs, in_specs=[V, V], out_spec...  75.4 us
    pallas_call x1, Pallas kernels, backward(): pl.pallas_call(back_kernel, out_shape=outs, in_specs=[SM, SM] + [V] * 18,...  29.3 us
    pallas_call x1, Pallas kernels, similar_call(): pl.pallas_call(similar_kernel, out_shape=[jax.ShapeDtypeStruct((16, 768),...  17.2 us

profile of v3, /device:TPU:0, one launch (start us, length us, event | category | flops | bytes accessed | tf_op | source)
XLA Modules:
  0.0 366.8 jit_solution(1675855522091871767)
XLA Ops:
  0.6 0.7 scatter.10
  1.3 1.5 scatter.11.refs_4_
  2.8 0.0 copy-start.5
  2.9 0.7 pad_bitcast_fusion
  3.5 0.7 pad_add_fusion
  4.2 0.1 tile.10
  4.3 0.6 scatter.14.refs_5_
  4.9 0.0 copy-done.5
  4.9 137.6 %gather.1 = (bf16[2,4,2,96,2304]{4,3,2,1,0:T(8,128)(2,1)}, bf16[2,4,2,96,768]{4,3,2,1,0:T(8,128)(2,1)}, bf16[2,4,2,96,3072]{4,3,2,1,0:T(8,128)(2,1)}, bf16[2,4,2...) custom-call(bf16[2,48,1152]{2,1,0:T(8,128)(2,1)} %refs_0_.1, ...), custom_call_target="tpu_custom_call" | custom-call | tf_op jit(solution)/shard_map/gather/pallas_call | solution.py:732
  142.5 0.9 reshape.220
  143.6 0.7 reshape.222.vec
  144.3 0.7 reshape.223.hb
  145.0 0.0 copy-start.1
  145.0 91.2 %fw.1 = (bf16[512,768]{1,0:T(8,128)(2,1)}, bf16[1536,768]{1,0:T(8,128)(2,1)}, bf16[512,768]{1,0:T(8,128)(2,1)}, bf16[512,768]{1,0:T(8,128)(2,1)}, bf16[1536,768]...) custom-call(s32[8]{0:T(128)} %ql.3, s32[6]{0:T(128)} %pln.1, ...), custom_call_target="tpu_custom_call" | custom-call | tf_op jit(solution)/shard_map/fw/pallas_call | solution.py:417
  236.2 0.0 copy-done.1
  236.3 0.0 copy-start.4
  236.3 0.8 copy-done.4
  237.1 17.2 %similar.1 = (f32[16,768]{1,0:T(8,128)S(1)}, f32[8,128]{1,0:T(8,128)S(1)}) custom-call(f32[16,768]{1,0:T(8,128)S(1)} %copy-done.4, s32[1,4,2,32,256]{4,3,2,1,0:T(8,128)S(1)} %copy-done.1), custom_call_target="tpu_custom_call" | custom-call | tf_op jit(solution)/shard_map/similar/pallas_call | solution.py:812
  254.3 0.0 copy-start.3
  254.3 0.6 copy-done.3
  254.9 0.5 slice.88
  255.4 29.3 %back.1 = (f32[512,768]{1,0:T(8,128)}, f32[1536,768]{1,0:T(8,128)}, bf16[16,288,128]{2,1,0:T(8,128)(2,1)}, bf16[2,16,3456]{2,1,0:T(8,128)(2,1)}) custom-call(s32[8]{0:T(128)} %ql.3, s32[6]{0:T(128)} %pln.1, f32[16,768]{1,0:T(8,128)} %copy-done.3, f32[16,768]{1,0:T(8,128)} %get-tuple-element.88.q0, f32[16,768]{1,0:T(8,128)} %get-tuple-element.89.a0, ...), custom_call_target="tpu_custom_call" | custom-call | tf_op jit(solution)/shard_map/back/pallas_call | solution.py:552
  284.7 0.0 copy-start
  284.7 1.3 copy-done
  286.0 0.0 copy-start.2
  286.0 0.9 copy-done.2
  286.9 75.4 %exchange.1 = (f32[2,48,1152]{2,1,0:T(8,128)S(1)}, f32[2,48,384]{2,1,0:T(8,128)S(1)}, f32[2,48,1536]{2,1,0:T(8,128)S(1)}, f32[2,192,384]{2,1,0:T(8,128)S(1)}, f3...) custom-call(bf16[16,288,128]{2,1,0:T(8,128)(2,1)S(1)} %copy-done, bf16[2,16,3456]{2,1,0:T(8,128)(2,1)S(1)} %copy-done.2), custom_call_target="tpu_custom_call" | custom-call | tf_op jit(solution)/shard_map/exchange/pallas_call | solution.py:979
  362.3 0.6 reshape.221
  363.0 0.8 copy.37
  363.8 0.7 copy.38
  364.4 0.8 copy.39
  365.2 0.8 copy.40
  366.0 0.6 copy.41
  (10 shorter events, 0.1 us)
Async XLA Ops:
  2.8 2.1 copy-start.5
  145.0 91.2 %copy-start.1 = (s32[1,4,2,32,256]{4,3,2,1,0:T(8,128)S(1)}, s32[1,4,2,32,256]{4,3,2,1,0:T(8,128)}, u32[]{:S(2)}) copy-start(s32[1,4,2,32,256]{4,3,2,1,0:T(8,128)} %get-tuple-element.83.marks) | copy-start | bytes 786436
  236.3 0.8 copy-start.4
  254.3 0.6 copy-start.3
  284.7 1.3 copy-start
  286.0 0.9 copy-start.2
